TPU v7x, 32 devices: a whole 2x2x4 slice. The times are simulated.
32 devices in a mesh: parts: 2 (over y), gx: 4 (over z), gy: 2 (over x), gz: 2 (over core).
Axes of the slice: x: 2, y: 2, z: 4, core: 2. Of those that a mesh axis runs over, the one named last changes fastest.
Arguments:
- populations: float32 [19, 128, 4, 512], P(None, ('parts', 'gz'), 'gy', 'gx'), parts along dimension 1, may hold values from 0 to 4
- solid_mask: int32 [128, 4, 512], P(('parts', 'gz'), 'gy', 'gx'), parts along dimension 0, may hold values 0 or 1
- recycle_plane: int32 [1], replicated, may hold values from 256 to 511
- fringe_bounds: int32 [2], replicated, may hold values from 0 to 383, as said below
- interp_rows: int32 [4], P('gy'), may hold values from 0 to 2
- interp_weights: float32 [4], P('gy'), may hold values from 0 to 1
- mean_scale: float32 [4], P('gy'), may hold values from 0.4 to 0.9
- fluct_scale: float32 [4], P('gy'), may hold values from 1 to 2
Outputs:
- final_populations: float32 [19, 128, 4, 512], P(None, ('parts', 'gz'), 'gy', 'gx'), parts along dimension 1
There are 2 independent parts, one for each index of `parts`. A program takes and returns all parts, laid end to end along the dimension named above; an argument that names none is the same for every part. Nothing has to cross between parts.
Inputs may be any that keep to these rules, and one draw needn't show every extreme that they name: `fringe_bounds`: the second entry is 383; the first lies below 128.
All inputs are finite; a program needn't handle non-finite values. No bound on the sum of `solid_mask` on one device may be relied on, other than what follows from the above.
Results may differ from a plain program's by a relative error of at most 0.0001.
Values sent between devices are 32-bit elements; how exact they have to be, the bound alone decides.
No kernel may reach another device: no remote copies, remote signals or barrier semaphores. Data moves between devices by JAX's collectives and lax.ppermute only.
A program may use at most 64 MiB of HBM per device.

v0:
```python
import math

import jax
import jax.numpy as jnp
from jax import lax
from jax.sharding import PartitionSpec as P

STEPS = 2


lattice_vel = (
    (0, 0, 0),
    (1, 0, 0),
    (-1, 0, 0),
    (0, 1, 0),
    (0, -1, 0),
    (0, 0, 1),
    (0, 0, -1),
    (1, 1, 0),
    (-1, -1, 0),
    (1, -1, 0),
    (-1, 1, 0),
    (1, 0, 1),
    (-1, 0, -1),
    (1, 0, -1),
    (-1, 0, 1),
    (0, 1, 1),
    (0, -1, -1),
    (0, 1, -1),
    (0, -1, 1),
)
lattice_weight = (1.0 / 3.0,) + (1.0 / 18.0,) * 6 + (1.0 / 36.0,) * 12
opposite = (0, 2, 1, 4, 3, 6, 5, 8, 7, 10, 9, 12, 11, 14, 13, 16, 15, 18, 17)
mirror_pop = (0, 1, 2, 4, 3, 5, 6, 9, 10, 7, 8, 11, 12, 13, 14, 18, 17, 16, 15)
relax_rate = 1.25
fringe_peak = 0.8


def spread(array, axis, root):
    mine = lax.axis_index(axis) == root
    return lax.psum(jnp.where(mine, array, jnp.zeros_like(array)), axis)


def with_halo(cells, sides, width):
    for axis, dim in sides:
        count = lax.axis_size(axis)
        head = lax.slice_in_dim(cells, 0, width, axis=dim)
        tail = lax.slice_in_dim(cells, cells.shape[dim] - width, cells.shape[dim], axis=dim)
        cells = jnp.concatenate(
            [
                lax.ppermute(tail, axis, [(i, (i + 1) % count) for i in range(count)]),
                cells,
                lax.ppermute(head, axis, [((i + 1) % count, i) for i in range(count)]),
            ],
            axis=dim,
        )
    return cells


def moments(current):
    density = lattice_weight[0] * current[0]
    moment = [jnp.zeros_like(density), jnp.zeros_like(density), jnp.zeros_like(density)]
    for population in range(1, 19):
        weighted = lattice_weight[population] * current[population]
        density = density + weighted
        for direction in range(3):
            component = lattice_vel[population][direction]
            if component != 0:
                moment[direction] = moment[direction] + component * weighted
    return (density, moment[0] / density, moment[1] / density, moment[2] / density)


def equilibrium(density, vel_x, vel_y, vel_z, population):
    step_x, step_y, step_z = lattice_vel[population]
    projected = step_x * vel_x + step_y * vel_y + step_z * vel_z
    speed_sq = vel_x * vel_x + vel_y * vel_y + vel_z * vel_z
    return density * (1.0 + 3.0 * projected + 4.5 * projected * projected - 1.5 * speed_sq)


def fringe_ramp(x_global, bounds):
    zone_start = bounds[0]
    finish = bounds[1]
    zone_width = (finish - zone_start).astype(jnp.float32)
    angle_arg = math.pi * ((x_global - zone_start).astype(jnp.float32) + 0.5) / zone_width
    inside = (x_global >= zone_start) & (x_global < finish)
    return jnp.where(inside, fringe_peak * jnp.sin(angle_arg) ** 2, 0.0)


def rescale(plane, plane_mean, row_index, row_weight, mean_gain, fluct_gain):
    lower = jnp.take(plane, row_index, axis=2)
    upper = jnp.take(plane, row_index + 1, axis=2)
    blended = (1.0 - row_weight) * lower + row_weight * upper
    mean_lower = jnp.take(plane_mean, row_index, axis=1)
    mean_upper = jnp.take(plane_mean, row_index + 1, axis=1)
    mean_part = ((1.0 - row_weight) * mean_lower + row_weight * mean_upper)[:, None, :]
    speeds = mean_gain * mean_part[1:] + fluct_gain * (blended[1:] - mean_part[1:])
    return (blended[0], speeds[0], speeds[1], speeds[2])


def span_mean(gathered, total_z):
    return lax.psum(jnp.sum(gathered, axis=1), "gz") / total_z


def body(
    populations,
    solid_mask,
    recycle_plane,
    fringe_bounds,
    interp_rows,
    interp_weights,
    mean_scale,
    fluct_scale,
):
    depth_z = populations.shape[1]
    rows_y = populations.shape[2]
    cols_x = populations.shape[3]
    total_z = depth_z * lax.axis_size("gz")
    total_y = rows_y * lax.axis_size("gy")
    total_x = cols_x * lax.axis_size("gx")
    x_global = (lax.axis_index("gx") * cols_x + jnp.arange(cols_x, dtype=jnp.int32))[None, None, :]
    y_global = (lax.axis_index("gy") * rows_y + jnp.arange(rows_y, dtype=jnp.int32))[None, :, None]
    solid_cell = solid_mask == 1
    fringe_weight = fringe_ramp(x_global, fringe_bounds)
    owner_x = recycle_plane[0] // cols_x
    offset = recycle_plane[0] - owner_x * cols_x
    current = [populations[population] for population in range(19)]
    for time_step in range(STEPS):
        density, vel_x, vel_y, vel_z = moments(current)
        recycle_rows = jnp.stack(
            [
                lax.dynamic_index_in_dim(moment_field, offset, 2, False)
                for moment_field in (density, vel_x, vel_y, vel_z)
            ]
        )
        gathered = lax.all_gather(recycle_rows, "gy", axis=2, tiled=True)
        target = jnp.stack(
            rescale(
                gathered,
                span_mean(gathered, total_z),
                interp_rows,
                interp_weights,
                mean_scale,
                fluct_scale,
            )
        )
        target = spread(target, "gx", owner_x)
        target_eq = [
            equilibrium(
                target[0][:, :, None],
                target[1][:, :, None],
                target[2][:, :, None],
                target[3][:, :, None],
                population,
            )
            for population in range(19)
        ]
        collided = []
        for population in range(19):
            local_eq = equilibrium(density, vel_x, vel_y, vel_z, population)
            relaxed = current[population] - relax_rate * (current[population] - local_eq)
            forced = relaxed + fringe_weight * (target_eq[population] - relaxed)
            collided.append(jnp.where(solid_cell, current[opposite[population]], forced))
        stacked = jnp.stack(collided)
        padded = with_halo(stacked, (("gx", 3), ("gy", 2), ("gz", 1)), 1)
        current = []
        for population in range(19):
            step_x, step_y, step_z = lattice_vel[population]
            pulled = padded[
                population,
                1 - step_z : 1 - step_z + depth_z,
                1 - step_y : 1 - step_y + rows_y,
                1 - step_x : 1 - step_x + cols_x,
            ]
            if step_x == 1:
                pulled = jnp.where(x_global == 0, target_eq[population], pulled)
            if step_x == -1:
                pulled = jnp.where(x_global == total_x - 1, collided[population], pulled)
            if step_y == 1:
                pulled = jnp.where(y_global == 0, collided[opposite[population]], pulled)
            if step_y == -1:
                pulled = jnp.where(
                    y_global == total_y - 1, collided[mirror_pop[population]], pulled
                )
            current.append(pulled)
    return jnp.stack(current)


def solution(mesh):
    placed = (
        P(None, ("parts", "gz"), "gy", "gx"),
        P(("parts", "gz"), "gy", "gx"),
        P(),
        P(),
        P("gy"),
        P("gy"),
        P("gy"),
        P("gy"),
    )
    return jax.shard_map(
        body,
        mesh=mesh,
        in_specs=placed,
        out_specs=P(None, ("parts", "gz"), "gy", "gx"),
        check_vma=False,
    )
```

profile of v0, /device:TPU:0, one launch (start us, length us, event | category | flops | bytes accessed | tf_op | source)
XLA Modules:
  0.0 144.1 jit_solution(3875547059339797605)
XLA Ops:
  0.7 0.7 compare_select_fusion.1
  1.3 0.7 compare_and_fusion
  2.0 1.1 fusion.439
  3.7 5.2 %all_gather.6 = f32[4,32,4]{1,0,2:T(4,128)S(1)} all-gather(f32[4,32,2]{1,0,2:T(4,128)S(1)} %copy.205), channel_id=1, replica_groups=mesh['parts'=2,'gx'=4,'gy'=2,'gz'=2] {'gy'}, dimensions={2}, use_global_device_ids=true | all-gather | bytes 3072 | tf_op jit(solution)/shard_map/all_gather | solution.py:135
  9.0 2.4 %psum.28 = f32[4,4]{0,1:T(4,128)S(1)} all-reduce(f32[4,4]{0,1:T(4,128)S(1)} %reduce_sum.18), channel_id=1, replica_groups=mesh['parts'=2,'gx'=4,'gy'=2,'gz'=2] {'gz'}, use_global_device_ids=true, to_apply=%region_1.3 | all-reduce | flops 16 | bytes 128 | tf_op jit(solution)/shard_map/psum | solution.py:101
  13.8 0.6 fusion.442
  16.0 12.5 %psum.29 = f32[4,32,2]{1,0,2:T(4,128)S(1)} all-reduce(f32[4,32,2]{1,0,2:T(4,128)S(1)} %maximum_select_fusion.2), channel_id=1, replica_groups=mesh['parts'=2,'gx'=4,'gy'=2,'gz'=2] {'gx'}, use_global_device_ids=true, to_apply=%region_2.5 | all-reduce | flops 256 | bytes 2048 | tf_op jit(solution)/shard_map/psum | solution.py:41
  28.6 1.3 and_select_fusion
  30.0 0.7 constant_dynamic-update-slice_fusion.18
  30.8 0.7 constant_dynamic-update-slice_fusion.16
  31.5 0.7 constant_dynamic-update-slice_fusion.15
  32.2 0.7 constant_dynamic-update-slice_fusion.14
  33.0 0.7 constant_dynamic-update-slice_fusion.11
  33.7 0.7 constant_dynamic-update-slice_fusion.10
  34.4 0.7 constant_dynamic-update-slice_fusion.9
  35.1 0.7 constant_dynamic-update-slice_fusion.8
  35.9 0.7 constant_dynamic-update-slice_fusion.6
  36.6 0.7 constant_dynamic-update-slice_fusion.4
  37.3 0.7 constant_dynamic-update-slice_fusion.3
  38.0 0.7 constant_dynamic-update-slice_fusion.2
  38.7 0.7 constant_dynamic-update-slice_fusion.1
  39.4 0.7 constant_dynamic-update-slice_fusion
  41.0 3.8 %collective-permute-start.1 = (f32[19,32,2,1]{1,2,3,0:T(2,128)S(1)}, f32[19,32,2,1]{1,2,3,0:T(2,128)S(1)}, u32[]{:S(2)}, u32[]{:S(2)}) collective-permute-start(f32[19,32,2,1]{1,2,3,0:T(2,128)S(1)} %copy.248), channel_id=1, source_target_pairs={{4,0},{8,4},{12,8},{0,12},{5,1},{9,5},{13,9},{1,13},{6,2},{10,6},{... | collective-permute-start | bytes 14600 | tf_op jit(solution)/shard_map/ppermute | solution.py:53
  44.8 1.4 collective-permute-done
  47.4 1.1 fusion.436
  48.6 1.5 %collective-permute-start.3 = (f32[19,32,1,130]{3,1,2,0:T(8,128)}, f32[19,32,1,130]{3,1,2,0:T(8,128)S(1)}, u32[]{:S(2)}, u32[]{:S(2)}) collective-permute-start(f32[19,32,1,130]{3,1,2,0:T(8,128)} %get-tuple-element.96), channel_id=1, source_target_pairs={{2,0},{0,2},{3,1},{1,3},{6,4},{4,6},{7,5},{5,7},{10,8},{8,10},{11,... | collective-permute-start | bytes 948488 | tf_op jit(solution)/shard_map/ppermute | solution.py:53
  50.8 15.0 %collective-permute-done.3 = f32[19,32,1,130]{3,1,2,0:T(8,128)S(1)} collective-permute-done((f32[19,32,1,130]{3,1,2,0:T(8,128)}, f32[19,32,1,130]{3,1,2,0:T(8,128)S(1)}, u32[]{:S(2)}, u32[]{:S(2)}) %collective-permute-start.3) | collective-permute-done | bytes 316192 | tf_op jit(solution)/shard_map/ppermute | solution.py:53
  65.7 9.3 %collective-permute-done.2 = f32[19,32,1,130]{3,1,2,0:T(8,128)S(1)} collective-permute-done((f32[19,32,1,130]{3,1,2,0:T(8,128)}, f32[19,32,1,130]{3,1,2,0:T(8,128)S(1)}, u32[]{:S(2)}, u32[]{:S(2)}) %collective-permute-start.2) | collective-permute-done | bytes 316192 | tf_op jit(solution)/shard_map/ppermute | solution.py:51
  76.0 0.7 collective-permute-done.4
  77.2 1.0 add_divide_fusion.2
  79.1 4.3 %all_gather.7 = f32[4,32,4]{1,0,2:T(4,128)S(1)} all-gather(f32[4,32,2]{1,0,2:T(4,128)S(1)} %copy.216), channel_id=1, replica_groups=mesh['parts'=2,'gx'=4,'gy'=2,'gz'=2] {'gy'}, dimensions={2}, use_global_device_ids=true | all-gather | bytes 3072 | tf_op jit(solution)/shard_map/all_gather | solution.py:135
  83.6 2.4 %psum.30 = f32[4,4]{0,1:T(4,128)S(1)} all-reduce(f32[4,4]{0,1:T(4,128)S(1)} %reduce_sum.19), channel_id=1, replica_groups=mesh['parts'=2,'gx'=4,'gy'=2,'gz'=2] {'gz'}, use_global_device_ids=true, to_apply=%region_4.7 | all-reduce | flops 16 | bytes 128 | tf_op jit(solution)/shard_map/psum | solution.py:101
  86.0 0.7 gather_fusion.7
  86.7 0.7 gather_fusion.6
  87.4 0.7 gather_fusion.4
  88.1 0.7 gather_fusion.5
  88.8 0.7 fusion.297
  89.5 0.7 fusion.413
  90.2 0.7 broadcast_multiply_fusion.6
  91.0 0.7 fusion.294
  91.7 11.9 %psum.31 = f32[4,32,2]{1,0,2:T(4,128)S(1)} all-reduce(f32[4,32,2]{1,0,2:T(4,128)S(1)} %maximum_select_fusion.3), channel_id=1, replica_groups=mesh['parts'=2,'gx'=4,'gy'=2,'gz'=2] {'gx'}, use_global_device_ids=true, to_apply=%region_5.8 | all-reduce | flops 256 | bytes 2048 | tf_op jit(solution)/shard_map/psum | solution.py:41
  106.6 2.0 %collective-permute-start.6 = (f32[19,32,2,1]{1,2,3,0:T(2,128)S(1)}, f32[19,32,2,1]{1,2,3,0:T(2,128)S(1)}, u32[]{:S(2)}, u32[]{:S(2)}) collective-permute-start(f32[19,32,2,1]{1,2,3,0:T(2,128)S(1)} %copy.251), channel_id=1, source_target_pairs={{0,4},{4,8},{8,12},{12,0},{1,5},{5,9},{9,13},{13,1},{2,6},{6,10},{... | collective-permute-start | bytes 14600 | tf_op jit(solution)/shard_map/ppermute | solution.py:51
  108.6 1.4 collective-permute-done.7
  110.4 1.8 %collective-permute-done.6 = f32[19,32,2,1]{1,2,3,0:T(2,128)S(1)} collective-permute-done((f32[19,32,2,1]{1,2,3,0:T(2,128)S(1)}, f32[19,32,2,1]{1,2,3,0:T(2,128)S(1)}, u32[]{:S(2)}, u32[]{:S(2)}) %collective-permute-start.6) | collective-permute-done | bytes 4896 | tf_op jit(solution)/shard_map/ppermute | solution.py:51
  113.2 1.6 %collective-permute-start.9 = (f32[19,32,1,130]{3,1,2,0:T(8,128)S(1)}, f32[19,32,1,130]{3,1,2,0:T(8,128)S(1)}, u32[]{:S(2)}, u32[]{:S(2)}) collective-permute-start(f32[19,32,1,130]{3,1,2,0:T(8,128)S(1)} %get-tuple-element.94), channel_id=1, source_target_pairs={{2,0},{0,2},{3,1},{1,3},{6,4},{4,6},{7,5},{5,7},{10,8},{8,10},{11,... | collective-permute-start | bytes 948488 | tf_op jit(solution)/shard_map/ppermute | solution.py:53
  115.5 14.7 %collective-permute-done.9 = f32[19,32,1,130]{3,1,2,0:T(8,128)S(1)} collective-permute-done((f32[19,32,1,130]{3,1,2,0:T(8,128)S(1)}, f32[19,32,1,130]{3,1,2,0:T(8,128)S(1)}, u32[]{:S(2)}, u32[]{:S(2)}) %collective-permute-start.9) | collective-permute-done | bytes 316192 | tf_op jit(solution)/shard_map/ppermute | solution.py:53
  130.2 9.3 %collective-permute-done.8 = f32[19,32,1,130]{3,1,2,0:T(8,128)S(1)} collective-permute-done((f32[19,32,1,130]{3,1,2,0:T(8,128)S(1)}, f32[19,32,1,130]{3,1,2,0:T(8,128)S(1)}, u32[]{:S(2)}, u32[]{:S(2)}) %collective-permute-start.8) | collective-permute-done | bytes 316192 | tf_op jit(solution)/shard_map/ppermute | solution.py:51
  142.8 1.3 copy.227
  (231 shorter events, 16.3 us)
Async XLA Ops:
  2.0 28.0 %copy-start.38 = (pred[2]{0:T(512)(128)(4,1)}, pred[2]{0:T(512)(128)(4,1)S(1)}, u32[]{:S(2)}) copy-start(pred[2]{0:T(512)(128)(4,1)S(1)} %get-tuple-element.86) | copy-start | bytes 10
  2.0 28.0 %copy-start.39 = (pred[2]{0:T(512)(128)(4,1)}, pred[2]{0:T(512)(128)(4,1)S(1)}, u32[]{:S(2)}) copy-start(pred[2]{0:T(512)(128)(4,1)S(1)} %get-tuple-element.175) | copy-start | bytes 10
  3.1 10.7 %copy-start.52 = (f32[2]{0:T(128)S(1)}, f32[2]{0:T(128)}, u32[]{:S(2)}) copy-start(f32[2]{0:T(128)} %param.17) | copy-start | bytes 28
  3.1 10.7 %copy-start.55 = (s32[2]{0:T(128)S(1)}, s32[2]{0:T(128)}, u32[]{:S(2)}) copy-start(s32[2]{0:T(128)} %param.15) | copy-start | bytes 28
  3.1 12.7 %copy-start.54 = (f32[2]{0:T(128)S(1)}, f32[2]{0:T(128)}, u32[]{:S(2)}) copy-start(f32[2]{0:T(128)} %param.18) | copy-start | bytes 28
  3.1 12.8 %copy-start.56 = (f32[2]{0:T(128)S(1)}, f32[2]{0:T(128)}, u32[]{:S(2)}) copy-start(f32[2]{0:T(128)} %param.19) | copy-start | bytes 28
  3.2 26.8 %copy-start.31 = (s32[32,2,128]{2,1,0:T(2,128)S(1)}, s32[32,2,128]{2,1,0:T(2,128)}, u32[]{:S(2)}) copy-start(s32[32,2,128]{2,1,0:T(2,128)} %param.13) | copy-start | bytes 98308
  28.6 6.5 %copy-start.46 = (f32[32,2]{0,1:T(2,128)}, f32[32,2]{0,1:T(2,128)S(1)}, u32[]{:S(2)}) copy-start(f32[32,2]{0,1:T(2,128)S(1)} %get-tuple-element.151) | copy-start | bytes 772
  28.6 6.5 %copy-start.48 = (f32[32,2]{0,1:T(2,128)}, f32[32,2]{0,1:T(2,128)S(1)}, u32[]{:S(2)}) copy-start(f32[32,2]{0,1:T(2,128)S(1)} %get-tuple-element.153) | copy-start | bytes 772
  28.6 7.2 %copy-start.44 = (f32[32,2]{0,1:T(2,128)}, f32[32,2]{0,1:T(2,128)S(1)}, u32[]{:S(2)}) copy-start(f32[32,2]{0,1:T(2,128)S(1)} %get-tuple-element.149) | copy-start | bytes 772
  28.6 7.9 %copy-start.42 = (f32[32,2]{0,1:T(2,128)}, f32[32,2]{0,1:T(2,128)S(1)}, u32[]{:S(2)}) copy-start(f32[32,2]{0,1:T(2,128)S(1)} %get-tuple-element.147) | copy-start | bytes 772
  40.6 5.6 %collective-permute-start = (f32[19,32,2,1]{1,2,3,0:T(2,128)S(1)}, f32[19,32,2,1]{1,2,3,0:T(2,128)S(1)}, u32[]{:S(2)}, u32[]{:S(2)}) collective-permute-start(f32[19,32,2,1]{1,2,3,0:T(2,128)S(1)} %copy.247), channel_id=1, source_target_pairs={{0,4},{4,8},{8,12},{12,0},{1,5},{5,9},{9,13},{13,1},{2,6},{6,10},{... | collective-permute-start | bytes 14600 | tf_op jit(solution)/shard_map/ppermute | solution.py:51
  41.0 5.6 %collective-permute-start.1 = (f32[19,32,2,1]{1,2,3,0:T(2,128)S(1)}, f32[19,32,2,1]{1,2,3,0:T(2,128)S(1)}, u32[]{:S(2)}, u32[]{:S(2)}) collective-permute-start(f32[19,32,2,1]{1,2,3,0:T(2,128)S(1)} %copy.248), channel_id=1, source_target_pairs={{4,0},{8,4},{12,8},{0,12},{5,1},{9,5},{13,9},{1,13},{6,2},{10,6},{... | collective-permute-start | bytes 14600 | tf_op jit(solution)/shard_map/ppermute | solution.py:53
  48.6 17.2 %collective-permute-start.3 = (f32[19,32,1,130]{3,1,2,0:T(8,128)}, f32[19,32,1,130]{3,1,2,0:T(8,128)S(1)}, u32[]{:S(2)}, u32[]{:S(2)}) collective-permute-start(f32[19,32,1,130]{3,1,2,0:T(8,128)} %get-tuple-element.96), channel_id=1, source_target_pairs={{2,0},{0,2},{3,1},{1,3},{6,4},{4,6},{7,5},{5,7},{10,8},{8,10},{11,... | collective-permute-start | bytes 948488 | tf_op jit(solution)/shard_map/ppermute | solution.py:53
  50.1 25.0 %collective-permute-start.2 = (f32[19,32,1,130]{3,1,2,0:T(8,128)}, f32[19,32,1,130]{3,1,2,0:T(8,128)S(1)}, u32[]{:S(2)}, u32[]{:S(2)}) collective-permute-start(f32[19,32,1,130]{3,1,2,0:T(8,128)} %get-tuple-element.97), channel_id=1, source_target_pairs={{0,2},{2,0},{1,3},{3,1},{4,6},{6,4},{5,7},{7,5},{8,10},{10,8},{9,1... | collective-permute-start | bytes 948488 | tf_op jit(solution)/shard_map/ppermute | solution.py:51
  50.6 26.4 %copy-start.32 = (pred[128]{0:T(512)(128)(4,1)}, pred[128]{0:T(512)(128)(4,1)S(1)}, u32[]{:S(2)}) copy-start(pred[128]{0:T(512)(128)(4,1)S(1)} %get-tuple-element.183) | copy-start | bytes 388
  50.6 26.4 %copy-start.14 = (f32[32,2,128]{2,0,1:T(8,128)S(1)}, f32[32,2,128]{2,0,1:T(8,128)}, u32[]{:S(2)}) copy-start(f32[32,2,128]{2,0,1:T(8,128)} %get-tuple-element.84) | copy-start | bytes 98308
  50.6 26.4 %copy-start.18 = (f32[32,2,128]{2,0,1:T(8,128)S(1)}, f32[32,2,128]{2,0,1:T(8,128)}, u32[]{:S(2)}) copy-start(f32[32,2,128]{2,0,1:T(8,128)} %get-tuple-element.82) | copy-start | bytes 98308
  50.6 26.4 %copy-start.19 = (f32[32,2,128]{2,0,1:T(8,128)S(1)}, f32[32,2,128]{2,0,1:T(8,128)}, u32[]{:S(2)}) copy-start(f32[32,2,128]{2,0,1:T(8,128)} %get-tuple-element.80) | copy-start | bytes 98308
  50.6 26.4 %copy-start.20 = (f32[32,2,128]{2,0,1:T(8,128)S(1)}, f32[32,2,128]{2,0,1:T(8,128)}, u32[]{:S(2)}) copy-start(f32[32,2,128]{2,0,1:T(8,128)} %get-tuple-element.78) | copy-start | bytes 98308
  50.6 26.4 %copy-start.21 = (f32[32,2,128]{2,0,1:T(8,128)S(1)}, f32[32,2,128]{2,0,1:T(8,128)}, u32[]{:S(2)}) copy-start(f32[32,2,128]{2,0,1:T(8,128)} %get-tuple-element.76) | copy-start | bytes 98308
  50.6 26.4 %copy-start.22 = (f32[32,2,128]{2,0,1:T(8,128)S(1)}, f32[32,2,128]{2,0,1:T(8,128)}, u32[]{:S(2)}) copy-start(f32[32,2,128]{2,0,1:T(8,128)} %get-tuple-element.74) | copy-start | bytes 98308
  50.7 26.4 %copy-start.23 = (f32[32,2,128]{2,0,1:T(8,128)S(1)}, f32[32,2,128]{2,0,1:T(8,128)}, u32[]{:S(2)}) copy-start(f32[32,2,128]{2,0,1:T(8,128)} %get-tuple-element.72) | copy-start | bytes 98308
  50.7 26.4 %copy-start.24 = (f32[32,2,128]{2,0,1:T(8,128)S(1)}, f32[32,2,128]{2,0,1:T(8,128)}, u32[]{:S(2)}) copy-start(f32[32,2,128]{2,0,1:T(8,128)} %get-tuple-element.70) | copy-start | bytes 98308
  50.7 26.4 %copy-start.25 = (f32[32,2,128]{2,0,1:T(8,128)S(1)}, f32[32,2,128]{2,0,1:T(8,128)}, u32[]{:S(2)}) copy-start(f32[32,2,128]{2,0,1:T(8,128)} %get-tuple-element.68) | copy-start | bytes 98308
  50.7 26.4 %copy-start.26 = (f32[32,2,128]{2,0,1:T(8,128)S(1)}, f32[32,2,128]{2,0,1:T(8,128)}, u32[]{:S(2)}) copy-start(f32[32,2,128]{2,0,1:T(8,128)} %get-tuple-element.66) | copy-start | bytes 98308
  50.7 26.4 %copy-start.27 = (f32[32,2,128]{2,0,1:T(8,128)S(1)}, f32[32,2,128]{2,0,1:T(8,128)}, u32[]{:S(2)}) copy-start(f32[32,2,128]{2,0,1:T(8,128)} %get-tuple-element.64) | copy-start | bytes 98308
  50.7 26.4 %copy-start.28 = (f32[32,2,128]{2,0,1:T(8,128)S(1)}, f32[32,2,128]{2,0,1:T(8,128)}, u32[]{:S(2)}) copy-start(f32[32,2,128]{2,0,1:T(8,128)} %get-tuple-element.62) | copy-start | bytes 98308
  50.7 26.4 %copy-start.29 = (f32[32,2,128]{2,0,1:T(8,128)S(1)}, f32[32,2,128]{2,0,1:T(8,128)}, u32[]{:S(2)}) copy-start(f32[32,2,128]{2,0,1:T(8,128)} %get-tuple-element.60) | copy-start | bytes 98308
  50.7 26.4 %copy-start.30 = (f32[32,2,128]{2,0,1:T(8,128)S(1)}, f32[32,2,128]{2,0,1:T(8,128)}, u32[]{:S(2)}) copy-start(f32[32,2,128]{2,0,1:T(8,128)} %get-tuple-element.56) | copy-start | bytes 98308
  50.7 26.4 %copy-start.43 = (f32[32,2]{0,1:T(2,128)S(1)}, f32[32,2]{0,1:T(2,128)}, u32[]{:S(2)}) copy-start(f32[32,2]{0,1:T(2,128)} %copy-done.42) | copy-start | bytes 772
  50.7 26.4 %copy-start.45 = (f32[32,2]{0,1:T(2,128)S(1)}, f32[32,2]{0,1:T(2,128)}, u32[]{:S(2)}) copy-start(f32[32,2]{0,1:T(2,128)} %copy-done.44) | copy-start | bytes 772
  50.8 26.4 %copy-start.47 = (f32[32,2]{0,1:T(2,128)S(1)}, f32[32,2]{0,1:T(2,128)}, u32[]{:S(2)}) copy-start(f32[32,2]{0,1:T(2,128)} %copy-done.46) | copy-start | bytes 772
  50.8 26.4 %copy-start.49 = (f32[32,2]{0,1:T(2,128)S(1)}, f32[32,2]{0,1:T(2,128)}, u32[]{:S(2)}) copy-start(f32[32,2]{0,1:T(2,128)} %copy-done.48) | copy-start | bytes 772
  50.8 26.4 %copy-start.51 = (f32[32,2]{0,1:T(2,128)S(1)}, f32[32,2]{0,1:T(2,128)}, u32[]{:S(2)}) copy-start(f32[32,2]{0,1:T(2,128)} %copy-done.50) | copy-start | bytes 772
  75.4 1.3 collective-permute-start.4
  75.5 1.4 collective-permute-start.5
  78.3 25.4 %copy-start.15 = (f32[32,2,128]{2,0,1:T(8,128)S(1)}, f32[32,2,128]{2,0,1:T(8,128)}, u32[]{:S(2)}) copy-start(f32[32,2,128]{2,0,1:T(8,128)} %get-tuple-element.84) | copy-start | bytes 98308
  78.6 25.3 %copy-start.16 = (f32[32,2,128]{2,0,1:T(8,128)S(1)}, f32[32,2,128]{2,0,1:T(8,128)}, u32[]{:S(2)}) copy-start(f32[32,2,128]{2,0,1:T(8,128)} %get-tuple-element.40) | copy-start | bytes 98308
  78.6 25.3 %copy-start.17 = (f32[32,2,128]{2,0,1:T(8,128)S(1)}, f32[32,2,128]{2,0,1:T(8,128)}, u32[]{:S(2)}) copy-start(f32[32,2,128]{2,0,1:T(8,128)} %get-tuple-element.49) | copy-start | bytes 98308
  79.1 25.0 %copy-start.1 = (f32[32,2,128]{2,0,1:T(8,128)S(1)}, f32[32,2,128]{2,0,1:T(8,128)}, u32[]{:S(2)}) copy-start(f32[32,2,128]{2,0,1:T(8,128)} %copy-done) | copy-start | bytes 98308
  106.2 3.8 %collective-permute-start.7 = (f32[19,32,2,1]{1,2,3,0:T(2,128)S(1)}, f32[19,32,2,1]{1,2,3,0:T(2,128)S(1)}, u32[]{:S(2)}, u32[]{:S(2)}) collective-permute-start(f32[19,32,2,1]{1,2,3,0:T(2,128)S(1)} %copy.252), channel_id=1, source_target_pairs={{4,0},{8,4},{12,8},{0,12},{5,1},{9,5},{13,9},{1,13},{6,2},{10,6},{... | collective-permute-start | bytes 14600 | tf_op jit(solution)/shard_map/ppermute | solution.py:53
  106.6 5.6 %collective-permute-start.6 = (f32[19,32,2,1]{1,2,3,0:T(2,128)S(1)}, f32[19,32,2,1]{1,2,3,0:T(2,128)S(1)}, u32[]{:S(2)}, u32[]{:S(2)}) collective-permute-start(f32[19,32,2,1]{1,2,3,0:T(2,128)S(1)} %copy.251), channel_id=1, source_target_pairs={{0,4},{4,8},{8,12},{12,0},{1,5},{5,9},{9,13},{13,1},{2,6},{6,10},{... | collective-permute-start | bytes 14600 | tf_op jit(solution)/shard_map/ppermute | solution.py:51
  113.2 17.0 %collective-permute-start.9 = (f32[19,32,1,130]{3,1,2,0:T(8,128)S(1)}, f32[19,32,1,130]{3,1,2,0:T(8,128)S(1)}, u32[]{:S(2)}, u32[]{:S(2)}) collective-permute-start(f32[19,32,1,130]{3,1,2,0:T(8,128)S(1)} %get-tuple-element.94), channel_id=1, source_target_pairs={{2,0},{0,2},{3,1},{1,3},{6,4},{4,6},{7,5},{5,7},{10,8},{8,10},{11,... | collective-permute-start | bytes 948488 | tf_op jit(solution)/shard_map/ppermute | solution.py:53
  114.7 24.8 %collective-permute-start.8 = (f32[19,32,1,130]{3,1,2,0:T(8,128)S(1)}, f32[19,32,1,130]{3,1,2,0:T(8,128)S(1)}, u32[]{:S(2)}, u32[]{:S(2)}) collective-permute-start(f32[19,32,1,130]{3,1,2,0:T(8,128)S(1)} %get-tuple-element.95), channel_id=1, source_target_pairs={{0,2},{2,0},{1,3},{3,1},{4,6},{6,4},{5,7},{7,5},{8,10},{10,8},{9,1... | collective-permute-start | bytes 948488 | tf_op jit(solution)/shard_map/ppermute | solution.py:51
  115.5 25.0 %copy-start.37 = (pred[2]{0:T(512)(128)(4,1)S(1)}, pred[2]{0:T(512)(128)(4,1)}, u32[]{:S(2)}) copy-start(pred[2]{0:T(512)(128)(4,1)} %copy-done.36) | copy-start | bytes 10
  139.9 1.3 collective-permute-start.10
  140.0 1.4 collective-permute-start.11
  (21 other events, 32.8 us)
where the time goes:
time: 145 us; the launch traced here: 144 us
  waiting for transfers between devices  53.9 us (37%)
  blocking collectives  38.9 us (27%)
  other arithmetic  22.3 us (15%)
  local copies, waits for them, and re-layouts  14.6 us (10%)
  starting transfers between devices  11.2 us (8%)
  between operations  3.07 us (2%)
    ppermute x6, waiting for transfers between devices, with_halo(): lax.ppermute(head, axis, [((i + 1) % count, i) for i in range(count)])  31.3 us
    psum x2, blocking collectives, spread(): return lax.psum(jnp.where(mine, array, jnp.zeros_like(array)), axis)  24.5 us
    ppermute x6, waiting for transfers between devices, with_halo(): lax.ppermute(tail, axis, [(i, (i + 1) % count) for i in range(count)])  22.6 us
    unnamed x53, other arithmetic  12.3 us
    all_gather x2, blocking collectives, body(): gathered = lax.all_gather(recycle_rows, 'gy', axis=2, tiled=True)  9.57 us
    ppermute x6, starting transfers between devices, with_halo(): lax.ppermute(head, axis, [((i + 1) % count, i) for i in range(count)])  7.93 us
    psum x2, blocking collectives, span_mean(): return lax.psum(jnp.sum(gathered, axis=1), 'gz') / total_z  4.89 us
    ppermute x6, starting transfers between devices, with_halo(): lax.ppermute(tail, axis, [(i, (i + 1) % count) for i in range(count)])  3.3 us
  transfers between devices with their start and end apart: 12, of which 10 were waited for; matrix products, arithmetic and copies ran while one was open for 1% of the time, Pallas kernels for 0%

commit v1 on v0

v1 whole, which is shorter than its diff:
```python
import functools
import math

import jax
import jax.numpy as jnp
from jax import lax
from jax.experimental import pallas as pl
from jax.experimental.pallas import tpu as pltpu
from jax.sharding import PartitionSpec as P

lattice_vel = (
    (0, 0, 0),
    (1, 0, 0),
    (-1, 0, 0),
    (0, 1, 0),
    (0, -1, 0),
    (0, 0, 1),
    (0, 0, -1),
    (1, 1, 0),
    (-1, -1, 0),
    (1, -1, 0),
    (-1, 1, 0),
    (1, 0, 1),
    (-1, 0, -1),
    (1, 0, -1),
    (-1, 0, 1),
    (0, 1, 1),
    (0, -1, -1),
    (0, 1, -1),
    (0, -1, 1),
)
lattice_weight = (1.0 / 3.0,) + (1.0 / 18.0,) * 6 + (1.0 / 36.0,) * 12
opposite = (0, 2, 1, 4, 3, 6, 5, 8, 7, 10, 9, 12, 11, 14, 13, 16, 15, 18, 17)
mirror_pop = (0, 1, 2, 4, 3, 5, 6, 9, 10, 7, 8, 11, 12, 13, 14, 18, 17, 16, 15)
relax_rate = 1.25
fringe_peak = 0.8

DEPTH, ROWS, COLS = 32, 2, 128
SPAN = 2 * DEPTH
MASK = 19
EAST = tuple(i for i in range(19) if lattice_vel[i][0] == 1)
WEST = tuple(i for i in range(19) if lattice_vel[i][0] == -1)
FLAT_X = tuple(i for i in range(19) if lattice_vel[i][0] == 0)
UP = tuple(i for i in range(19) if lattice_vel[i][1] == 1)
DOWN = tuple(i for i in range(19) if lattice_vel[i][1] == -1)
FLAT_Y = tuple(i for i in range(19) if lattice_vel[i][1] == 0)

COLUMN = EAST + (MASK,) + WEST + FLAT_X + (20, 21, 22, 23)
PLACE = {field: at for at, field in enumerate(COLUMN)}
HALF = len(COLUMN) // 2
TROWS = HALF * 8
SIDE = 20
PLANE = 40
EDGE = 4
INNER = DEPTH - EDGE
YFIELDS = 21


def up_down(rows_up):
    moving = UP if rows_up else DOWN
    near = FLAT_Y + moving + (MASK,)
    far = moving + (MASK,)
    return [(f, True) for f in near] + [(f, False) for f in far]


def moments(g):
    w0, w1, w2 = lattice_weight[0], lattice_weight[1], lattice_weight[7]
    axis = g[1] + g[2] + g[3] + g[4] + g[5] + g[6]
    diag = (g[7] + g[8] + g[9] + g[10]) + (g[11] + g[12] + g[13] + g[14]) + (g[15] + g[16] + g[17] + g[18])
    density = w0 * g[0] + w1 * axis + w2 * diag
    inverse = 1.0 / density
    d78, d910 = g[7] - g[8], g[9] - g[10]
    d1112, d1314 = g[11] - g[12], g[13] - g[14]
    d1516, d1718 = g[15] - g[16], g[17] - g[18]
    mx = w1 * (g[1] - g[2]) + w2 * ((d78 + d910) + (d1112 + d1314))
    my = w1 * (g[3] - g[4]) + w2 * ((d78 - d910) + (d1516 + d1718))
    mz = w1 * (g[5] - g[6]) + w2 * ((d1112 - d1314) + (d1516 - d1718))
    return density, mx * inverse, my * inverse, mz * inverse


def equilibria(density, vx, vy, vz, wanted=range(19)):
    base = density - 1.5 * density * (vx * vx + vy * vy + vz * vz)
    linear = 3.0 * density
    square = 4.5 * density
    out = {}
    for i in wanted:
        if i in out:
            continue
        if i == 0:
            out[0] = base
            continue
        first = i if i % 2 == 1 else i - 1
        cx, cy, cz = lattice_vel[first]
        p = None
        for c, v in ((cx, vx), (cy, vy), (cz, vz)):
            if c == 0:
                continue
            p = (v if c == 1 else -v) if p is None else (p + v if c == 1 else p - v)
        even = base + square * p * p
        odd = linear * p
        out[first] = even + odd
        out[first + 1] = even - odd
    return out


def lanes(shape):
    return lax.broadcasted_iota(jnp.int32, shape, len(shape) - 1)


def ramp(x, start, finish):
    width = (finish - start).astype(jnp.float32)
    angle = math.pi * ((x - start).astype(jnp.float32) + 0.5) / width
    inside = (x >= start) & (x < finish)
    return jnp.where(inside, fringe_peak * jnp.sin(angle) ** 2, 0.0)


def relax_kernel(ways, sc, prm, pops, solid, relaxed, lam, zmsg, *rest):
    ysm, ymn, grid = rest[: len(ways)], rest[len(ways) : 2 * len(ways)], rest[-1]
    gx, gy, rp = sc[0], sc[1], sc[2]
    x0 = gx * COLS
    off = rp - x0
    lane = lanes((8, 128))
    sub = lax.broadcasted_iota(jnp.int32, (8, 128), 0)
    special = jnp.where(
        lane < 3, x0 - 2 + lane, jnp.where(lane < 6, x0 + COLS - 4 + lane, rp - 7 + lane)
    )
    lam[...] = ramp(jnp.where(sub == 0, x0 + lane, special), sc[3], sc[4])

    col = lane % 8
    slot = lane // 8
    place = off + col - 5
    here = (place >= 0) & (place < COLS) & (col >= 4) & (col < 7)
    owner = (off >= 0) & (off < COLS)
    static = col < 4
    shift0 = 5 - off + 8 * 128 * 64
    for y in range(ROWS):
        values = jnp.zeros((8, 128), jnp.float32)
        for k in range(4):
            values = jnp.where((slot == k) & (col == 7) & owner, prm[k, y], values)
        for chunk in range(DEPTH // 8):
            rows = pl.ds(16 * chunk + y, 8, stride=2)
            g = [pops[i, rows, :] for i in range(19)]
            wall = solid[rows, :] == 1
            density, vx, vy, vz = moments(g)
            eq = equilibria(density, vx, vy, vz)
            field = {}
            for i in range(19):
                loose = g[i] - relax_rate * (g[i] - eq[i])
                field[i] = jnp.where(wall, g[opposite[i]], loose)
            field[MASK] = jnp.where(wall, 1.0, 0.0)
            field[20], field[21], field[22], field[23] = density, vx, vy, vz
            here_z = pl.ds(8 * chunk, 8)
            for f in range(20):
                relaxed[f, y, here_z, :] = field[f]
            for half in range(2):
                fixed = jnp.zeros((8, 128), jnp.float32)
                moving = jnp.zeros((8, 128), jnp.float32)
                for k in range(HALF):
                    v = field[COLUMN[half * HALF + k]]
                    mine = slot == k
                    if half * HALF + k < SIDE:
                        fixed = jnp.where(mine, pltpu.roll(v, 2 + 8 * k, 1), fixed)
                    moving = jnp.where(mine, pltpu.roll(v, (shift0 + 8 * k) % 128, 1), moving)
                rest_of = values if half == 0 else jnp.zeros((8, 128), jnp.float32)
                packed = jnp.where(static, fixed, jnp.where(here, moving, rest_of))
                grid[pl.ds((y * 2 + half) * DEPTH + 8 * chunk, 8), :] = packed
    columns = grid[...].T[:TROWS]
    zmsg[pl.ds(0, TROWS), :] = columns
    for f in range(20):
        for y in range(ROWS):
            at = TROWS + (f * 2 + y) * EDGE
            zmsg[pl.ds(at, 2), :] = relaxed[f, y, pl.ds(0, 2), :]
            zmsg[pl.ds(at + 2, 2), :] = relaxed[f, y, pl.ds(DEPTH - 2, 2), :]

    def pack(way, small, bulk):
        for n, (f, near) in enumerate(up_down(way)):
            y = 1 if near == way else 0
            at = TROWS + n * EDGE
            small[pl.ds(at, 2), :] = relaxed[f, y, pl.ds(0, 2), :]
            small[pl.ds(at + 2, 2), :] = relaxed[f, y, pl.ds(DEPTH - 2, 2), :]
            bulk[pl.ds(n * INNER, INNER), :] = relaxed[f, y, pl.ds(2, INNER), :]

    for at, way in enumerate(ways):
        ysm[at][pl.ds(0, TROWS), :] = columns
        if way is None:

            @pl.when(gy == 0)
            def _():
                pack(True, ysm[at], ymn[at])

            @pl.when(gy != 0)
            def _():
                pack(False, ysm[at], ymn[at])

        else:
            pack(way, ysm[at], ymn[at])


def join(mine, other):
    even = (lanes(mine.shape) // DEPTH) % 2 == 0
    first = jnp.where(even, mine, pltpu.roll(other, DEPTH, 1))
    second = jnp.where(even, pltpu.roll(mine, 128 - DEPTH, 1), other)
    return first, second


def cross_kernel(pairs, swap, sc, *refs):
    blocks = refs[: 2 * pairs]
    full, right, left, plane = refs[2 * pairs :]
    gy = sc[1]
    for n in range(pairs):
        first, second = join(
            blocks[2 * n][pl.ds(0, TROWS), :], blocks[2 * n + 1][pl.ds(0, TROWS), :]
        )
        full[n, pl.ds(0, TROWS), :] = first
        full[n, pl.ds(TROWS, TROWS), :] = second
        for c in range(2):
            at = (n * 2 + c) * SIDE
            right[pl.ds(at, SIDE), :] = full[n, pl.ds(c, SIDE, stride=8), :]
            left[pl.ds(at, SIDE), :] = full[n, pl.ds(2 + c, SIDE, stride=8), :]
        if n == 0 or swap:
            base = 0
            if swap:
                base = pl.multiple_of((gy if n == 0 else 1 - gy) * PLANE, 8)
            plane[pl.ds(base, 6), :] = full[n, pl.ds(4, 6, stride=8), :]
            plane[pl.ds(base + 6, 24), :] = full[n, pl.ds(5, 24, stride=8), :]
            plane[pl.ds(base + 30, 6), :] = full[n, pl.ds(5 * 8 + 6, 6, stride=8), :]
            plane[pl.ds(base + 36, 4), :] = full[n, pl.ds(7, 4, stride=8), :]
    if swap:
        tail = pairs * 2 * SIDE
        right[pl.ds(tail, 2 * PLANE), :] = plane[...]
        left[pl.ds(tail, 2 * PLANE), :] = plane[...]


def strips_kernel(pairs, slots, total_y, total_x, sc, lam, full, west, east, plane_in, out, side, deck, shelf):
    gx, gy, rp = sc[0], sc[1], sc[2]
    last_x = sc[5]
    deep = deck.shape[0] // PLANE
    side[...] = jnp.zeros_like(side)
    deck[...] = jnp.zeros_like(deck)
    shelf[...] = jnp.zeros_like(shelf)

    def apart(v):
        low = lanes(v.shape) < SPAN
        turned = pltpu.roll(v, SPAN, 1)
        return jnp.where(low, v, turned), jnp.where(low, turned, v)

    def lay(strip, c, first, v):
        top, bottom = apart(v)
        side[strip, c, pl.ds(first, SIDE, stride=8), :] = top
        side[strip, c, pl.ds(first + 1, SIDE, stride=8), :] = bottom

    def spread(n, first):
        sides = (n * 2) * SIDE
        lay(0, 0, first, west[pl.ds(sides, SIDE), :])
        lay(0, 1, first, west[pl.ds(sides + SIDE, SIDE), :])
        lay(0, 2, first, full[n, pl.ds(2, SIDE, stride=8), :])
        lay(1, 0, first, full[n, pl.ds(1, SIDE, stride=8), :])
        lay(1, 1, first, east[pl.ds(sides, SIDE), :])
        lay(1, 2, first, east[pl.ds(sides + SIDE, SIDE), :])

    for n in range(pairs):
        if slots[n] is None:

            @pl.when(gy == 0)
            def _():
                spread(n, 4)

            @pl.when(gy != 0)
            def _():
                spread(n, 0)

        else:
            spread(n, slots[n])
    for n in range(total_y // 2):
        top, bottom = apart(plane_in[pl.ds(n * PLANE, PLANE), :])
        deck[pl.ds(2 * n, PLANE, stride=deep), :] = top
        deck[pl.ds(2 * n + 1, PLANE, stride=deep), :] = bottom

    def deck_at(row):
        return deck[pl.ds(row * deep, deep), :]

    which, ratio, mean_gain, fluct_gain = (deck_at(36 + k) for k in range(4))

    def target(fields):
        def blend(v):
            low, high = v[0:1], v[1:2]
            low = jnp.broadcast_to(low, v.shape)
            high = jnp.broadcast_to(high, v.shape)
            for r in range(1, total_y - 1):
                chosen = which == float(r)
                low = jnp.where(chosen, jnp.broadcast_to(v[r : r + 1], v.shape), low)
                high = jnp.where(chosen, jnp.broadcast_to(v[r + 1 : r + 2], v.shape), high)
            return (1.0 - ratio) * low + ratio * high

        result = [blend(fields[0])]
        for v in fields[1:]:
            mean = jnp.sum(v, axis=1, keepdims=True) * (1.0 / 128.0)
            mean = blend(jnp.broadcast_to(mean, v.shape))
            result.append(mean_gain * mean + fluct_gain * (blend(v) - mean))
        return result

    def local(fields):
        got = []
        for k, v in enumerate(fields):
            shelf[k, pl.ds(8, deep), :] = v
            got.append(shelf[k, pl.ds(6 + 2 * gy, 8), :])
        return got

    def shifted(v, i):
        _, cy, cz = lattice_vel[i]
        if cz:
            v = pltpu.roll(v, cz % 128, 1)
        if cy:
            v = pltpu.roll(v, cy % v.shape[0], 0)
        return v

    def forced(value, gate, goal):
        return value + gate * (goal - value)

    def strip(read, gates, teq, row, edge):
        gate = [(1.0 - read(c, MASK)) * gates[c] for c in range(3)]
        middle = [forced(read(1, i), gate[1], teq[i]) for i in range(19)]
        bottom, top = row == 0, row == total_y - 1
        g = []
        for i in range(19):
            cx, cy, _ = lattice_vel[i]
            if cx == 0:
                v = shifted(middle[i], i)
            else:
                c = 1 - cx
                v = shifted(forced(read(c, i), gate[c], teq[i]), i)
                if cx == -1 and edge is not None:
                    v = jnp.where(edge, middle[i], v)
            if cy == 1:
                v = jnp.where(bottom, middle[opposite[i]], v)
            if cy == -1:
                v = jnp.where(top, middle[mirror_pop[i]], v)
            g.append(v)
        return middle, g, gate

    def lam_at(c, rows):
        return jnp.broadcast_to(lam[1:2, c : c + 1], (rows, 128))

    target0 = target([deck_at(6 + 20 + k) for k in range(4)])
    teq0 = equilibria(*target0)
    start = {0: (0, 0), 1: (6, 0), 2: (30, 5)}

    def read_plane(c, f):
        base, less = start[c]
        return deck_at(base + PLACE[f] - less)

    row = lax.broadcasted_iota(jnp.int32, (deep, 128), 0)
    _, g1, _ = strip(
        read_plane, [lam_at(6 + c, deep) for c in range(3)], teq0, row, rp == total_x - 1
    )
    target1 = target(list(moments(g1)))
    near0, near1 = local(target0), local(target1)
    goal0, goal1 = equilibria(*near0), equilibria(*near1)

    row = lax.broadcasted_iota(jnp.int32, (8, 128), 0) + 2 * gy - 2
    first, second = [], []
    for s, wanted in ((0, EAST), (1, WEST)):

        def read_side(c, f):
            return side[s, c, pl.ds(PLACE[f] * 8, 8), :]

        middle, g1, gate = strip(
            read_side, [lam_at(3 * s + c, 8) for c in range(3)], goal0, row, None
        )
        density, vx, vy, vz = moments(g1)
        eq = equilibria(density, vx, vy, vz, wanted)
        wall = read_side(1, MASK) == 1.0
        for i in wanted:
            loose = g1[i] - relax_rate * (g1[i] - eq[i])
            later = forced(jnp.where(wall, g1[opposite[i]], loose), gate[1], goal1[i])
            a, b = shifted(middle[i], i), shifted(later, i)
            if s == 0:
                a, b = jnp.where(gx == 0, goal0[i], a), jnp.where(gx == 0, goal1[i], b)
            else:
                a = jnp.where(gx == last_x, forced(read_side(0, i), gate[0], goal0[i]), a)
            first.append(a)
            second.append(b)
    blank = [jnp.zeros((16, 128), jnp.float32)]
    for n, rows in enumerate((first + near0 + blank, second + near1 + blank)):
        turned = pltpu.roll(jnp.concatenate(rows, axis=0), 2, 1).T
        out[pl.ds(48 * n, 48), :] = turned[:48]


def steps_kernel(ways, total_y, sc, lam, relaxed, zmsg, cols, *rest):
    count = len(ways)
    bulk, small, small_other = rest[:count], rest[count : 2 * count], rest[2 * count : 3 * count]
    out, early, late = rest[3 * count :]
    gx, gy = sc[0], sc[1]
    at_end = gx == sc[5]
    bottom, top = gy == 0, gy == sc[6]
    lane = lanes((8, 128))
    at_first, at_last = lane == 0, lane == COLS - 1
    zone = jnp.broadcast_to(lam[0:1, :], (8, 128))

    def column(step, index, at):
        return jnp.broadcast_to(cols[pl.ds(48 * step + at, 8), index : index + 1], (8, 128))

    def goals(step, slot, at, wanted):
        return equilibria(*(column(step, 80 + 8 * k + slot, at) for k in range(4)), wanted)

    def finish(slot, fields):
        for chunk in range(5):
            rows = pl.ds(8 * chunk, 8)
            gate = (1.0 - early[MASK, slot, rows, :]) * zone
            goal = goals(0, slot, 8 * chunk, fields)
            for i in fields:
                v = early[i, slot, rows, :]
                early[i, slot, rows, :] = v + gate * (goal[i] - v)

    def pull(ref, slot, lead, step, at, lift, mine):
        r = at - lift
        g = []
        for i in range(19):
            cx, cy, cz = lattice_vel[i]
            v = ref[i, slot - cy - lead, pl.ds(r - cz, 8), :]
            if cx == 1:
                edge = column(step, EAST.index(i) * 8 + slot, at)
                v = jnp.where(at_first, edge, pltpu.roll(v, 1, 1))
            if cx == -1:
                edge = column(step, 40 + WEST.index(i) * 8 + slot, at)
                if step == 1:
                    edge = jnp.where(at_end, ref[i, slot - lead, pl.ds(r, 8), :], edge)
                v = jnp.where(at_last, edge, pltpu.roll(v, COLS - 1, 1))
            if mine and cy == 1 and slot == 2:
                v = jnp.where(bottom, ref[opposite[i], slot - lead, pl.ds(r, 8), :], v)
            if mine and cy == -1 and slot == 3:
                v = jnp.where(top, ref[mirror_pop[i], slot - lead, pl.ds(r, 8), :], v)
            g.append(v)
        return g

    def collide(slot, wanted, mine):
        for chunk in range(5):
            at = 1 + 8 * chunk
            g = pull(early, slot, 0, 0, at, 0, mine)
            density, vx, vy, vz = moments(g)
            eq = equilibria(density, vx, vy, vz, wanted)
            goal = goals(1, slot, at, wanted)
            solid = early[MASK, slot, pl.ds(at, 8), :]
            gate = (1.0 - solid) * zone
            wall = solid == 1.0
            for i in wanted:
                loose = g[i] - relax_rate * (g[i] - eq[i])
                v = jnp.where(wall, g[opposite[i]], loose)
                late[i, slot - 1, pl.ds(8 * chunk, 8), :] = v + gate * (goal[i] - v)

    for f in range(20):
        for y in range(ROWS):
            slot = 2 + y
            at = TROWS + (f * 2 + y) * EDGE
            early[f, slot, pl.ds(2, DEPTH), :] = relaxed[f, y, :, :]
            early[f, slot, pl.ds(DEPTH + 2, 2), :] = zmsg[pl.ds(at, 2), :]
            early[f, slot, pl.ds(0, 2), :] = zmsg[pl.ds(at + 2, 2), :]
    for slot in (2, 3):
        finish(slot, range(19))

    def beside(n, came_up):
        near_slot, far_slot = (1, 0) if came_up else (4, 5)
        for k, (f, near) in enumerate(up_down(came_up)):
            slot = near_slot if near else far_slot
            at = TROWS + k * EDGE
            early[f, slot, pl.ds(0, 2), :] = small_other[n][pl.ds(at + 2, 2), :]
            early[f, slot, pl.ds(2, 2), :] = small[n][pl.ds(at, 2), :]
            early[f, slot, pl.ds(4, INNER), :] = bulk[n][pl.ds(k * INNER, INNER), :]
            early[f, slot, pl.ds(DEPTH, 2), :] = small[n][pl.ds(at + 2, 2), :]
            early[f, slot, pl.ds(DEPTH + 2, 2), :] = small_other[n][pl.ds(at, 2), :]
        moving = UP if came_up else DOWN
        finish(near_slot, FLAT_Y + moving)
        finish(far_slot, moving)
        collide(near_slot, moving, False)

    for n, way in enumerate(ways):
        if way is not False:

            @pl.when(jnp.logical_not(bottom))
            def _():
                beside(n, True)

        if way is not True:

            @pl.when(jnp.logical_not(top))
            def _():
                beside(n, False)

    for slot in (2, 3):
        collide(slot, range(19), True)
    for y in range(ROWS):
        for chunk in range(DEPTH // 8):
            g = pull(late, 2 + y, 1, 1, 2 + 8 * chunk, 1, True)
            for i in range(19):
                out[i, pl.ds(16 * chunk + y, 8, stride=2), :] = g[i]


def call(kernel, outs, scratch, limit, *args, scalars=1):
    smem = pl.BlockSpec(memory_space=pltpu.SMEM)
    vmem = pl.BlockSpec(memory_space=pltpu.VMEM)
    return pl.pallas_call(
        kernel,
        out_shape=[jax.ShapeDtypeStruct(s, jnp.float32) for s in outs],
        in_specs=[smem] * scalars + [vmem] * (len(args) - scalars),
        out_specs=[vmem] * len(outs),
        scratch_shapes=[pltpu.VMEM(s, jnp.float32) for s in scratch],
        compiler_params=pltpu.CompilerParams(vmem_limit_bytes=limit << 20),
    )(*args)


def ring(count, step):
    return [(i, (i + step) % count) for i in range(count)]


def body(populations, solid_mask, recycle_plane, fringe_bounds, interp_rows, interp_weights, mean_scale, fluct_scale):
    size_x, size_y = lax.axis_size("gx"), lax.axis_size("gy")
    total_x, total_y = COLS * size_x, ROWS * size_y
    gx, gy = lax.axis_index("gx"), lax.axis_index("gy")
    swap = size_y == 2
    ways = (None,) if swap else (True, False)
    pairs = 1 + len(ways)
    sc = jnp.stack([gx, gy, recycle_plane[0], fringe_bounds[0], fringe_bounds[1], jnp.int32(size_x - 1), jnp.int32(size_y - 1)])
    prm = jnp.stack([interp_rows.astype(jnp.float32), interp_weights, mean_scale, fluct_scale])
    pops = populations.reshape(19, DEPTH * ROWS, COLS)
    solid = solid_mask.reshape(DEPTH * ROWS, COLS)

    small_rows = TROWS + 88
    bulk_rows = 592
    z_rows = TROWS + 40 * EDGE
    made = call(
        functools.partial(relax_kernel, ways),
        [(20, ROWS, DEPTH, COLS), (8, 128), (z_rows, 128)] + [(small_rows, 128)] * len(ways) + [(bulk_rows, 128)] * len(ways),
        [(128, 128)],
        8,
        sc,
        prm,
        pops,
        solid,
        scalars=2,
    )
    relaxed, lam, z_out = made[:3]
    small_out, bulk_out = made[3 : 3 + len(ways)], made[3 + len(ways) :]

    def across(v, way):
        if way is None:
            return lax.ppermute(v, "gy", ring(2, 1))
        step = 1 if way else -1
        return lax.ppermute(v, "gy", [(i, i + step) for i in range(size_y) if 0 <= i + step < size_y])

    small = [across(v, way) for v, way in zip(small_out, ways)]
    bulk = [across(v, way) for v, way in zip(bulk_out, ways)]
    z_in = lax.ppermute(z_out, "gz", ring(2, 1))
    small_other = [lax.ppermute(v, "gz", ring(2, 1)) for v in small]

    blocks = [z_out, z_in]
    for a, b in zip(small, small_other):
        blocks += [a, b]
    edge_rows = pairs * 2 * SIDE + (2 * PLANE if swap else 0)
    full, right, left, plane = call(
        functools.partial(cross_kernel, pairs, swap),
        [(pairs, 2 * TROWS, 128), (edge_rows, 128), (edge_rows, 128), (PLANE * (2 if swap else 1), 128)],
        [],
        4,
        sc,
        *blocks,
    )
    west = lax.ppermute(right, "gx", ring(size_x, 1))
    east = lax.ppermute(left, "gx", ring(size_x, -1))
    if swap and size_x == 4:
        tail = pairs * 2 * SIDE
        far = lax.ppermute(plane, "gx", ring(4, 2))
        plane = plane + far + west[tail:] + east[tail:]
    elif swap:
        plane = lax.psum(plane, "gx")
    else:
        spot = jnp.zeros((size_y, PLANE, 128), jnp.float32)
        spot = lax.dynamic_update_slice(spot, plane[None], (gy, 0, 0))
        plane = lax.psum(spot, ("gx", "gy")).reshape(size_y * PLANE, 128)

    deep = max(8, total_y)
    slots = (2,) + ((None,) if swap else (0, 4))
    (cols,) = call(
        functools.partial(strips_kernel, pairs, slots, total_y, total_x),
        [(96, 128)],
        [(2, 3, SIDE * 8, 128), (PLANE * deep, 128), (4, 16 + deep, 128)],
        8,
        sc,
        lam,
        full,
        west,
        east,
        plane,
    )
    (out,) = call(
        functools.partial(steps_kernel, ways, total_y),
        [(19, DEPTH * ROWS, COLS)],
        [(20, 6, 48, 128), (19, 4, 48, 128)],
        12,
        sc,
        lam,
        relaxed,
        z_in,
        cols,
        *bulk,
        *small,
        *small_other,
    )
    return out.reshape(populations.shape)


def solution(mesh):
    placed = (
        P(None, ("parts", "gz"), "gy", "gx"),
        P(("parts", "gz"), "gy", "gx"),
        P(),
        P(),
        P("gy"),
        P("gy"),
        P("gy"),
        P("gy"),
    )
    return jax.shard_map(
        body,
        mesh=mesh,
        in_specs=placed,
        out_specs=P(None, ("parts", "gz"), "gy", "gx"),
        check_vma=False,
    )
```

time: 145 us -> 29 us (0.20)
  waiting for transfers between devices: 53.9 us -> 9.18 us
  blocking collectives: 38.9 us -> 0 us
  other arithmetic: 22.3 us -> 1.37 us
  local copies, waits for them, and re-layouts: 14.6 us -> 1.81 us
  Pallas kernels: 0 us -> 6.16 us
  between operations: 3.07 us -> 0.7 us
  starting transfers between devices: 11.2 us -> 9.56 us
    ppermute x12 -> x7, waiting for transfers between devices: 53.9 us -> 9.18 us  [the longest x1 4.11 us: body(): far = lax.ppermute(plane, 'gx', ring(4, 2))]
    psum x4 -> x0, blocking collectives: 29.4 us -> none  [the longest x2 24.5 us: spread(): return lax.psum(jnp.where(mine, array, jnp.zeros_like(array)), axis)]
    unnamed x53 -> x0, other arithmetic: 12.3 us -> none
    all_gather x2 -> x0, blocking collectives: 9.57 us -> none  [body(): gathered = lax.all_gather(recycle_rows, 'gy', axis=2, tiled=True)]
    pallas_call x0 -> x4, Pallas kernels: none -> 6.16 us  [call(): pl.pallas_call(kernel, out_shape=[jax.ShapeDtypeStruct(s, jnp.float32) fo...]
    gather x8 -> x0, local copies, waits for them, and re-layouts: 4.99 us -> none  [the longest x2 1.26 us: rescale(): upper = jnp.take(plane, row_index + 1, axis=2)]
    slice x10 -> x0, local copies, waits for them, and re-layouts: 3.44 us -> none  [the longest x3 1.5 us: with_halo(): head = lax.slice_in_dim(cells, 0, width, axis=dim)]
    add x6 -> x1, other arithmetic: 2.43 us -> 0.01 us  [body(): plane = plane + far + west[tail:] + east[tail:]]
  transfers between devices with their start and end apart: 12 -> 7, of which waited for: 10 -> 4; matrix products, arithmetic and copies ran while one was open for 1% -> 0% of each run, Pallas kernels for 0% -> 5%
where the time goes in v1:
time: 29 us; the launch traced here: 28.8 us
  starting transfers between devices  9.56 us (33%)
  waiting for transfers between devices  9.18 us (32%)
  Pallas kernels  6.16 us (21%)
  local copies, waits for them, and re-layouts  1.81 us (6%)
  other arithmetic  1.37 us (5%)
  between operations  0.7 us (2%)
    pallas_call x4, Pallas kernels, call(): pl.pallas_call(kernel, out_shape=[jax.ShapeDtypeStruct(s, jnp.float32) fo...  6.16 us
    ppermute x2, starting transfers between devices, across(): return lax.ppermute(v, 'gy', ring(2, 1))  4.68 us
    ppermute x1, waiting for transfers between devices, body(): far = lax.ppermute(plane, 'gx', ring(4, 2))  4.11 us
    ppermute x2, waiting for transfers between devices, across(): return lax.ppermute(v, 'gy', ring(2, 1))  3.77 us
    ppermute x1, starting transfers between devices, body(): east = lax.ppermute(left, 'gx', ring(size_x, -1))  2.09 us
    ppermute x1, starting transfers between devices, body(): west = lax.ppermute(right, 'gx', ring(size_x, 1))  1.99 us
    another operation x2, other arithmetic, body(): jnp.stack([interp_rows.astype(jnp.float32), interp_weights, mean_scale, f...  1.36 us
    ppermute x1, waiting for transfers between devices, body(): small_other = [lax.ppermute(v, 'gz', ring(2, 1)) for v in small]  1.29 us
  transfers between devices with their start and end apart: 7, of which 4 were waited for; matrix products, arithmetic and copies ran while one was open for 0% of the time, Pallas kernels for 5%

profile of v1, /device:TPU:0, one launch (start us, length us, event | category | flops | bytes accessed | tf_op | source)
XLA Modules:
  0.0 28.8 jit_solution(9287016044926489219)
XLA Ops:
  0.0 0.0 copy-start.1
  0.7 0.7 %convert_bitcast_fusion = f32[1,2]{1,0:T(1,128)S(1)} fusion(s32[2]{0:T(128)} %param.12), kind=kLoop, calls=%fused_computation.3 | loop fusion | flops 2 | bytes 16 | tf_op jit(solution)/shard_map/stack | solution.py:523
  1.3 0.7 %pad_maximum_fusion.prm = f32[4,2]{1,0:T(4,128)S(1)} fusion(f32[1,2]{1,0:T(1,128)} %bitcast.12, f32[1,2]{1,0:T(1,128)} %bitcast.13, f32[1,2]{1,0:T(1,128)} %bitcast.14, f32[1,2]{1,0:T(1,128)S(1)} %convert_bitcast_fusion), kind=kLoop, calls=%fused_computation.2 | loop fusion | flops 24 | bytes 64 | tf_op jit(solution)/shard_map/stack | solution.py:523
  2.0 0.7 %stack.26.sc = s32[7]{0:T(128)S(1)} concatenate(s32[1]{0:T(128)} %bitcast, s32[1]{0:T(128)} %bitcast.1, s32[1]{0:T(128)S(6)} %copy.9, s32[2]{0:T(128)} %param.11, s32[1]{0:T(128)} %constant.11.clone.1, s32[1]{0:T(128)} %constant.12.clone.1), dimensions={0} | concatenate | bytes 56 | tf_op jit(solution)/shard_map/stack | solution.py:522
  2.7 0.0 copy-done.1
  2.8 0.0 copy-start
  2.8 1.1 %copy-done = f32[19,32,2,128]{3,2,1,0:T(2,128)S(1)} copy-done((f32[19,32,2,128]{3,2,1,0:T(2,128)S(1)}, f32[19,32,2,128]{3,2,1,0:T(2,128)}, u32[]{:S(2)}) %copy-start) | copy-done | bytes 622616
  3.8 1.2 %shard_map.82 = (f32[20,2,32,128]{3,2,1,0:T(8,128)S(1)}, f32[8,128]{1,0:T(8,128)S(1)}, f32[256,128]{1,0:T(8,128)S(1)}, f32[184,128]{1,0:T(8,128)S(1)}, f32[592,128]{1,0:T(8,128)S(1)}) custom-call(s32[7]{0:T(128)S(1)} %stack.26.sc, f32[4,2]{1,0:T(4,128)S(1)} %pad_maximum_fusion.prm, f32[19,64,128]{2,1,0:T(8,128)S(1)} %bitcast.10, s32[64,128]{1,0:T(8,128)S(1)} %bitcast.11), custom_call_target="tpu_custom_call" | custom-call | tf_op jit(solution)/shard_map/pallas_call | solution.py:501
  5.0 3.0 %collective-permute-start.1 = (f32[184,128]{1,0:T(8,128)S(1)}, f32[184,128]{1,0:T(8,128)S(1)}, u32[]{:S(2)}, u32[]{:S(2)}) collective-permute-start(f32[184,128]{1,0:T(8,128)S(1)} %get-tuple-element.17), channel_id=1, source_target_pairs={{0,2},{2,0},{1,3},{3,1},{4,6},{6,4},{5,7},{7,5},{8,10},{10,8},{9,1... | collective-permute-start | bytes 282632 | tf_op jit(solution)/shard_map/ppermute | solution.py:546
  8.0 0.0 collective-permute-start
  8.0 2.7 %collective-permute-done.1.refs_2_.rest_1_ = f32[184,128]{1,0:T(8,128)S(1)} collective-permute-done((f32[184,128]{1,0:T(8,128)S(1)}, f32[184,128]{1,0:T(8,128)S(1)}, u32[]{:S(2)}, u32[]{:S(2)}) %collective-permute-start.1) | collective-permute-done | bytes 94240 | tf_op jit(solution)/shard_map/ppermute | solution.py:546
  10.7 0.0 collective-permute-start.2
  10.7 0.0 collective-permute-done.refs_1_.zmsg
  10.8 1.3 %collective-permute-done.2.refs_3_.rest_2_ = f32[184,128]{1,0:T(8,128)S(1)} collective-permute-done((f32[184,128]{1,0:T(8,128)S(1)}, f32[184,128]{1,0:T(8,128)S(1)}, u32[]{:S(2)}, u32[]{:S(2)}) %collective-permute-start.2) | collective-permute-done | bytes 94240 | tf_op jit(solution)/shard_map/ppermute | solution.py:553
  12.0 0.7 %shard_map.83 = (f32[2,192,128]{2,1,0:T(8,128)S(1)}, f32[160,128]{1,0:T(8,128)S(1)}, f32[160,128]{1,0:T(8,128)S(1)}, f32[80,128]{1,0:T(8,128)S(1)}) custom-call(s32[7]{0:T(128)S(1)} %stack.26.sc, f32[256,128]{1,0:T(8,128)S(1)} %get-tuple-element.16.refs_0_, f32[256,128]{1,0:T(8,128)S(1)} %collective-permute-done.refs_1_.zmsg, ...), custom_call_target="tpu_custom_call" | custom-call | tf_op jit(solution)/shard_map/pallas_call | solution.py:501
  12.7 2.0 %collective-permute-start.3 = (f32[160,128]{1,0:T(8,128)S(1)}, f32[160,128]{1,0:T(8,128)S(1)}, u32[]{:S(2)}, u32[]{:S(2)}) collective-permute-start(f32[160,128]{1,0:T(8,128)S(1)} %get-tuple-element.19), channel_id=1, source_target_pairs={{0,4},{4,8},{8,12},{12,0},{1,5},{5,9},{9,13},{13,1},{2,6},{6,10},{... | collective-permute-start | bytes 245768 | tf_op jit(solution)/shard_map/ppermute | solution.py:567
  14.7 2.1 %collective-permute-start.4 = (f32[160,128]{1,0:T(8,128)S(1)}, f32[160,128]{1,0:T(8,128)S(1)}, u32[]{:S(2)}, u32[]{:S(2)}) collective-permute-start(f32[160,128]{1,0:T(8,128)S(1)} %get-tuple-element.20), channel_id=1, source_target_pairs={{0,12},{4,0},{8,4},{12,8},{1,13},{5,1},{9,5},{13,9},{2,14},{6,2},{... | collective-permute-start | bytes 245768 | tf_op jit(solution)/shard_map/ppermute | solution.py:568
  16.8 1.7 %collective-permute-start.6 = (f32[592,128]{1,0:T(8,128)S(1)}, f32[592,128]{1,0:T(8,128)S(1)}, u32[]{:S(2)}, u32[]{:S(2)}) collective-permute-start(f32[592,128]{1,0:T(8,128)S(1)} %get-tuple-element.22), channel_id=1, source_target_pairs={{0,2},{2,0},{1,3},{3,1},{4,6},{6,4},{5,7},{7,5},{8,10},{10,8},{9,1... | collective-permute-start | bytes 909320 | tf_op jit(solution)/shard_map/ppermute | solution.py:546
  18.5 0.8 %collective-permute-start.5 = (f32[80,128]{1,0:T(8,128)S(1)}, f32[80,128]{1,0:T(8,128)S(1)}, u32[]{:S(2)}, u32[]{:S(2)}) collective-permute-start(f32[80,128]{1,0:T(8,128)S(1)} %get-tuple-element.21), channel_id=1, source_target_pairs={{0,8},{4,12},{8,0},{12,4},{1,9},{5,13},{9,1},{13,5},{2,10},{6,14},... | collective-permute-start | bytes 122888 | tf_op jit(solution)/shard_map/ppermute | solution.py:571
  19.3 4.1 %collective-permute-done.5 = f32[80,128]{1,0:T(8,128)S(1)} collective-permute-done((f32[80,128]{1,0:T(8,128)S(1)}, f32[80,128]{1,0:T(8,128)S(1)}, u32[]{:S(2)}, u32[]{:S(2)}) %collective-permute-start.5) | collective-permute-done | bytes 40992 | tf_op jit(solution)/shard_map/ppermute | solution.py:571
  23.4 0.0 collective-permute-done.3.west
  23.4 0.0 collective-permute-done.4.east
  23.4 1.3 %shard_map.84.cols = f32[96,128]{1,0:T(8,128)S(1)} custom-call(s32[7]{0:T(128)S(1)} %stack.26.sc, f32[8,128]{1,0:T(8,128)S(1)} %get-tuple-element.14.lam, f32[2,192,128]{2,1,0:T(8,128)S(1)} %get-tuple-element.18.full, f32[160,128]{1,0:T(8,128)S(1)} %collective-permute-done.3.west, f32[160,128]{1,0:T(8,128)S(1)} %collective-permute-done.4.east, ...), custom_call_target="tpu_custom_call" | custom-call | tf_op jit(solution)/shard_map/pallas_call | solution.py:501
  24.7 1.1 %collective-permute-done.6.rest_0_ = f32[592,128]{1,0:T(8,128)S(1)} collective-permute-done((f32[592,128]{1,0:T(8,128)S(1)}, f32[592,128]{1,0:T(8,128)S(1)}, u32[]{:S(2)}, u32[]{:S(2)}) %collective-permute-start.6) | collective-permute-done | bytes 303136 | tf_op jit(solution)/shard_map/ppermute | solution.py:546
  25.8 3.0 %shard_map.85 = f32[19,64,128]{2,1,0:T(8,128)} custom-call(s32[7]{0:T(128)S(1)} %stack.26.sc, f32[8,128]{1,0:T(8,128)S(1)} %get-tuple-element.14.lam, f32[20,2,32,128]{3,2,1,0:T(8,128)S(1)} %get-tuple-element.15.relaxed, f32[256,128]{1,0:T(8,128)S(1)} %collective-permute-done.refs_1_.zmsg, f32[96,128]{1,0:T(8,128)S(1)} %shard_map.84.cols, ...), custom_call_target="tpu_custom_call" | custom-call | tf_op jit(solution)/shard_map/pallas_call | solution.py:501
  (1 shorter events, 0.0 us)
Async XLA Ops:
  0.0 2.8 %copy-start.1 = (s32[32,2,128]{2,1,0:T(2,128)S(1)}, s32[32,2,128]{2,1,0:T(2,128)}, u32[]{:S(2)}) copy-start(s32[32,2,128]{2,1,0:T(2,128)} %param.9) | copy-start | bytes 98308
  2.8 1.1 %copy-start = (f32[19,32,2,128]{3,2,1,0:T(2,128)S(1)}, f32[19,32,2,128]{3,2,1,0:T(2,128)}, u32[]{:S(2)}) copy-start(f32[19,32,2,128]{3,2,1,0:T(2,128)} %param.8) | copy-start | bytes 1867780
  5.0 5.7 %collective-permute-start.1 = (f32[184,128]{1,0:T(8,128)S(1)}, f32[184,128]{1,0:T(8,128)S(1)}, u32[]{:S(2)}, u32[]{:S(2)}) collective-permute-start(f32[184,128]{1,0:T(8,128)S(1)} %get-tuple-element.17), channel_id=1, source_target_pairs={{0,2},{2,0},{1,3},{3,1},{4,6},{6,4},{5,7},{7,5},{8,10},{10,8},{9,1... | collective-permute-start | bytes 282632 | tf_op jit(solution)/shard_map/ppermute | solution.py:546
  8.0 2.7 %collective-permute-start = (f32[256,128]{1,0:T(8,128)S(1)}, f32[256,128]{1,0:T(8,128)S(1)}, u32[]{:S(2)}, u32[]{:S(2)}) collective-permute-start(f32[256,128]{1,0:T(8,128)S(1)} %get-tuple-element.16.refs_0_), channel_id=1, source_target_pairs={{0,1},{1,0},{2,3},{3,2},{4,5},{5,4},{6,7},{7,6},{8,9},{9,8},{10,11... | collective-permute-start | bytes 393224 | tf_op jit(solution)/shard_map/ppermute | solution.py:552
  10.7 1.3 %collective-permute-start.2 = (f32[184,128]{1,0:T(8,128)S(1)}, f32[184,128]{1,0:T(8,128)S(1)}, u32[]{:S(2)}, u32[]{:S(2)}) collective-permute-start(f32[184,128]{1,0:T(8,128)S(1)} %collective-permute-done.1.refs_2_.rest_1_), channel_id=1, source_target_pairs={{0,1},{1,0},{2,3},{3,2},{4,5},{5,4},{6,7},{7,6},{8,9},{9,8},{10,11... | collective-permute-start | bytes 282632 | tf_op jit(solution)/shard_map/ppermute | solution.py:553
  12.7 10.6 %collective-permute-start.3 = (f32[160,128]{1,0:T(8,128)S(1)}, f32[160,128]{1,0:T(8,128)S(1)}, u32[]{:S(2)}, u32[]{:S(2)}) collective-permute-start(f32[160,128]{1,0:T(8,128)S(1)} %get-tuple-element.19), channel_id=1, source_target_pairs={{0,4},{4,8},{8,12},{12,0},{1,5},{5,9},{9,13},{13,1},{2,6},{6,10},{... | collective-permute-start | bytes 245768 | tf_op jit(solution)/shard_map/ppermute | solution.py:567
  14.7 8.7 %collective-permute-start.4 = (f32[160,128]{1,0:T(8,128)S(1)}, f32[160,128]{1,0:T(8,128)S(1)}, u32[]{:S(2)}, u32[]{:S(2)}) collective-permute-start(f32[160,128]{1,0:T(8,128)S(1)} %get-tuple-element.20), channel_id=1, source_target_pairs={{0,12},{4,0},{8,4},{12,8},{1,13},{5,1},{9,5},{13,9},{2,14},{6,2},{... | collective-permute-start | bytes 245768 | tf_op jit(solution)/shard_map/ppermute | solution.py:568
  16.8 9.0 %collective-permute-start.6 = (f32[592,128]{1,0:T(8,128)S(1)}, f32[592,128]{1,0:T(8,128)S(1)}, u32[]{:S(2)}, u32[]{:S(2)}) collective-permute-start(f32[592,128]{1,0:T(8,128)S(1)} %get-tuple-element.22), channel_id=1, source_target_pairs={{0,2},{2,0},{1,3},{3,1},{4,6},{6,4},{5,7},{7,5},{8,10},{10,8},{9,1... | collective-permute-start | bytes 909320 | tf_op jit(solution)/shard_map/ppermute | solution.py:546
  18.5 4.9 %collective-permute-start.5 = (f32[80,128]{1,0:T(8,128)S(1)}, f32[80,128]{1,0:T(8,128)S(1)}, u32[]{:S(2)}, u32[]{:S(2)}) collective-permute-start(f32[80,128]{1,0:T(8,128)S(1)} %get-tuple-element.21), channel_id=1, source_target_pairs={{0,8},{4,12},{8,0},{12,4},{1,9},{5,13},{9,1},{13,5},{2,10},{6,14},... | collective-permute-start | bytes 122888 | tf_op jit(solution)/shard_map/ppermute | solution.py:571

commit v2 on v1

--- a/solution.py
+++ b/solution.py
@@ -38,8 +38,8 @@
 DEPTH, ROWS, COLS = 32, 2, 128
 SPAN = 2 * DEPTH
 MASK = 19
-EAST = tuple(i for i in range(19) if lattice_vel[i][0] == 1)
-WEST = tuple(i for i in range(19) if lattice_vel[i][0] == -1)
+EAST = (1, 11, 13, 7, 9)
+WEST = (8, 10, 2, 12, 14)
 FLAT_X = tuple(i for i in range(19) if lattice_vel[i][0] == 0)
 UP = tuple(i for i in range(19) if lattice_vel[i][1] == 1)
 DOWN = tuple(i for i in range(19) if lattice_vel[i][1] == -1)
@@ -50,10 +50,16 @@
 HALF = len(COLUMN) // 2
 TROWS = HALF * 8
 SIDE = 20
-PLANE = 40
+TO_EAST = ((0, 0, 8), (0, 11, 9), (1, 0, 6))
+TO_WEST = ((0, 3, 8), (0, 11, 9), (1, 5, 6))
+TRAVEL = 23
+DECK = ((4, 0, 6), (5, 0, 24), (6, 5, 6), (7, 0, 4))
+DECK_AT = {4: 0, 5: 6, 6: 30 - 5, 7: 36}
+DECK_ROWS = 40
+SUMS = 11
 EDGE = 4
 INNER = DEPTH - EDGE
-YFIELDS = 21
+PIECES = 2
 
 
 def up_down(rows_up):
@@ -63,19 +69,27 @@
     return [(f, True) for f in near] + [(f, False) for f in far]
 
 
-def moments(g):
+def sums(g):
     w0, w1, w2 = lattice_weight[0], lattice_weight[1], lattice_weight[7]
     axis = g[1] + g[2] + g[3] + g[4] + g[5] + g[6]
     diag = (g[7] + g[8] + g[9] + g[10]) + (g[11] + g[12] + g[13] + g[14]) + (g[15] + g[16] + g[17] + g[18])
     density = w0 * g[0] + w1 * axis + w2 * diag
-    inverse = 1.0 / density
     d78, d910 = g[7] - g[8], g[9] - g[10]
     d1112, d1314 = g[11] - g[12], g[13] - g[14]
     d1516, d1718 = g[15] - g[16], g[17] - g[18]
     mx = w1 * (g[1] - g[2]) + w2 * ((d78 + d910) + (d1112 + d1314))
     my = w1 * (g[3] - g[4]) + w2 * ((d78 - d910) + (d1516 + d1718))
     mz = w1 * (g[5] - g[6]) + w2 * ((d1112 - d1314) + (d1516 - d1718))
+    return density, mx, my, mz
+
+
+def velocity(density, mx, my, mz):
+    inverse = 1.0 / density
     return density, mx * inverse, my * inverse, mz * inverse
+
+
+def moments(g):
+    return velocity(*sums(g))
 
 
 def equilibria(density, vx, vy, vz, wanted=range(19)):
@@ -114,9 +128,29 @@
     return jnp.where(inside, fringe_peak * jnp.sin(angle) ** 2, 0.0)
 
 
-def relax_kernel(ways, sc, prm, pops, solid, relaxed, lam, zmsg, *rest):
-    ysm, ymn, grid = rest[: len(ways)], rest[len(ways) : 2 * len(ways)], rest[-1]
-    gx, gy, rp = sc[0], sc[1], sc[2]
+def relax_kernel(ways, total_x, *refs):
+    recycle, pops_in, solid_in = refs[:3]
+    small_in = refs[3:8]
+    relaxed, lam, zmsg = refs[8:11]
+    rest = refs[11:]
+    ysm, ymn = rest[: len(ways)], rest[len(ways) : 2 * len(ways)]
+    grid, pops, solid = rest[2 * len(ways) : 2 * len(ways) + 3]
+    small, sem = rest[2 * len(ways) + 3 : -1], rest[-1]
+    loads = [
+        [pltpu.make_async_copy(a.at[..., rows, :], b.at[..., rows, :], sem.at[2 * n + m]) for m, (a, b) in enumerate(((pops_in, pops), (solid_in, solid)))]
+        for n, rows in enumerate(pl.ds(n * 2 * DEPTH // PIECES, 2 * DEPTH // PIECES) for n in range(PIECES))
+    ]
+    pieces = DEPTH // 8
+    scalars = [pltpu.make_async_copy(a, b, sem.at[2 * PIECES + n]) for n, (a, b) in enumerate(zip(small_in, small))]
+    for copy in loads[0] + scalars:
+        copy.start()
+    for load in loads[1:]:
+        for copy in load:
+            copy.start()
+    for copy in scalars:
+        copy.wait()
+    bounds, rows_in, weights_in, mean_in, fluct_in = small
+    gx, gy, rp = lax.axis_index("gx"), lax.axis_index("gy"), recycle[0]
     x0 = gx * COLS
     off = rp - x0
     lane = lanes((8, 128))
@@ -124,20 +158,26 @@
     special = jnp.where(
         lane < 3, x0 - 2 + lane, jnp.where(lane < 6, x0 + COLS - 4 + lane, rp - 7 + lane)
     )
-    lam[...] = ramp(jnp.where(sub == 0, x0 + lane, special), sc[3], sc[4])
+    shares = ramp(jnp.where(sub == 0, x0 + lane, special), bounds[0], bounds[1])
+    lam[...] = jnp.where(sub < 2, shares, jnp.where(rp == total_x - 1, 1.0, 0.0))
 
     col = lane % 8
     slot = lane // 8
     place = off + col - 5
     here = (place >= 0) & (place < COLS) & (col >= 4) & (col < 7)
-    owner = (off >= 0) & (off < COLS)
     static = col < 4
     shift0 = 5 - off + 8 * 128 * 64
+    extras = []
     for y in range(ROWS):
         values = jnp.zeros((8, 128), jnp.float32)
-        for k in range(4):
-            values = jnp.where((slot == k) & (col == 7) & owner, prm[k, y], values)
-        for chunk in range(DEPTH // 8):
+        for k, v in enumerate((rows_in[y].astype(jnp.float32), weights_in[y], mean_in[y], fluct_in[y])):
+            values = jnp.where((slot == k) & (col == 7), v, values)
+        extras.append(values)
+    for chunk in range(pieces):
+        if chunk % (pieces // PIECES) == 0:
+            for copy in loads[chunk // (pieces // PIECES)]:
+                copy.wait()
+        for y in range(ROWS):
             rows = pl.ds(16 * chunk + y, 8, stride=2)
             g = [pops[i, rows, :] for i in range(19)]
             wall = solid[rows, :] == 1
@@ -161,7 +201,7 @@
                     if half * HALF + k < SIDE:
                         fixed = jnp.where(mine, pltpu.roll(v, 2 + 8 * k, 1), fixed)
                     moving = jnp.where(mine, pltpu.roll(v, (shift0 + 8 * k) % 128, 1), moving)
-                rest_of = values if half == 0 else jnp.zeros((8, 128), jnp.float32)
+                rest_of = extras[y] if half == 0 else jnp.zeros((8, 128), jnp.float32)
                 packed = jnp.where(static, fixed, jnp.where(here, moving, rest_of))
                 grid[pl.ds((y * 2 + half) * DEPTH + 8 * chunk, 8), :] = packed
     columns = grid[...].T[:TROWS]
@@ -203,83 +243,146 @@
     return first, second
 
 
-def cross_kernel(pairs, swap, sc, *refs):
+def apart(v):
+    low = lanes(v.shape) < SPAN
+    turned = pltpu.roll(v, SPAN, 1)
+    return jnp.where(low, v, turned), jnp.where(low, turned, v)
+
+
+def shifted(v, i):
+    _, cy, cz = lattice_vel[i]
+    if cz:
+        v = pltpu.roll(v, cz % 128, 1)
+    if cy:
+        v = pltpu.roll(v, cy % v.shape[0], 0)
+    return v
+
+
+def strip(value, row, total_y, edge):
+    held = {}
+
+    def middle(i):
+        if i not in held:
+            held[i] = value(1, i)
+        return held[i]
+
+    bottom, top = row == 0, row == total_y - 1
+    g = []
+    for i in range(19):
+        cx, cy, _ = lattice_vel[i]
+        v = shifted(middle(i) if cx == 0 else value(1 - cx, i), i)
+        if cx == -1 and edge is not None:
+            v = jnp.where(edge, middle(i), v)
+        if cy == 1:
+            v = jnp.where(bottom, middle(opposite[i]), v)
+        if cy == -1:
+            v = jnp.where(top, middle(mirror_pop[i]), v)
+        g.append(v)
+    return middle, g
+
+
+def lam_at(lam, c, rows):
+    return jnp.broadcast_to(lam[1:2, c : c + 1], (rows, 128))
+
+
+def at_outlet(lam, rows):
+    return jnp.broadcast_to(lam[2:3, 0:1], (rows, 128)) == 1.0
+
+
+def cross_kernel(slots, swap, total_y, lam, *refs):
+    pairs = len(slots)
     blocks = refs[: 2 * pairs]
-    full, right, left, plane = refs[2 * pairs :]
-    gy = sc[1]
+    full, right, left, plane, gains, deck = refs[2 * pairs :]
+    gy = lax.axis_index("gy")
+    if swap:
+        deck[...] = jnp.zeros_like(deck)
     for n in range(pairs):
         first, second = join(
             blocks[2 * n][pl.ds(0, TROWS), :], blocks[2 * n + 1][pl.ds(0, TROWS), :]
         )
         full[n, pl.ds(0, TROWS), :] = first
         full[n, pl.ds(TROWS, TROWS), :] = second
-        for c in range(2):
-            at = (n * 2 + c) * SIDE
-            right[pl.ds(at, SIDE), :] = full[n, pl.ds(c, SIDE, stride=8), :]
-            left[pl.ds(at, SIDE), :] = full[n, pl.ds(2 + c, SIDE, stride=8), :]
-        if n == 0 or swap:
-            base = 0
-            if swap:
-                base = pl.multiple_of((gy if n == 0 else 1 - gy) * PLANE, 8)
-            plane[pl.ds(base, 6), :] = full[n, pl.ds(4, 6, stride=8), :]
-            plane[pl.ds(base + 6, 24), :] = full[n, pl.ds(5, 24, stride=8), :]
-            plane[pl.ds(base + 30, 6), :] = full[n, pl.ds(5 * 8 + 6, 6, stride=8), :]
-            plane[pl.ds(base + 36, 4), :] = full[n, pl.ds(7, 4, stride=8), :]
+        at = n * TRAVEL
+        for (c, place, many), (d, spot, count) in zip(TO_EAST, TO_WEST):
+            right[pl.ds(at, many), :] = full[n, pl.ds(8 * place + 1 - c, many, stride=8), :]
+            left[pl.ds(at, count), :] = full[n, pl.ds(8 * spot + 2 + d, count, stride=8), :]
+            at += many
+        slot = 4 - 4 * gy if slots[n] is None else slots[n]
+        at = 0
+        for c, place, many in DECK:
+            top, bottom = apart(full[n, pl.ds(8 * place + c, many, stride=8), :])
+            deck[pl.ds(8 * at + slot, many, stride=8), :] = top
+            deck[pl.ds(8 * at + slot + 1, many, stride=8), :] = bottom
+            at += many
+
+    def deck_at(row):
+        return deck[pl.ds(8 * row, 8), :]
+
+    def read(c, f):
+        return deck_at(DECK_AT[4 + c] + PLACE[f])
+
+    keep = [1.0 - (1.0 - read(c, MASK)) * lam_at(lam, 6 + c, 8) for c in range(3)]
+    row = lax.broadcasted_iota(jnp.int32, (8, 128), 0) + 2 * gy - 2
+    _, g = strip(lambda c, i: read(c, i) * keep[c], row, total_y, at_outlet(lam, 8))
+    fields = list(sums(g)) + [read(c, MASK) for c in range(3)] + [read(1, 20 + k) for k in range(4)]
+    params = [deck_at(36 + k) for k in range(4)]
+    if not swap:
+        for n, v in enumerate(fields + params):
+            plane[pl.ds(8 * n, 8), :] = v
+        return
+
+    def settle(v):
+        return jnp.where(gy == 0, pltpu.roll(v, 6, 0), v)
+
+    for n, v in enumerate(params):
+        gains[pl.ds(8 * n, 8), :] = settle(v)
+    fields = [settle(v) for v in fields] + [jnp.zeros((8, 128), jnp.float32)]
+    low, upper = lanes((8, 128)) < SPAN, lax.broadcasted_iota(jnp.int32, (8, 128), 0) < 4
+    for n in range(3):
+        a, b, c, d = fields[4 * n : 4 * n + 4]
+        lower = pltpu.roll(jnp.where(low, c, d), 4, 0)
+        plane[pl.ds(8 * n, 8), :] = jnp.where(upper, jnp.where(low, a, b), lower)
+    tail = right.shape[0] - 24
+    right[pl.ds(tail, 24), :] = plane[...]
+    left[pl.ds(tail, 24), :] = plane[...]
+
+
+def strips_kernel(slots, swap, total_y, total_x, lam, full, west, east, plane, gains, out, side, shelf):
+    gx, gy = lax.axis_index("gx"), lax.axis_index("gy")
+    last_x = total_x // COLS - 1
+    deep = max(8, total_y)
     if swap:
-        tail = pairs * 2 * SIDE
-        right[pl.ds(tail, 2 * PLANE), :] = plane[...]
-        left[pl.ds(tail, 2 * PLANE), :] = plane[...]
-
-
-def strips_kernel(pairs, slots, total_y, total_x, sc, lam, full, west, east, plane_in, out, side, deck, shelf):
-    gx, gy, rp = sc[0], sc[1], sc[2]
-    last_x = sc[5]
-    deep = deck.shape[0] // PLANE
-    side[...] = jnp.zeros_like(side)
-    deck[...] = jnp.zeros_like(deck)
-    shelf[...] = jnp.zeros_like(shelf)
-
-    def apart(v):
-        low = lanes(v.shape) < SPAN
-        turned = pltpu.roll(v, SPAN, 1)
-        return jnp.where(low, v, turned), jnp.where(low, turned, v)
-
-    def lay(strip, c, first, v):
+        side[...] = jnp.zeros_like(side)
+        shelf[...] = jnp.zeros_like(shelf)
+
+    def lay(s, c, first, place, v):
         top, bottom = apart(v)
-        side[strip, c, pl.ds(first, SIDE, stride=8), :] = top
-        side[strip, c, pl.ds(first + 1, SIDE, stride=8), :] = bottom
-
-    def spread(n, first):
-        sides = (n * 2) * SIDE
-        lay(0, 0, first, west[pl.ds(sides, SIDE), :])
-        lay(0, 1, first, west[pl.ds(sides + SIDE, SIDE), :])
-        lay(0, 2, first, full[n, pl.ds(2, SIDE, stride=8), :])
-        lay(1, 0, first, full[n, pl.ds(1, SIDE, stride=8), :])
-        lay(1, 1, first, east[pl.ds(sides, SIDE), :])
-        lay(1, 2, first, east[pl.ds(sides + SIDE, SIDE), :])
-
-    for n in range(pairs):
-        if slots[n] is None:
-
-            @pl.when(gy == 0)
-            def _():
-                spread(n, 4)
-
-            @pl.when(gy != 0)
-            def _():
-                spread(n, 0)
-
-        else:
-            spread(n, slots[n])
-    for n in range(total_y // 2):
-        top, bottom = apart(plane_in[pl.ds(n * PLANE, PLANE), :])
-        deck[pl.ds(2 * n, PLANE, stride=deep), :] = top
-        deck[pl.ds(2 * n + 1, PLANE, stride=deep), :] = bottom
-
-    def deck_at(row):
-        return deck[pl.ds(row * deep, deep), :]
-
-    which, ratio, mean_gain, fluct_gain = (deck_at(36 + k) for k in range(4))
+        many = v.shape[0]
+        side[s, c, pl.ds(8 * place + first, many, stride=8), :] = top
+        side[s, c, pl.ds(8 * place + first + 1, many, stride=8), :] = bottom
+
+    for n, slot in enumerate(slots):
+        slot = 4 - 4 * gy if slot is None else slot
+        lay(0, 2, slot, 0, full[n, pl.ds(2, SIDE, stride=8), :])
+        lay(1, 0, slot, 0, full[n, pl.ds(1, SIDE, stride=8), :])
+        at = n * TRAVEL
+        for (c, place, many), (d, spot, count) in zip(TO_EAST, TO_WEST):
+            lay(0, 1 - c, slot, place, west[pl.ds(at, many), :])
+            lay(1, 1 + d, slot, spot, east[pl.ds(at, count), :])
+            at += many
+
+    if swap:
+        fields = []
+        low = lanes((8, 128)) < SPAN
+        for n in range(3):
+            v = plane[pl.ds(8 * n, 8), :]
+            for w in (v, pltpu.roll(v, 4, 0)):
+                turned = pltpu.roll(w, SPAN, 1)
+                fields += [jnp.where(low, w, turned), jnp.where(low, turned, w)]
+        which, ratio, mean_gain, fluct_gain = (gains[pl.ds(8 * k, 8), :] for k in range(4))
+    else:
+        fields = [plane[pl.ds(deep * n, deep), :] for n in range(SUMS + 4)]
+        which, ratio, mean_gain, fluct_gain = fields[SUMS:]
 
     def target(fields):
         def blend(v):
@@ -306,54 +409,13 @@
             got.append(shelf[k, pl.ds(6 + 2 * gy, 8), :])
         return got
 
-    def shifted(v, i):
-        _, cy, cz = lattice_vel[i]
-        if cz:
-            v = pltpu.roll(v, cz % 128, 1)
-        if cy:
-            v = pltpu.roll(v, cy % v.shape[0], 0)
-        return v
-
-    def forced(value, gate, goal):
-        return value + gate * (goal - value)
-
-    def strip(read, gates, teq, row, edge):
-        gate = [(1.0 - read(c, MASK)) * gates[c] for c in range(3)]
-        middle = [forced(read(1, i), gate[1], teq[i]) for i in range(19)]
-        bottom, top = row == 0, row == total_y - 1
-        g = []
-        for i in range(19):
-            cx, cy, _ = lattice_vel[i]
-            if cx == 0:
-                v = shifted(middle[i], i)
-            else:
-                c = 1 - cx
-                v = shifted(forced(read(c, i), gate[c], teq[i]), i)
-                if cx == -1 and edge is not None:
-                    v = jnp.where(edge, middle[i], v)
-            if cy == 1:
-                v = jnp.where(bottom, middle[opposite[i]], v)
-            if cy == -1:
-                v = jnp.where(top, middle[mirror_pop[i]], v)
-            g.append(v)
-        return middle, g, gate
-
-    def lam_at(c, rows):
-        return jnp.broadcast_to(lam[1:2, c : c + 1], (rows, 128))
-
-    target0 = target([deck_at(6 + 20 + k) for k in range(4)])
+    target0 = target(fields[7:11])
     teq0 = equilibria(*target0)
-    start = {0: (0, 0), 1: (6, 0), 2: (30, 5)}
-
-    def read_plane(c, f):
-        base, less = start[c]
-        return deck_at(base + PLACE[f] - less)
-
+    gates = [(1.0 - fields[4 + c]) * lam_at(lam, 6 + c, deep) for c in range(3)]
     row = lax.broadcasted_iota(jnp.int32, (deep, 128), 0)
-    _, g1, _ = strip(
-        read_plane, [lam_at(6 + c, deep) for c in range(3)], teq0, row, rp == total_x - 1
-    )
-    target1 = target(list(moments(g1)))
+    _, g = strip(lambda c, i: gates[c] * teq0[i], row, total_y, at_outlet(lam, deep))
+    total = [a + b for a, b in zip(sums(g), fields[:4])]
+    target1 = target(list(velocity(*total)))
     near0, near1 = local(target0), local(target1)
     goal0, goal1 = equilibria(*near0), equilibria(*near1)
 
@@ -361,23 +423,26 @@
     first, second = [], []
     for s, wanted in ((0, EAST), (1, WEST)):
 
-        def read_side(c, f):
+        def read(c, f):
             return side[s, c, pl.ds(PLACE[f] * 8, 8), :]
 
-        middle, g1, gate = strip(
-            read_side, [lam_at(3 * s + c, 8) for c in range(3)], goal0, row, None
-        )
-        density, vx, vy, vz = moments(g1)
-        eq = equilibria(density, vx, vy, vz, wanted)
-        wall = read_side(1, MASK) == 1.0
+        gate = [(1.0 - read(c, MASK)) * lam_at(lam, 3 * s + c, 8) for c in range(3)]
+
+        def value(c, i):
+            v = read(c, i)
+            return v + gate[c] * (goal0[i] - v)
+
+        middle, g = strip(value, row, total_y, None)
+        eq = equilibria(*moments(g), wanted)
+        wall = read(1, MASK) == 1.0
         for i in wanted:
-            loose = g1[i] - relax_rate * (g1[i] - eq[i])
-            later = forced(jnp.where(wall, g1[opposite[i]], loose), gate[1], goal1[i])
-            a, b = shifted(middle[i], i), shifted(later, i)
+            loose = g[i] - relax_rate * (g[i] - eq[i])
+            v = jnp.where(wall, g[opposite[i]], loose)
+            a, b = shifted(middle(i), i), shifted(v + gate[1] * (goal1[i] - v), i)
             if s == 0:
                 a, b = jnp.where(gx == 0, goal0[i], a), jnp.where(gx == 0, goal1[i], b)
             else:
-                a = jnp.where(gx == last_x, forced(read_side(0, i), gate[0], goal0[i]), a)
+                a = jnp.where(gx == last_x, value(0, i), a)
             first.append(a)
             second.append(b)
     blank = [jnp.zeros((16, 128), jnp.float32)]
@@ -386,13 +451,13 @@
         out[pl.ds(48 * n, 48), :] = turned[:48]
 
 
-def steps_kernel(ways, total_y, sc, lam, relaxed, zmsg, cols, *rest):
+def steps_kernel(ways, total_y, total_x, lam, relaxed, zmsg, cols, *rest):
     count = len(ways)
     bulk, small, small_other = rest[:count], rest[count : 2 * count], rest[2 * count : 3 * count]
-    out, early, late = rest[3 * count :]
-    gx, gy = sc[0], sc[1]
-    at_end = gx == sc[5]
-    bottom, top = gy == 0, gy == sc[6]
+    result, early, late, out, sem = rest[3 * count :]
+    gx, gy = lax.axis_index("gx"), lax.axis_index("gy")
+    at_end = gx == total_x // COLS - 1
+    bottom, top = gy == 0, gy == total_y // ROWS - 1
     lane = lanes((8, 128))
     at_first, at_last = lane == 0, lane == COLS - 1
     zone = jnp.broadcast_to(lam[0:1, :], (8, 128))
@@ -488,22 +553,32 @@
 
     for slot in (2, 3):
         collide(slot, range(19), True)
-    for y in range(ROWS):
-        for chunk in range(DEPTH // 8):
+    stores = []
+    for chunk in range(DEPTH // 8):
+        for y in range(ROWS):
             g = pull(late, 2 + y, 1, 1, 2 + 8 * chunk, 1, True)
             for i in range(19):
                 out[i, pl.ds(16 * chunk + y, 8, stride=2), :] = g[i]
-
-
-def call(kernel, outs, scratch, limit, *args, scalars=1):
-    smem = pl.BlockSpec(memory_space=pltpu.SMEM)
-    vmem = pl.BlockSpec(memory_space=pltpu.VMEM)
+        rows = pl.ds(16 * chunk, 16)
+        stores.append(pltpu.make_async_copy(out.at[:, rows, :], result.at[:, rows, :], sem.at[chunk]))
+        stores[-1].start()
+    for copy in stores:
+        copy.wait()
+
+
+def call(kernel, outs, scratch, limit, *args, held=False, leave=False):
+    near = pl.BlockSpec(memory_space=pltpu.VMEM)
+    far = pl.BlockSpec(memory_space=pltpu.HBM)
+    inputs = [near] * len(args)
+    if held:
+        inputs = [pl.BlockSpec(memory_space=pltpu.SMEM)] + [far] * (len(args) - 1)
+        args = [args[0]] + [pltpu.with_memory_space_constraint(v, pltpu.HBM) for v in args[1:]]
     return pl.pallas_call(
         kernel,
         out_shape=[jax.ShapeDtypeStruct(s, jnp.float32) for s in outs],
-        in_specs=[smem] * scalars + [vmem] * (len(args) - scalars),
-        out_specs=[vmem] * len(outs),
-        scratch_shapes=[pltpu.VMEM(s, jnp.float32) for s in scratch],
+        in_specs=inputs,
+        out_specs=[far if leave else near] * len(outs),
+        scratch_shapes=[pltpu.VMEM(s, jnp.float32) if isinstance(s, tuple) else s for s in scratch],
         compiler_params=pltpu.CompilerParams(vmem_limit_bytes=limit << 20),
     )(*args)
 
@@ -515,28 +590,37 @@
 def body(populations, solid_mask, recycle_plane, fringe_bounds, interp_rows, interp_weights, mean_scale, fluct_scale):
     size_x, size_y = lax.axis_size("gx"), lax.axis_size("gy")
     total_x, total_y = COLS * size_x, ROWS * size_y
-    gx, gy = lax.axis_index("gx"), lax.axis_index("gy")
     swap = size_y == 2
     ways = (None,) if swap else (True, False)
-    pairs = 1 + len(ways)
-    sc = jnp.stack([gx, gy, recycle_plane[0], fringe_bounds[0], fringe_bounds[1], jnp.int32(size_x - 1), jnp.int32(size_y - 1)])
-    prm = jnp.stack([interp_rows.astype(jnp.float32), interp_weights, mean_scale, fluct_scale])
+    slots = (2,) + ((None,) if swap else (0, 4))
+    pairs = len(slots)
     pops = populations.reshape(19, DEPTH * ROWS, COLS)
     solid = solid_mask.reshape(DEPTH * ROWS, COLS)
 
-    small_rows = TROWS + 88
-    bulk_rows = 592
-    z_rows = TROWS + 40 * EDGE
     made = call(
-        functools.partial(relax_kernel, ways),
-        [(20, ROWS, DEPTH, COLS), (8, 128), (z_rows, 128)] + [(small_rows, 128)] * len(ways) + [(bulk_rows, 128)] * len(ways),
-        [(128, 128)],
+        functools.partial(relax_kernel, ways, total_x),
+        [(20, ROWS, DEPTH, COLS), (8, 128), (TROWS + 40 * EDGE, 128)] + [(TROWS + 88, 128)] * len(ways) + [(592, 128)] * len(ways),
+        [
+            (128, 128),
+            pops.shape,
+            pltpu.VMEM(solid.shape, jnp.int32),
+            pltpu.SMEM((2,), jnp.int32),
+            pltpu.SMEM((ROWS,), jnp.int32),
+            pltpu.SMEM((ROWS,), jnp.float32),
+            pltpu.SMEM((ROWS,), jnp.float32),
+            pltpu.SMEM((ROWS,), jnp.float32),
+            pltpu.SemaphoreType.DMA((2 * PIECES + 5,)),
+        ],
         8,
-        sc,
-        prm,
+        recycle_plane,
         pops,
         solid,
-        scalars=2,
+        fringe_bounds,
+        interp_rows,
+        interp_weights,
+        mean_scale,
+        fluct_scale,
+        held=True,
     )
     relaxed, lam, z_out = made[:3]
     small_out, bulk_out = made[3 : 3 + len(ways)], made[3 + len(ways) :]
@@ -555,48 +639,48 @@
     blocks = [z_out, z_in]
     for a, b in zip(small, small_other):
         blocks += [a, b]
-    edge_rows = pairs * 2 * SIDE + (2 * PLANE if swap else 0)
-    full, right, left, plane = call(
-        functools.partial(cross_kernel, pairs, swap),
-        [(pairs, 2 * TROWS, 128), (edge_rows, 128), (edge_rows, 128), (PLANE * (2 if swap else 1), 128)],
-        [],
+    edge_rows = 72
+    full, right, left, plane, gains = call(
+        functools.partial(cross_kernel, slots, swap, total_y),
+        [(pairs, 2 * TROWS, 128), (edge_rows, 128), (edge_rows, 128), (24 if swap else 8 * (SUMS + 4), 128), (32, 128)],
+        [(8 * DECK_ROWS, 128)],
         4,
-        sc,
+        lam,
         *blocks,
     )
     west = lax.ppermute(right, "gx", ring(size_x, 1))
     east = lax.ppermute(left, "gx", ring(size_x, -1))
     if swap and size_x == 4:
-        tail = pairs * 2 * SIDE
         far = lax.ppermute(plane, "gx", ring(4, 2))
-        plane = plane + far + west[tail:] + east[tail:]
+        plane = plane + far + west[edge_rows - 24 :] + east[edge_rows - 24 :]
     elif swap:
         plane = lax.psum(plane, "gx")
     else:
-        spot = jnp.zeros((size_y, PLANE, 128), jnp.float32)
-        spot = lax.dynamic_update_slice(spot, plane[None], (gy, 0, 0))
-        plane = lax.psum(spot, ("gx", "gy")).reshape(size_y * PLANE, 128)
-
-    deep = max(8, total_y)
-    slots = (2,) + ((None,) if swap else (0, 4))
+        own = plane.reshape(SUMS + 4, 8, 128)[:, 2:4]
+        first = (lax.axis_index("gx") == 0) | (jnp.arange(SUMS + 4) < SUMS)
+        own = jnp.where(first[:, None, None], own, 0.0)
+        whole = lax.dynamic_update_slice(
+            jnp.zeros((SUMS + 4, total_y, 128), jnp.float32), own, (0, 2 * lax.axis_index("gy"), 0)
+        )
+        plane = lax.psum(whole, ("gx", "gy")).reshape((SUMS + 4) * total_y, 128)
+
     (cols,) = call(
-        functools.partial(strips_kernel, pairs, slots, total_y, total_x),
+        functools.partial(strips_kernel, slots, swap, total_y, total_x),
         [(96, 128)],
-        [(2, 3, SIDE * 8, 128), (PLANE * deep, 128), (4, 16 + deep, 128)],
+        [(2, 3, SIDE * 8, 128), (4, 16 + max(8, total_y), 128)],
         8,
-        sc,
         lam,
         full,
         west,
         east,
         plane,
+        gains,
     )
     (out,) = call(
-        functools.partial(steps_kernel, ways, total_y),
+        functools.partial(steps_kernel, ways, total_y, total_x),
         [(19, DEPTH * ROWS, COLS)],
-        [(20, 6, 48, 128), (19, 4, 48, 128)],
+        [(20, 6, 48, 128), (19, 4, 48, 128), (19, DEPTH * ROWS, COLS), pltpu.SemaphoreType.DMA((DEPTH // 8,))],
         12,
-        sc,
         lam,
         relaxed,
         z_in,
@@ -604,6 +688,7 @@
         *bulk,
         *small,
         *small_other,
+        leave=True,
     )
     return out.reshape(populations.shape)
 

time: 29 us -> 21.9 us (0.76)
  waiting for transfers between devices: 9.18 us -> 6.52 us
  local copies, waits for them, and re-layouts: 1.81 us -> 0 us
  other arithmetic: 1.37 us -> 0.01 us
  Pallas kernels: 6.16 us -> 5 us
    another operation x2 -> x0, other arithmetic: 1.36 us -> none  [body(): jnp.stack([interp_rows.astype(jnp.float32), interp_weights, mean_scale, f...]
    ppermute x1, waiting for transfers between devices: 1.29 us -> 0.01 us  [body(): small_other = [lax.ppermute(v, 'gz', ring(2, 1)) for v in small]]
    pallas_call x4, Pallas kernels: 6.16 us -> 5 us  [call(): pl.pallas_call(kernel, out_shape=[jax.ShapeDtypeStruct(s, jnp.float32) fo...]
    unnamed x4 -> x0, local copies, waits for them, and re-layouts: 1.08 us -> none
    ppermute x2, waiting for transfers between devices: 3.77 us -> 2.71 us  [across(): return lax.ppermute(v, 'gy', ring(2, 1))]
    another operation x1 -> x0, local copies, waits for them, and re-layouts: 0.73 us -> none  [body(): jnp.stack([gx, gy, recycle_plane[0], fringe_bounds[0], fringe_bounds[1],...]
    ppermute x1, starting transfers between devices: 1.99 us -> 1.63 us  [body(): west = lax.ppermute(right, 'gx', ring(size_x, 1))]
    ppermute x1, waiting for transfers between devices: 4.11 us -> 3.8 us  [body(): far = lax.ppermute(plane, 'gx', ring(4, 2))]
  transfers between devices with their start and end apart: 7 -> 7, of which waited for: 4 -> 2; matrix products, arithmetic and copies ran while one was open for 0% -> 0% of each run, Pallas kernels for 5% -> 4%
where the time goes in v2:
time: 21.9 us; the launch traced here: 21.8 us
  starting transfers between devices  9.56 us (44%)
  waiting for transfers between devices  6.52 us (30%)
  Pallas kernels  5 us (23%)
  between operations  0.68 us (3%)
    pallas_call x4, Pallas kernels, call(): pl.pallas_call(kernel, out_shape=[jax.ShapeDtypeStruct(s, jnp.float32) fo...  5 us
    ppermute x2, starting transfers between devices, across(): return lax.ppermute(v, 'gy', ring(2, 1))  4.88 us
    ppermute x1, waiting for transfers between devices, body(): far = lax.ppermute(plane, 'gx', ring(4, 2))  3.8 us
    ppermute x2, waiting for transfers between devices, across(): return lax.ppermute(v, 'gy', ring(2, 1))  2.71 us
    ppermute x1, starting transfers between devices, body(): east = lax.ppermute(left, 'gx', ring(size_x, -1))  2.25 us
    ppermute x1, starting transfers between devices, body(): west = lax.ppermute(right, 'gx', ring(size_x, 1))  1.63 us
    ppermute x1, starting transfers between devices, body(): far = lax.ppermute(plane, 'gx', ring(4, 2))  0.79 us
  transfers between devices with their start and end apart: 7, of which 2 were waited for; matrix products, arithmetic and copies ran while one was open for 0% of the time, Pallas kernels for 4%

profile of v2, /device:TPU:0, one launch (start us, length us, event | category | flops | bytes accessed | tf_op | source)
XLA Modules:
  0.0 21.8 jit_solution(7613608216093664353)
XLA Ops:
  0.7 1.8 %shard_map.82 = (f32[20,2,32,128]{3,2,1,0:T(8,128)S(1)}, f32[8,128]{1,0:T(8,128)S(1)}, f32[256,128]{1,0:T(8,128)S(1)}, f32[184,128]{1,0:T(8,128)S(1)}, f32[592,128]{1,0:T(8,128)S(1)}) custom-call(s32[1]{0:T(128)S(6)} %copy.9.refs_0_, f32[19,64,128]{2,1,0:T(8,128)} %bitcast.3, s32[64,128]{1,0:T(8,128)} %bitcast.4, s32[2]{0:T(128)} %refs_3_.1, s32[2]{0:T(128)} %refs_4_.1, ...), custom_call_target="tpu_custom_call" | custom-call | tf_op jit(solution)/shard_map/pallas_call | solution.py:576
  2.4 3.0 %collective-permute-start.1 = (f32[184,128]{1,0:T(8,128)S(1)}, f32[184,128]{1,0:T(8,128)S(1)}, u32[]{:S(2)}, u32[]{:S(2)}) collective-permute-start(f32[184,128]{1,0:T(8,128)S(1)} %get-tuple-element.18), channel_id=1, source_target_pairs={{0,2},{2,0},{1,3},{3,1},{4,6},{6,4},{5,7},{7,5},{8,10},{10,8},{9,1... | collective-permute-start | bytes 282632 | tf_op jit(solution)/shard_map/ppermute | solution.py:630
  5.4 0.0 collective-permute-start
  5.4 2.7 %collective-permute-done.1.refs_2_.rest_1_ = f32[184,128]{1,0:T(8,128)S(1)} collective-permute-done((f32[184,128]{1,0:T(8,128)S(1)}, f32[184,128]{1,0:T(8,128)S(1)}, u32[]{:S(2)}, u32[]{:S(2)}) %collective-permute-start.1) | collective-permute-done | bytes 94240 | tf_op jit(solution)/shard_map/ppermute | solution.py:630
  8.1 0.0 collective-permute-start.2
  8.1 1.9 %collective-permute-start.6 = (f32[592,128]{1,0:T(8,128)S(1)}, f32[592,128]{1,0:T(8,128)S(1)}, u32[]{:S(2)}, u32[]{:S(2)}) collective-permute-start(f32[592,128]{1,0:T(8,128)S(1)} %get-tuple-element.24), channel_id=1, source_target_pairs={{0,2},{2,0},{1,3},{3,1},{4,6},{6,4},{5,7},{7,5},{8,10},{10,8},{9,1... | collective-permute-start | bytes 909320 | tf_op jit(solution)/shard_map/ppermute | solution.py:630
  10.0 0.0 collective-permute-done.refs_1_.zmsg
  10.0 0.0 collective-permute-done.2.refs_3_.rest_2_
  10.0 0.3 %shard_map.83 = (f32[2,192,128]{2,1,0:T(8,128)S(1)}, f32[72,128]{1,0:T(8,128)S(1)}, f32[72,128]{1,0:T(8,128)S(1)}, f32[24,128]{1,0:T(8,128)S(1)}, f32[32,128]{1,0:T(8,128)S(1)}) custom-call(f32[8,128]{1,0:T(8,128)S(1)} %get-tuple-element.15.lam, f32[256,128]{1,0:T(8,128)S(1)} %get-tuple-element.17.refs_0_, f32[256,128]{1,0:T(8,128)S(1)} %collective-permute-done.refs_1_.zmsg, ...), custom_call_target="tpu_custom_call" | custom-call | tf_op jit(solution)/shard_map/pallas_call | solution.py:576
  10.3 1.6 %collective-permute-start.3 = (f32[72,128]{1,0:T(8,128)S(1)}, f32[72,128]{1,0:T(8,128)S(1)}, u32[]{:S(2)}, u32[]{:S(2)}) collective-permute-start(f32[72,128]{1,0:T(8,128)S(1)} %get-tuple-element.20), channel_id=1, source_target_pairs={{0,4},{4,8},{8,12},{12,0},{1,5},{5,9},{9,13},{13,1},{2,6},{6,10},{... | collective-permute-start | bytes 110600 | tf_op jit(solution)/shard_map/ppermute | solution.py:651
  11.9 2.2 %collective-permute-start.4 = (f32[72,128]{1,0:T(8,128)S(1)}, f32[72,128]{1,0:T(8,128)S(1)}, u32[]{:S(2)}, u32[]{:S(2)}) collective-permute-start(f32[72,128]{1,0:T(8,128)S(1)} %get-tuple-element.21), channel_id=1, source_target_pairs={{0,12},{4,0},{8,4},{12,8},{1,13},{5,1},{9,5},{13,9},{2,14},{6,2},{... | collective-permute-start | bytes 110600 | tf_op jit(solution)/shard_map/ppermute | solution.py:652
  14.2 0.8 %collective-permute-start.5 = (f32[24,128]{1,0:T(8,128)S(1)}, f32[24,128]{1,0:T(8,128)S(1)}, u32[]{:S(2)}, u32[]{:S(2)}) collective-permute-start(f32[24,128]{1,0:T(8,128)S(1)} %get-tuple-element.22), channel_id=1, source_target_pairs={{0,8},{4,12},{8,0},{12,4},{1,9},{5,13},{9,1},{13,5},{2,10},{6,14},... | collective-permute-start | bytes 36872 | tf_op jit(solution)/shard_map/ppermute | solution.py:654
  15.0 3.8 %collective-permute-done.5 = f32[24,128]{1,0:T(8,128)S(1)} collective-permute-done((f32[24,128]{1,0:T(8,128)S(1)}, f32[24,128]{1,0:T(8,128)S(1)}, u32[]{:S(2)}, u32[]{:S(2)}) %collective-permute-start.5) | collective-permute-done | bytes 12320 | tf_op jit(solution)/shard_map/ppermute | solution.py:654
  18.8 0.0 collective-permute-done.3.west
  18.8 0.0 collective-permute-done.4.east
  18.8 0.6 %shard_map.84.cols = f32[96,128]{1,0:T(8,128)S(1)} custom-call(f32[8,128]{1,0:T(8,128)S(1)} %get-tuple-element.15.lam, f32[2,192,128]{2,1,0:T(8,128)S(1)} %get-tuple-element.19.full, f32[72,128]{1,0:T(8,128)S(1)} %collective-permute-done.3.west, f32[72,128]{1,0:T(8,128)S(1)} %collective-permute-done.4.east, f32[24,128]{1,0:T(8,128)S(1)} %slice_add_fusion.plane, ...), custom_call_target="tpu_custom_call" | custom-call | tf_op jit(solution)/shard_map/pallas_call | solution.py:576
  19.4 0.0 collective-permute-done.6.rest_0_
  19.5 2.3 %shard_map.85 = f32[19,64,128]{2,1,0:T(8,128)} custom-call(f32[8,128]{1,0:T(8,128)S(1)} %get-tuple-element.15.lam, f32[20,2,32,128]{3,2,1,0:T(8,128)S(1)} %get-tuple-element.16.relaxed, f32[256,128]{1,0:T(8,128)S(1)} %collective-permute-done.refs_1_.zmsg, f32[96,128]{1,0:T(8,128)S(1)} %shard_map.84.cols, f32[592,128]{1,0:T(8,128)S(1)} %collective-permute-done.6.rest_0_, ...), custom_call_target="tpu_custom_call" | custom-call | tf_op jit(solution)/shard_map/pallas_call | solution.py:576
  (1 shorter events, 0.0 us)
Async XLA Ops:
  2.4 5.7 %collective-permute-start.1 = (f32[184,128]{1,0:T(8,128)S(1)}, f32[184,128]{1,0:T(8,128)S(1)}, u32[]{:S(2)}, u32[]{:S(2)}) collective-permute-start(f32[184,128]{1,0:T(8,128)S(1)} %get-tuple-element.18), channel_id=1, source_target_pairs={{0,2},{2,0},{1,3},{3,1},{4,6},{6,4},{5,7},{7,5},{8,10},{10,8},{9,1... | collective-permute-start | bytes 282632 | tf_op jit(solution)/shard_map/ppermute | solution.py:630
  5.4 4.6 %collective-permute-start = (f32[256,128]{1,0:T(8,128)S(1)}, f32[256,128]{1,0:T(8,128)S(1)}, u32[]{:S(2)}, u32[]{:S(2)}) collective-permute-start(f32[256,128]{1,0:T(8,128)S(1)} %get-tuple-element.17.refs_0_), channel_id=1, source_target_pairs={{0,1},{1,0},{2,3},{3,2},{4,5},{5,4},{6,7},{7,6},{8,9},{9,8},{10,11... | collective-permute-start | bytes 393224 | tf_op jit(solution)/shard_map/ppermute | solution.py:636
  8.1 1.9 %collective-permute-start.2 = (f32[184,128]{1,0:T(8,128)S(1)}, f32[184,128]{1,0:T(8,128)S(1)}, u32[]{:S(2)}, u32[]{:S(2)}) collective-permute-start(f32[184,128]{1,0:T(8,128)S(1)} %collective-permute-done.1.refs_2_.rest_1_), channel_id=1, source_target_pairs={{0,1},{1,0},{2,3},{3,2},{4,5},{5,4},{6,7},{7,6},{8,9},{9,8},{10,11... | collective-permute-start | bytes 282632 | tf_op jit(solution)/shard_map/ppermute | solution.py:637
  8.1 11.3 %collective-permute-start.6 = (f32[592,128]{1,0:T(8,128)S(1)}, f32[592,128]{1,0:T(8,128)S(1)}, u32[]{:S(2)}, u32[]{:S(2)}) collective-permute-start(f32[592,128]{1,0:T(8,128)S(1)} %get-tuple-element.24), channel_id=1, source_target_pairs={{0,2},{2,0},{1,3},{3,1},{4,6},{6,4},{5,7},{7,5},{8,10},{10,8},{9,1... | collective-permute-start | bytes 909320 | tf_op jit(solution)/shard_map/ppermute | solution.py:630
  10.3 8.5 %collective-permute-start.3 = (f32[72,128]{1,0:T(8,128)S(1)}, f32[72,128]{1,0:T(8,128)S(1)}, u32[]{:S(2)}, u32[]{:S(2)}) collective-permute-start(f32[72,128]{1,0:T(8,128)S(1)} %get-tuple-element.20), channel_id=1, source_target_pairs={{0,4},{4,8},{8,12},{12,0},{1,5},{5,9},{9,13},{13,1},{2,6},{6,10},{... | collective-permute-start | bytes 110600 | tf_op jit(solution)/shard_map/ppermute | solution.py:651
  11.9 6.8 %collective-permute-start.4 = (f32[72,128]{1,0:T(8,128)S(1)}, f32[72,128]{1,0:T(8,128)S(1)}, u32[]{:S(2)}, u32[]{:S(2)}) collective-permute-start(f32[72,128]{1,0:T(8,128)S(1)} %get-tuple-element.21), channel_id=1, source_target_pairs={{0,12},{4,0},{8,4},{12,8},{1,13},{5,1},{9,5},{13,9},{2,14},{6,2},{... | collective-permute-start | bytes 110600 | tf_op jit(solution)/shard_map/ppermute | solution.py:652
  14.2 4.6 %collective-permute-start.5 = (f32[24,128]{1,0:T(8,128)S(1)}, f32[24,128]{1,0:T(8,128)S(1)}, u32[]{:S(2)}, u32[]{:S(2)}) collective-permute-start(f32[24,128]{1,0:T(8,128)S(1)} %get-tuple-element.22), channel_id=1, source_target_pairs={{0,8},{4,12},{8,0},{12,4},{1,9},{5,13},{9,1},{13,5},{2,10},{6,14},... | collective-permute-start | bytes 36872 | tf_op jit(solution)/shard_map/ppermute | solution.py:654

commit v3 on v2

--- a/solution.py
+++ b/solution.py
@@ -58,7 +58,9 @@
 DECK_ROWS = 40
 SUMS = 11
 EDGE = 4
-INNER = DEPTH - EDGE
+BLOCK_AT = 88
+SUMS_AT = BLOCK_AT + 12 * DEPTH
+BULK = 656
 PIECES = 2
 
 
@@ -128,14 +130,12 @@
     return jnp.where(inside, fringe_peak * jnp.sin(angle) ** 2, 0.0)
 
 
-def relax_kernel(ways, total_x, *refs):
+def relax_kernel(total_x, *refs):
     recycle, pops_in, solid_in = refs[:3]
     small_in = refs[3:8]
-    relaxed, lam, zmsg = refs[8:11]
-    rest = refs[11:]
-    ysm, ymn = rest[: len(ways)], rest[len(ways) : 2 * len(ways)]
-    grid, pops, solid = rest[2 * len(ways) : 2 * len(ways) + 3]
-    small, sem = rest[2 * len(ways) + 3 : -1], rest[-1]
+    relaxed, lam, columns, zmsg = refs[8:12]
+    grid, pops, solid = refs[12:15]
+    small, sem = refs[15:-1], refs[-1]
     loads = [
         [pltpu.make_async_copy(a.at[..., rows, :], b.at[..., rows, :], sem.at[2 * n + m]) for m, (a, b) in enumerate(((pops_in, pops), (solid_in, solid)))]
         for n, rows in enumerate(pl.ds(n * 2 * DEPTH // PIECES, 2 * DEPTH // PIECES) for n in range(PIECES))
@@ -150,7 +150,7 @@
     for copy in scalars:
         copy.wait()
     bounds, rows_in, weights_in, mean_in, fluct_in = small
-    gx, gy, rp = lax.axis_index("gx"), lax.axis_index("gy"), recycle[0]
+    gx, rp = lax.axis_index("gx"), recycle[0]
     x0 = gx * COLS
     off = rp - x0
     lane = lanes((8, 128))
@@ -204,36 +204,74 @@
                 rest_of = extras[y] if half == 0 else jnp.zeros((8, 128), jnp.float32)
                 packed = jnp.where(static, fixed, jnp.where(here, moving, rest_of))
                 grid[pl.ds((y * 2 + half) * DEPTH + 8 * chunk, 8), :] = packed
-    columns = grid[...].T[:TROWS]
-    zmsg[pl.ds(0, TROWS), :] = columns
+    columns[...] = grid[...].T[:TROWS]
+    zmsg[pl.ds(0, TROWS), :] = columns[...]
     for f in range(20):
         for y in range(ROWS):
             at = TROWS + (f * 2 + y) * EDGE
             zmsg[pl.ds(at, 2), :] = relaxed[f, y, pl.ds(0, 2), :]
             zmsg[pl.ds(at + 2, 2), :] = relaxed[f, y, pl.ds(DEPTH - 2, 2), :]
 
-    def pack(way, small, bulk):
+
+def pack_kernel(ways, relaxed, lam, z_in, *rest):
+    bulk, inside = rest[:-1], rest[-1]
+    lane = lanes((8, 128))
+    zone = jnp.broadcast_to(lam[0:1, :], (8, 128))
+    zero = jnp.zeros((8, 128), jnp.float32)
+
+    def pack(way, to):
+        inner = 0
         for n, (f, near) in enumerate(up_down(way)):
             y = 1 if near == way else 0
-            at = TROWS + n * EDGE
-            small[pl.ds(at, 2), :] = relaxed[f, y, pl.ds(0, 2), :]
-            small[pl.ds(at + 2, 2), :] = relaxed[f, y, pl.ds(DEPTH - 2, 2), :]
-            bulk[pl.ds(n * INNER, INNER), :] = relaxed[f, y, pl.ds(2, INNER), :]
+            to[pl.ds(n * EDGE, EDGE), :] = z_in[pl.ds(TROWS + (f * 2 + y) * EDGE, EDGE), :]
+            if f not in FLAT_Y:
+                to[pl.ds(BLOCK_AT + inner * DEPTH, DEPTH), :] = relaxed[f, y, :, :]
+                inner += 1
+        y = 1 if way else 0
+        for chunk in range(DEPTH // 8):
+            rows = pl.ds(8 * chunk, 8)
+            keep = 1.0 - (1.0 - relaxed[MASK, y, rows, :]) * zone
+            for n, i in enumerate(FLAT_Y):
+                inside[n, pl.ds(8 + 8 * chunk, 8), :] = relaxed[i, y, rows, :] * keep
+        for n in range(len(FLAT_Y)):
+            inside[n, pl.ds(0, 8), :] = zero
+            inside[n, pl.ds(8 + DEPTH, 16), :] = jnp.zeros((16, 128), jnp.float32)
+        for chunk in range(5):
+            g = {}
+            for n, i in enumerate(FLAT_Y):
+                cx, _, cz = lattice_vel[i]
+                v = inside[n, pl.ds(7 + 8 * chunk - cz, 8), :]
+                if cx == 1:
+                    v = jnp.where(lane == 0, 0.0, pltpu.roll(v, 1, 1))
+                if cx == -1:
+                    v = jnp.where(lane == COLS - 1, 0.0, pltpu.roll(v, COLS - 1, 1))
+                g[i] = v
+            w0, w1, w2 = lattice_weight[0], lattice_weight[1], lattice_weight[7]
+            d12, d56 = g[1] - g[2], g[5] - g[6]
+            d1112, d1314 = g[11] - g[12], g[13] - g[14]
+            totals = (
+                w0 * g[0] + w1 * ((g[1] + g[2]) + (g[5] + g[6])) + w2 * ((g[11] + g[12]) + (g[13] + g[14])),
+                w1 * d12 + w2 * (d1112 + d1314),
+                w1 * d56 + w2 * (d1112 - d1314),
+            )
+            many = min(8, DEPTH + 2 - 8 * chunk)
+            for n, v in enumerate(totals):
+                to[pl.ds(SUMS_AT + n * (DEPTH + 2) + 8 * chunk, many), :] = v[:many]
 
     for at, way in enumerate(ways):
-        ysm[at][pl.ds(0, TROWS), :] = columns
         if way is None:
+            gy = lax.axis_index("gy")
 
             @pl.when(gy == 0)
             def _():
-                pack(True, ysm[at], ymn[at])
+                pack(True, bulk[at])
 
             @pl.when(gy != 0)
             def _():
-                pack(False, ysm[at], ymn[at])
+                pack(False, bulk[at])
 
         else:
-            pack(way, ysm[at], ymn[at])
+            pack(way, bulk[at])
 
 
 def join(mine, other):
@@ -453,8 +491,8 @@
 
 def steps_kernel(ways, total_y, total_x, lam, relaxed, zmsg, cols, *rest):
     count = len(ways)
-    bulk, small, small_other = rest[:count], rest[count : 2 * count], rest[2 * count : 3 * count]
-    result, early, late, out, sem = rest[3 * count :]
+    bulk = rest[:count]
+    result, early, late, out, sem = rest[count:]
     gx, gy = lax.axis_index("gx"), lax.axis_index("gy")
     at_end = gx == total_x // COLS - 1
     bottom, top = gy == 0, gy == total_y // ROWS - 1
@@ -498,20 +536,23 @@
             g.append(v)
         return g
 
-    def collide(slot, wanted, mine):
-        for chunk in range(5):
-            at = 1 + 8 * chunk
-            g = pull(early, slot, 0, 0, at, 0, mine)
-            density, vx, vy, vz = moments(g)
-            eq = equilibria(density, vx, vy, vz, wanted)
-            goal = goals(1, slot, at, wanted)
-            solid = early[MASK, slot, pl.ds(at, 8), :]
-            gate = (1.0 - solid) * zone
-            wall = solid == 1.0
-            for i in wanted:
-                loose = g[i] - relax_rate * (g[i] - eq[i])
-                v = jnp.where(wall, g[opposite[i]], loose)
-                late[i, slot - 1, pl.ds(8 * chunk, 8), :] = v + gate * (goal[i] - v)
+    def collide(slot, wanted, chunk, came=None):
+        at = 1 + 8 * chunk
+        g = pull(early, slot, 0, 0, at, 0, came is None)
+        total = sums(g)
+        if came is not None:
+            density, mx, mz = (came[pl.ds(SUMS_AT + n * (DEPTH + 2) + 8 * chunk, 8), :] for n in range(3))
+            total = (total[0] + density, total[1] + mx, total[2], total[3] + mz)
+        density, vx, vy, vz = velocity(*total)
+        eq = equilibria(density, vx, vy, vz, wanted)
+        goal = goals(1, slot, at, wanted)
+        solid = early[MASK, slot, pl.ds(at, 8), :]
+        gate = (1.0 - solid) * zone
+        wall = solid == 1.0
+        for i in wanted:
+            loose = g[i] - relax_rate * (g[i] - eq[i])
+            v = jnp.where(wall, g[opposite[i]], loose)
+            late[i, slot - 1, pl.ds(8 * chunk, 8), :] = v + gate * (goal[i] - v)
 
     for f in range(20):
         for y in range(ROWS):
@@ -525,18 +566,22 @@
 
     def beside(n, came_up):
         near_slot, far_slot = (1, 0) if came_up else (4, 5)
+        inner = 0
         for k, (f, near) in enumerate(up_down(came_up)):
             slot = near_slot if near else far_slot
-            at = TROWS + k * EDGE
-            early[f, slot, pl.ds(0, 2), :] = small_other[n][pl.ds(at + 2, 2), :]
-            early[f, slot, pl.ds(2, 2), :] = small[n][pl.ds(at, 2), :]
-            early[f, slot, pl.ds(4, INNER), :] = bulk[n][pl.ds(k * INNER, INNER), :]
-            early[f, slot, pl.ds(DEPTH, 2), :] = small[n][pl.ds(at + 2, 2), :]
-            early[f, slot, pl.ds(DEPTH + 2, 2), :] = small_other[n][pl.ds(at, 2), :]
+            at = k * EDGE
+            early[f, slot, pl.ds(0, 2), :] = bulk[n][pl.ds(at + 2, 2), :]
+            early[f, slot, pl.ds(DEPTH + 2, 2), :] = bulk[n][pl.ds(at, 2), :]
+            if f in FLAT_Y:
+                early[f, slot, pl.ds(2, DEPTH), :] = jnp.zeros((DEPTH, 128), jnp.float32)
+            else:
+                early[f, slot, pl.ds(2, DEPTH), :] = bulk[n][pl.ds(BLOCK_AT + inner * DEPTH, DEPTH), :]
+                inner += 1
         moving = UP if came_up else DOWN
         finish(near_slot, FLAT_Y + moving)
         finish(far_slot, moving)
-        collide(near_slot, moving, False)
+        for chunk in range(5):
+            collide(near_slot, moving, chunk, bulk[n])
 
     for n, way in enumerate(ways):
         if way is not False:
@@ -551,16 +596,18 @@
             def _():
                 beside(n, False)
 
-    for slot in (2, 3):
-        collide(slot, range(19), True)
     stores = []
-    for chunk in range(DEPTH // 8):
+    for chunk in range(5):
+        for slot in (2, 3):
+            collide(slot, range(19), chunk)
+        if chunk == 0:
+            continue
         for y in range(ROWS):
-            g = pull(late, 2 + y, 1, 1, 2 + 8 * chunk, 1, True)
+            g = pull(late, 2 + y, 1, 1, 8 * chunk - 6, 1, True)
             for i in range(19):
-                out[i, pl.ds(16 * chunk + y, 8, stride=2), :] = g[i]
-        rows = pl.ds(16 * chunk, 16)
-        stores.append(pltpu.make_async_copy(out.at[:, rows, :], result.at[:, rows, :], sem.at[chunk]))
+                out[i, pl.ds(16 * (chunk - 1) + y, 8, stride=2), :] = g[i]
+        rows = pl.ds(16 * (chunk - 1), 16)
+        stores.append(pltpu.make_async_copy(out.at[:, rows, :], result.at[:, rows, :], sem.at[chunk - 1]))
         stores[-1].start()
     for copy in stores:
         copy.wait()
@@ -597,9 +644,9 @@
     pops = populations.reshape(19, DEPTH * ROWS, COLS)
     solid = solid_mask.reshape(DEPTH * ROWS, COLS)
 
-    made = call(
-        functools.partial(relax_kernel, ways, total_x),
-        [(20, ROWS, DEPTH, COLS), (8, 128), (TROWS + 40 * EDGE, 128)] + [(TROWS + 88, 128)] * len(ways) + [(592, 128)] * len(ways),
+    relaxed, lam, columns, z_out = call(
+        functools.partial(relax_kernel, total_x),
+        [(20, ROWS, DEPTH, COLS), (8, 128), (TROWS, 128), (TROWS + 40 * EDGE, 128)],
         [
             (128, 128),
             pops.shape,
@@ -622,22 +669,28 @@
         fluct_scale,
         held=True,
     )
-    relaxed, lam, z_out = made[:3]
-    small_out, bulk_out = made[3 : 3 + len(ways)], made[3 + len(ways) :]
-
     def across(v, way):
         if way is None:
             return lax.ppermute(v, "gy", ring(2, 1))
         step = 1 if way else -1
         return lax.ppermute(v, "gy", [(i, i + step) for i in range(size_y) if 0 <= i + step < size_y])
 
-    small = [across(v, way) for v, way in zip(small_out, ways)]
+    beside = [across(columns, way) for way in ways]
+    z_in = lax.ppermute(z_out, "gz", ring(2, 1))
+    bulk_out = call(
+        functools.partial(pack_kernel, ways),
+        [(BULK, 128)] * len(ways),
+        [(len(FLAT_Y), DEPTH + 24, 128)],
+        4,
+        relaxed,
+        lam,
+        z_in,
+    )
     bulk = [across(v, way) for v, way in zip(bulk_out, ways)]
-    z_in = lax.ppermute(z_out, "gz", ring(2, 1))
-    small_other = [lax.ppermute(v, "gz", ring(2, 1)) for v in small]
-
-    blocks = [z_out, z_in]
-    for a, b in zip(small, small_other):
+    beside_other = [lax.ppermute(v, "gz", ring(2, 1)) for v in beside]
+
+    blocks = [columns, z_in]
+    for a, b in zip(beside, beside_other):
         blocks += [a, b]
     edge_rows = 72
     full, right, left, plane, gains = call(
@@ -686,8 +739,6 @@
         z_in,
         cols,
         *bulk,
-        *small,
-        *small_other,
         leave=True,
     )
     return out.reshape(populations.shape)

time: 21.9 us -> 21.3 us (0.973)
  waiting for transfers between devices: 6.52 us -> 5.76 us
  Pallas kernels: 5 us -> 5.35 us
  starting transfers between devices: 9.56 us -> 9.34 us
    ppermute x2, waiting for transfers between devices: 2.71 us -> 0.88 us  [across(): return lax.ppermute(v, 'gy', ring(2, 1))]
    ppermute x1, waiting for transfers between devices: 0.01 us -> 1.23 us  [body(): beside_other = [lax.ppermute(v, 'gz', ring(2, 1)) for v in beside]]
    ppermute x2, starting transfers between devices: 4.88 us -> 3.89 us  [across(): return lax.ppermute(v, 'gy', ring(2, 1))]
    ppermute x1, starting transfers between devices: 0.01 us -> 0.52 us  [body(): z_in = lax.ppermute(z_out, 'gz', ring(2, 1))]
    pallas_call x4 -> x5, Pallas kernels: 5 us -> 5.35 us  [call(): pl.pallas_call(kernel, out_shape=[jax.ShapeDtypeStruct(s, jnp.float32) fo...]
    ppermute x1, starting transfers between devices: 1.63 us -> 1.9 us  [body(): west = lax.ppermute(right, 'gx', ring(size_x, 1))]
  transfers between devices with their start and end apart: 7 -> 7, of which waited for: 2 -> 3; matrix products, arithmetic and copies ran while one was open for 0% -> 0% of each run, Pallas kernels for 4% -> 5%
where the time goes in v3:
time: 21.3 us; the launch traced here: 21.1 us
  starting transfers between devices  9.34 us (44%)
  waiting for transfers between devices  5.76 us (27%)
  Pallas kernels  5.35 us (25%)
  between operations  0.69 us (3%)
    pallas_call x5, Pallas kernels, call(): pl.pallas_call(kernel, out_shape=[jax.ShapeDtypeStruct(s, jnp.float32) fo...  5.35 us
    ppermute x2, starting transfers between devices, across(): return lax.ppermute(v, 'gy', ring(2, 1))  3.89 us
    ppermute x1, waiting for transfers between devices, body(): far = lax.ppermute(plane, 'gx', ring(4, 2))  3.65 us
    ppermute x1, starting transfers between devices, body(): east = lax.ppermute(left, 'gx', ring(size_x, -1))  2.09 us
    ppermute x1, starting transfers between devices, body(): west = lax.ppermute(right, 'gx', ring(size_x, 1))  1.9 us
    ppermute x1, waiting for transfers between devices, body(): beside_other = [lax.ppermute(v, 'gz', ring(2, 1)) for v in beside]  1.23 us
    ppermute x1, starting transfers between devices, body(): far = lax.ppermute(plane, 'gx', ring(4, 2))  0.95 us
    ppermute x2, waiting for transfers between devices, across(): return lax.ppermute(v, 'gy', ring(2, 1))  0.88 us
  transfers between devices with their start and end apart: 7, of which 3 were waited for; matrix products, arithmetic and copies ran while one was open for 0% of the time, Pallas kernels for 5%

profile of v3, /device:TPU:0, one launch (start us, length us, event | category | flops | bytes accessed | tf_op | source)
XLA Modules:
  0.0 21.1 jit_solution(3156075932134307921)
XLA Ops:
  0.7 1.7 %shard_map.82 = (f32[20,2,32,128]{3,2,1,0:T(8,128)S(1)}, f32[8,128]{1,0:T(8,128)S(1)}, f32[96,128]{1,0:T(8,128)S(1)}, f32[256,128]{1,0:T(8,128)S(1)}) custom-call(s32[1]{0:T(128)S(6)} %copy.9.refs_0_, f32[19,64,128]{2,1,0:T(8,128)} %bitcast.3, s32[64,128]{1,0:T(8,128)} %bitcast.4, s32[2]{0:T(128)} %refs_3_.1, s32[2]{0:T(128)} %refs_4_.1, f32[2]{0:T(128)} %refs_5_.1, ...), custom_call_target="tpu_custom_call" | custom-call | tf_op jit(solution)/shard_map/pallas_call | solution.py:623
  2.4 0.5 %collective-permute-start = (f32[256,128]{1,0:T(8,128)S(1)}, f32[256,128]{1,0:T(8,128)S(1)}, u32[]{:S(2)}, u32[]{:S(2)}) collective-permute-start(f32[256,128]{1,0:T(8,128)S(1)} %get-tuple-element.16), channel_id=1, source_target_pairs={{0,1},{1,0},{2,3},{3,2},{4,5},{5,4},{6,7},{7,6},{8,9},{9,8},{10,11... | collective-permute-start | bytes 393224 | tf_op jit(solution)/shard_map/ppermute | solution.py:679
  2.9 2.6 %collective-permute-start.1 = (f32[96,128]{1,0:T(8,128)S(1)}, f32[96,128]{1,0:T(8,128)S(1)}, u32[]{:S(2)}, u32[]{:S(2)}) collective-permute-start(f32[96,128]{1,0:T(8,128)S(1)} %get-tuple-element.17.refs_0_), channel_id=1, source_target_pairs={{0,2},{2,0},{1,3},{3,1},{4,6},{6,4},{5,7},{7,5},{8,10},{10,8},{9,1... | collective-permute-start | bytes 147464 | tf_op jit(solution)/shard_map/ppermute | solution.py:674
  5.5 0.0 collective-permute-done.refs_1_.z_in.zmsg
  5.5 0.1 shard_map.85
  5.6 1.3 %collective-permute-start.6 = (f32[656,128]{1,0:T(8,128)S(1)}, f32[656,128]{1,0:T(8,128)S(1)}, u32[]{:S(2)}, u32[]{:S(2)}) collective-permute-start(f32[656,128]{1,0:T(8,128)S(1)} %shard_map.85), channel_id=1, source_target_pairs={{0,2},{2,0},{1,3},{3,1},{4,6},{6,4},{5,7},{7,5},{8,10},{10,8},{9,1... | collective-permute-start | bytes 1007624 | tf_op jit(solution)/shard_map/ppermute | solution.py:674
  6.9 0.9 %collective-permute-done.1.refs_2_ = f32[96,128]{1,0:T(8,128)S(1)} collective-permute-done((f32[96,128]{1,0:T(8,128)S(1)}, f32[96,128]{1,0:T(8,128)S(1)}, u32[]{:S(2)}, u32[]{:S(2)}) %collective-permute-start.1) | collective-permute-done | bytes 49184 | tf_op jit(solution)/shard_map/ppermute | solution.py:674
  7.8 0.0 collective-permute-start.2
  7.8 1.2 %collective-permute-done.2.refs_3_ = f32[96,128]{1,0:T(8,128)S(1)} collective-permute-done((f32[96,128]{1,0:T(8,128)S(1)}, f32[96,128]{1,0:T(8,128)S(1)}, u32[]{:S(2)}, u32[]{:S(2)}) %collective-permute-start.2) | collective-permute-done | bytes 49184 | tf_op jit(solution)/shard_map/ppermute | solution.py:690
  9.0 0.3 %shard_map.83 = (f32[2,192,128]{2,1,0:T(8,128)S(1)}, f32[72,128]{1,0:T(8,128)S(1)}, f32[72,128]{1,0:T(8,128)S(1)}, f32[24,128]{1,0:T(8,128)S(1)}, f32[32,128]{1,0:T(8,128)S(1)}) custom-call(f32[8,128]{1,0:T(8,128)S(1)} %get-tuple-element.14.lam, f32[96,128]{1,0:T(8,128)S(1)} %get-tuple-element.17.refs_0_, ...), custom_call_target="tpu_custom_call" | custom-call | tf_op jit(solution)/shard_map/pallas_call | solution.py:623
  9.3 1.9 %collective-permute-start.3 = (f32[72,128]{1,0:T(8,128)S(1)}, f32[72,128]{1,0:T(8,128)S(1)}, u32[]{:S(2)}, u32[]{:S(2)}) collective-permute-start(f32[72,128]{1,0:T(8,128)S(1)} %get-tuple-element.19), channel_id=1, source_target_pairs={{0,4},{4,8},{8,12},{12,0},{1,5},{5,9},{9,13},{13,1},{2,6},{6,10},{... | collective-permute-start | bytes 110600 | tf_op jit(solution)/shard_map/ppermute | solution.py:704
  11.2 2.1 %collective-permute-start.4 = (f32[72,128]{1,0:T(8,128)S(1)}, f32[72,128]{1,0:T(8,128)S(1)}, u32[]{:S(2)}, u32[]{:S(2)}) collective-permute-start(f32[72,128]{1,0:T(8,128)S(1)} %get-tuple-element.20), channel_id=1, source_target_pairs={{0,12},{4,0},{8,4},{12,8},{1,13},{5,1},{9,5},{13,9},{2,14},{6,2},{... | collective-permute-start | bytes 110600 | tf_op jit(solution)/shard_map/ppermute | solution.py:705
  13.3 0.9 %collective-permute-start.5 = (f32[24,128]{1,0:T(8,128)S(1)}, f32[24,128]{1,0:T(8,128)S(1)}, u32[]{:S(2)}, u32[]{:S(2)}) collective-permute-start(f32[24,128]{1,0:T(8,128)S(1)} %get-tuple-element.21), channel_id=1, source_target_pairs={{0,8},{4,12},{8,0},{12,4},{1,9},{5,13},{9,1},{13,5},{2,10},{6,14},... | collective-permute-start | bytes 36872 | tf_op jit(solution)/shard_map/ppermute | solution.py:707
  14.3 3.6 %collective-permute-done.5 = f32[24,128]{1,0:T(8,128)S(1)} collective-permute-done((f32[24,128]{1,0:T(8,128)S(1)}, f32[24,128]{1,0:T(8,128)S(1)}, u32[]{:S(2)}, u32[]{:S(2)}) %collective-permute-start.5) | collective-permute-done | bytes 12320 | tf_op jit(solution)/shard_map/ppermute | solution.py:707
  17.9 0.0 collective-permute-done.3.west
  17.9 0.0 collective-permute-done.4.east
  17.9 0.6 %shard_map.84.cols = f32[96,128]{1,0:T(8,128)S(1)} custom-call(f32[8,128]{1,0:T(8,128)S(1)} %get-tuple-element.14.lam, f32[2,192,128]{2,1,0:T(8,128)S(1)} %get-tuple-element.18.full, f32[72,128]{1,0:T(8,128)S(1)} %collective-permute-done.3.west, f32[72,128]{1,0:T(8,128)S(1)} %collective-permute-done.4.east, f32[24,128]{1,0:T(8,128)S(1)} %slice_add_fusion.plane, ...), custom_call_target="tpu_custom_call" | custom-call | tf_op jit(solution)/shard_map/pallas_call | solution.py:623
  18.6 0.0 collective-permute-done.6.rest_0_
  18.6 2.6 %shard_map.86 = f32[19,64,128]{2,1,0:T(8,128)} custom-call(f32[8,128]{1,0:T(8,128)S(1)} %get-tuple-element.14.lam, f32[20,2,32,128]{3,2,1,0:T(8,128)S(1)} %get-tuple-element.15.relaxed, f32[256,128]{1,0:T(8,128)S(1)} %collective-permute-done.refs_1_.z_in.zmsg, f32[96,128]{1,0:T(8,128)S(1)} %shard_map.84.cols, f32[656,128]{1,0:T(8,128)S(1)} %collective-permute-done.6.rest_0_), custom_call_target="tpu_custom_call" | custom-call | tf_op jit(solution)/shard_map/pallas_call | solution.py:623
  (1 shorter events, 0.0 us)
Async XLA Ops:
  2.4 3.1 %collective-permute-start = (f32[256,128]{1,0:T(8,128)S(1)}, f32[256,128]{1,0:T(8,128)S(1)}, u32[]{:S(2)}, u32[]{:S(2)}) collective-permute-start(f32[256,128]{1,0:T(8,128)S(1)} %get-tuple-element.16), channel_id=1, source_target_pairs={{0,1},{1,0},{2,3},{3,2},{4,5},{5,4},{6,7},{7,6},{8,9},{9,8},{10,11... | collective-permute-start | bytes 393224 | tf_op jit(solution)/shard_map/ppermute | solution.py:679
  2.9 4.9 %collective-permute-start.1 = (f32[96,128]{1,0:T(8,128)S(1)}, f32[96,128]{1,0:T(8,128)S(1)}, u32[]{:S(2)}, u32[]{:S(2)}) collective-permute-start(f32[96,128]{1,0:T(8,128)S(1)} %get-tuple-element.17.refs_0_), channel_id=1, source_target_pairs={{0,2},{2,0},{1,3},{3,1},{4,6},{6,4},{5,7},{7,5},{8,10},{10,8},{9,1... | collective-permute-start | bytes 147464 | tf_op jit(solution)/shard_map/ppermute | solution.py:674
  5.6 13.0 %collective-permute-start.6 = (f32[656,128]{1,0:T(8,128)S(1)}, f32[656,128]{1,0:T(8,128)S(1)}, u32[]{:S(2)}, u32[]{:S(2)}) collective-permute-start(f32[656,128]{1,0:T(8,128)S(1)} %shard_map.85), channel_id=1, source_target_pairs={{0,2},{2,0},{1,3},{3,1},{4,6},{6,4},{5,7},{7,5},{8,10},{10,8},{9,1... | collective-permute-start | bytes 1007624 | tf_op jit(solution)/shard_map/ppermute | solution.py:674
  7.8 1.2 %collective-permute-start.2 = (f32[96,128]{1,0:T(8,128)S(1)}, f32[96,128]{1,0:T(8,128)S(1)}, u32[]{:S(2)}, u32[]{:S(2)}) collective-permute-start(f32[96,128]{1,0:T(8,128)S(1)} %collective-permute-done.1.refs_2_), channel_id=1, source_target_pairs={{0,1},{1,0},{2,3},{3,2},{4,5},{5,4},{6,7},{7,6},{8,9},{9,8},{10,11... | collective-permute-start | bytes 147464 | tf_op jit(solution)/shard_map/ppermute | solution.py:690
  9.3 8.6 %collective-permute-start.3 = (f32[72,128]{1,0:T(8,128)S(1)}, f32[72,128]{1,0:T(8,128)S(1)}, u32[]{:S(2)}, u32[]{:S(2)}) collective-permute-start(f32[72,128]{1,0:T(8,128)S(1)} %get-tuple-element.19), channel_id=1, source_target_pairs={{0,4},{4,8},{8,12},{12,0},{1,5},{5,9},{9,13},{13,1},{2,6},{6,10},{... | collective-permute-start | bytes 110600 | tf_op jit(solution)/shard_map/ppermute | solution.py:704
  11.2 6.7 %collective-permute-start.4 = (f32[72,128]{1,0:T(8,128)S(1)}, f32[72,128]{1,0:T(8,128)S(1)}, u32[]{:S(2)}, u32[]{:S(2)}) collective-permute-start(f32[72,128]{1,0:T(8,128)S(1)} %get-tuple-element.20), channel_id=1, source_target_pairs={{0,12},{4,0},{8,4},{12,8},{1,13},{5,1},{9,5},{13,9},{2,14},{6,2},{... | collective-permute-start | bytes 110600 | tf_op jit(solution)/shard_map/ppermute | solution.py:705
  13.3 4.6 %collective-permute-start.5 = (f32[24,128]{1,0:T(8,128)S(1)}, f32[24,128]{1,0:T(8,128)S(1)}, u32[]{:S(2)}, u32[]{:S(2)}) collective-permute-start(f32[24,128]{1,0:T(8,128)S(1)} %get-tuple-element.21), channel_id=1, source_target_pairs={{0,8},{4,12},{8,0},{12,4},{1,9},{5,13},{9,1},{13,5},{2,10},{6,14},... | collective-permute-start | bytes 36872 | tf_op jit(solution)/shard_map/ppermute | solution.py:707

commit v4 on v3

--- a/solution.py
+++ b/solution.py
@@ -48,7 +48,9 @@
 COLUMN = EAST + (MASK,) + WEST + FLAT_X + (20, 21, 22, 23)
 PLACE = {field: at for at, field in enumerate(COLUMN)}
 HALF = len(COLUMN) // 2
-TROWS = HALF * 8
+PACKED = ((1, 0, 12), (2, 0, 12), (5, 0, 12), (0, 0, 6), (4, 0, 6), (3, 5, 6), (6, 5, 6), (7, 0, 4))
+WHOLE = 36
+TROWS = 64
 SIDE = 20
 TO_EAST = ((0, 0, 8), (0, 11, 9), (1, 0, 6))
 TO_WEST = ((0, 3, 8), (0, 11, 9), (1, 5, 6))
@@ -60,7 +62,7 @@
 EDGE = 4
 BLOCK_AT = 88
 SUMS_AT = BLOCK_AT + 12 * DEPTH
-BULK = 656
+BULK = SUMS_AT + 2 * (DEPTH + 2) + 44
 PIECES = 2
 
 
@@ -204,8 +206,13 @@
                 rest_of = extras[y] if half == 0 else jnp.zeros((8, 128), jnp.float32)
                 packed = jnp.where(static, fixed, jnp.where(here, moving, rest_of))
                 grid[pl.ds((y * 2 + half) * DEPTH + 8 * chunk, 8), :] = packed
-    columns[...] = grid[...].T[:TROWS]
-    zmsg[pl.ds(0, TROWS), :] = columns[...]
+    grid[...] = grid[...].T
+    at = 0
+    for c, place, many in PACKED:
+        v = grid[pl.ds(8 * place + c, many, stride=8), :]
+        columns[pl.ds(at, many), :] = v
+        zmsg[pl.ds(at, many), :] = v
+        at += many
     for f in range(20):
         for y in range(ROWS):
             at = TROWS + (f * 2 + y) * EDGE
@@ -214,7 +221,13 @@
 
 
 def pack_kernel(ways, relaxed, lam, z_in, *rest):
-    bulk, inside = rest[:-1], rest[-1]
+    laid, bulk, inside = rest[0], rest[1:-1], rest[-1]
+    for f in range(20):
+        for y in range(ROWS):
+            at = TROWS + (f * 2 + y) * EDGE
+            laid[f, y, pl.ds(0, 2), :] = z_in[pl.ds(at + 2, 2), :]
+            laid[f, y, pl.ds(2, DEPTH), :] = relaxed[f, y, :, :]
+            laid[f, y, pl.ds(DEPTH + 2, 2), :] = z_in[pl.ds(at, 2), :]
     lane = lanes((8, 128))
     zone = jnp.broadcast_to(lam[0:1, :], (8, 128))
     zero = jnp.zeros((8, 128), jnp.float32)
@@ -338,8 +351,12 @@
         first, second = join(
             blocks[2 * n][pl.ds(0, TROWS), :], blocks[2 * n + 1][pl.ds(0, TROWS), :]
         )
-        full[n, pl.ds(0, TROWS), :] = first
-        full[n, pl.ds(TROWS, TROWS), :] = second
+        at = 0
+        for c, place, many in PACKED:
+            full[n, pl.ds(8 * place + c, many, stride=8), :] = first[at : at + many]
+            if at < WHOLE:
+                full[n, pl.ds(8 * HALF + c, many, stride=8), :] = second[at : at + many]
+            at += many
         at = n * TRAVEL
         for (c, place, many), (d, spot, count) in zip(TO_EAST, TO_WEST):
             right[pl.ds(at, many), :] = full[n, pl.ds(8 * place + 1 - c, many, stride=8), :]
@@ -489,7 +506,7 @@
         out[pl.ds(48 * n, 48), :] = turned[:48]
 
 
-def steps_kernel(ways, total_y, total_x, lam, relaxed, zmsg, cols, *rest):
+def steps_kernel(ways, total_y, total_x, lam, laid, cols, *rest):
     count = len(ways)
     bulk = rest[:count]
     result, early, late, out, sem = rest[count:]
@@ -503,17 +520,21 @@
     def column(step, index, at):
         return jnp.broadcast_to(cols[pl.ds(48 * step + at, 8), index : index + 1], (8, 128))
 
-    def goals(step, slot, at, wanted):
-        return equilibria(*(column(step, 80 + 8 * k + slot, at) for k in range(4)), wanted)
+    def goals(step, slot, at, wanted, gate):
+        density, vx, vy, vz = (column(step, 80 + 8 * k + slot, at) for k in range(4))
+        return equilibria(gate * density, vx, vy, vz, wanted)
+
+    def field(i, slot, rows):
+        return laid[i, slot - 2, rows, :] if slot in (2, 3) else early[i, slot, rows, :]
 
     def finish(slot, fields):
         for chunk in range(5):
             rows = pl.ds(8 * chunk, 8)
-            gate = (1.0 - early[MASK, slot, rows, :]) * zone
-            goal = goals(0, slot, 8 * chunk, fields)
+            gate = (1.0 - field(MASK, slot, rows)) * zone
+            goal = goals(0, slot, 8 * chunk, fields, gate)
+            keep = 1.0 - gate
             for i in fields:
-                v = early[i, slot, rows, :]
-                early[i, slot, rows, :] = v + gate * (goal[i] - v)
+                early[i, slot, rows, :] = keep * field(i, slot, rows) + goal[i]
 
     def pull(ref, slot, lead, step, at, lift, mine):
         r = at - lift
@@ -544,23 +565,16 @@
             density, mx, mz = (came[pl.ds(SUMS_AT + n * (DEPTH + 2) + 8 * chunk, 8), :] for n in range(3))
             total = (total[0] + density, total[1] + mx, total[2], total[3] + mz)
         density, vx, vy, vz = velocity(*total)
-        eq = equilibria(density, vx, vy, vz, wanted)
-        goal = goals(1, slot, at, wanted)
-        solid = early[MASK, slot, pl.ds(at, 8), :]
+        eq = equilibria(relax_rate * density, vx, vy, vz, wanted)
+        solid = field(MASK, slot, pl.ds(at, 8))
         gate = (1.0 - solid) * zone
+        goal = goals(1, slot, at, wanted, gate)
+        keep = 1.0 - gate
         wall = solid == 1.0
         for i in wanted:
-            loose = g[i] - relax_rate * (g[i] - eq[i])
-            v = jnp.where(wall, g[opposite[i]], loose)
-            late[i, slot - 1, pl.ds(8 * chunk, 8), :] = v + gate * (goal[i] - v)
-
-    for f in range(20):
-        for y in range(ROWS):
-            slot = 2 + y
-            at = TROWS + (f * 2 + y) * EDGE
-            early[f, slot, pl.ds(2, DEPTH), :] = relaxed[f, y, :, :]
-            early[f, slot, pl.ds(DEPTH + 2, 2), :] = zmsg[pl.ds(at, 2), :]
-            early[f, slot, pl.ds(0, 2), :] = zmsg[pl.ds(at + 2, 2), :]
+            v = jnp.where(wall, g[opposite[i]], (1.0 - relax_rate) * g[i] + eq[i])
+            late[i, slot - 1, pl.ds(8 * chunk, 8), :] = keep * v + goal[i]
+
     for slot in (2, 3):
         finish(slot, range(19))
 
@@ -600,8 +614,7 @@
     for chunk in range(5):
         for slot in (2, 3):
             collide(slot, range(19), chunk)
-        if chunk == 0:
-            continue
+    for chunk in range(1, 5):
         for y in range(ROWS):
             g = pull(late, 2 + y, 1, 1, 8 * chunk - 6, 1, True)
             for i in range(19):
@@ -677,9 +690,9 @@
 
     beside = [across(columns, way) for way in ways]
     z_in = lax.ppermute(z_out, "gz", ring(2, 1))
-    bulk_out = call(
+    laid, *bulk_out = call(
         functools.partial(pack_kernel, ways),
-        [(BULK, 128)] * len(ways),
+        [(20, ROWS, DEPTH + 16, COLS)] + [(BULK, 128)] * len(ways),
         [(len(FLAT_Y), DEPTH + 24, 128)],
         4,
         relaxed,
@@ -695,7 +708,7 @@
     edge_rows = 72
     full, right, left, plane, gains = call(
         functools.partial(cross_kernel, slots, swap, total_y),
-        [(pairs, 2 * TROWS, 128), (edge_rows, 128), (edge_rows, 128), (24 if swap else 8 * (SUMS + 4), 128), (32, 128)],
+        [(pairs, 16 * HALF, 128), (edge_rows, 128), (edge_rows, 128), (24 if swap else 8 * (SUMS + 4), 128), (32, 128)],
         [(8 * DECK_ROWS, 128)],
         4,
         lam,
@@ -732,11 +745,10 @@
     (out,) = call(
         functools.partial(steps_kernel, ways, total_y, total_x),
         [(19, DEPTH * ROWS, COLS)],
-        [(20, 6, 48, 128), (19, 4, 48, 128), (19, DEPTH * ROWS, COLS), pltpu.SemaphoreType.DMA((DEPTH // 8,))],
+        [(20, 6, 48, 128), (19, 4, 40, 128), (19, DEPTH * ROWS, COLS), pltpu.SemaphoreType.DMA((DEPTH // 8,))],
         12,
         lam,
-        relaxed,
-        z_in,
+        laid,
         cols,
         *bulk,
         leave=True,

time: 21.3 us -> 20.8 us (0.977)
  waiting for transfers between devices: 5.76 us -> 5.35 us
  Pallas kernels: 5.35 us -> 5.06 us
    ppermute x2, waiting for transfers between devices: 0.88 us -> 0.49 us  [across(): return lax.ppermute(v, 'gy', ring(2, 1))]
    pallas_call x5, Pallas kernels: 5.35 us -> 5.06 us  [call(): pl.pallas_call(kernel, out_shape=[jax.ShapeDtypeStruct(s, jnp.float32) fo...]
where the time goes in v4:
time: 20.8 us; the launch traced here: 20.6 us
  starting transfers between devices  9.49 us (46%)
  waiting for transfers between devices  5.35 us (26%)
  Pallas kernels  5.06 us (24%)
  between operations  0.68 us (3%)
    pallas_call x5, Pallas kernels, call(): pl.pallas_call(kernel, out_shape=[jax.ShapeDtypeStruct(s, jnp.float32) fo...  5.06 us
    ppermute x2, starting transfers between devices, across(): return lax.ppermute(v, 'gy', ring(2, 1))  3.87 us
    ppermute x1, waiting for transfers between devices, body(): far = lax.ppermute(plane, 'gx', ring(4, 2))  3.65 us
    ppermute x1, starting transfers between devices, body(): east = lax.ppermute(left, 'gx', ring(size_x, -1))  2.09 us
    ppermute x1, starting transfers between devices, body(): west = lax.ppermute(right, 'gx', ring(size_x, 1))  2.07 us
    ppermute x1, waiting for transfers between devices, body(): beside_other = [lax.ppermute(v, 'gz', ring(2, 1)) for v in beside]  1.2 us
    ppermute x1, starting transfers between devices, body(): far = lax.ppermute(plane, 'gx', ring(4, 2))  0.95 us
    ppermute x1, starting transfers between devices, body(): z_in = lax.ppermute(z_out, 'gz', ring(2, 1))  0.52 us
  transfers between devices with their start and end apart: 7, of which 3 were waited for; matrix products, arithmetic and copies ran while one was open for 0% of the time, Pallas kernels for 5%

profile of v4, /device:TPU:0, one launch (start us, length us, event | category | flops | bytes accessed | tf_op | source)
XLA Modules:
  0.0 20.6 jit_solution(8739116026721510112)
XLA Ops:
  0.7 1.7 %shard_map.82 = (f32[20,2,32,128]{3,2,1,0:T(8,128)S(1)}, f32[8,128]{1,0:T(8,128)S(1)}, f32[64,128]{1,0:T(8,128)S(1)}, f32[224,128]{1,0:T(8,128)S(1)}) custom-call(s32[1]{0:T(128)S(6)} %copy.9.refs_0_, f32[19,64,128]{2,1,0:T(8,128)} %bitcast.3, s32[64,128]{1,0:T(8,128)} %bitcast.4, s32[2]{0:T(128)} %refs_3_.1, s32[2]{0:T(128)} %refs_4_.1, f32[2]{0:T(128)} %refs_5_.1, ...), custom_call_target="tpu_custom_call" | custom-call | tf_op jit(solution)/shard_map/pallas_call | solution.py:636
  2.4 0.5 %collective-permute-start = (f32[224,128]{1,0:T(8,128)S(1)}, f32[224,128]{1,0:T(8,128)S(1)}, u32[]{:S(2)}, u32[]{:S(2)}) collective-permute-start(f32[224,128]{1,0:T(8,128)S(1)} %get-tuple-element.18), channel_id=1, source_target_pairs={{0,1},{1,0},{2,3},{3,2},{4,5},{5,4},{6,7},{7,6},{8,9},{9,8},{10,11... | collective-permute-start | bytes 344072 | tf_op jit(solution)/shard_map/ppermute | solution.py:692
  2.9 2.6 %collective-permute-start.1 = (f32[64,128]{1,0:T(8,128)S(1)}, f32[64,128]{1,0:T(8,128)S(1)}, u32[]{:S(2)}, u32[]{:S(2)}) collective-permute-start(f32[64,128]{1,0:T(8,128)S(1)} %get-tuple-element.20.refs_0_), channel_id=1, source_target_pairs={{0,2},{2,0},{1,3},{3,1},{4,6},{6,4},{5,7},{7,5},{8,10},{10,8},{9,1... | collective-permute-start | bytes 98312 | tf_op jit(solution)/shard_map/ppermute | solution.py:687
  5.5 0.0 collective-permute-done.z_in.refs_1_
  5.5 0.2 shard_map.83
  5.7 1.3 %collective-permute-start.6 = (f32[584,128]{1,0:T(8,128)S(1)}, f32[584,128]{1,0:T(8,128)S(1)}, u32[]{:S(2)}, u32[]{:S(2)}) collective-permute-start(f32[584,128]{1,0:T(8,128)S(1)} %get-tuple-element.26), channel_id=1, source_target_pairs={{0,2},{2,0},{1,3},{3,1},{4,6},{6,4},{5,7},{7,5},{8,10},{10,8},{9,1... | collective-permute-start | bytes 897032 | tf_op jit(solution)/shard_map/ppermute | solution.py:687
  7.0 0.5 %collective-permute-done.1.refs_2_ = f32[64,128]{1,0:T(8,128)S(1)} collective-permute-done((f32[64,128]{1,0:T(8,128)S(1)}, f32[64,128]{1,0:T(8,128)S(1)}, u32[]{:S(2)}, u32[]{:S(2)}) %collective-permute-start.1) | collective-permute-done | bytes 32800 | tf_op jit(solution)/shard_map/ppermute | solution.py:687
  7.5 0.0 collective-permute-start.2
  7.5 1.2 %collective-permute-done.2.refs_3_ = f32[64,128]{1,0:T(8,128)S(1)} collective-permute-done((f32[64,128]{1,0:T(8,128)S(1)}, f32[64,128]{1,0:T(8,128)S(1)}, u32[]{:S(2)}, u32[]{:S(2)}) %collective-permute-start.2) | collective-permute-done | bytes 32800 | tf_op jit(solution)/shard_map/ppermute | solution.py:703
  8.7 0.3 %shard_map.84 = (f32[2,192,128]{2,1,0:T(8,128)S(1)}, f32[72,128]{1,0:T(8,128)S(1)}, f32[72,128]{1,0:T(8,128)S(1)}, f32[24,128]{1,0:T(8,128)S(1)}, f32[32,128]{1,0:T(8,128)S(1)}) custom-call(f32[8,128]{1,0:T(8,128)S(1)} %get-tuple-element.16.lam, f32[64,128]{1,0:T(8,128)S(1)} %get-tuple-element.20.refs_0_, f32[224,128]{1,0:T(8,128)S(1)} %collective-permute-done.z_in.refs_1_, ...), custom_call_target="tpu_custom_call" | custom-call | tf_op jit(solution)/shard_map/pallas_call | solution.py:636
  9.0 2.1 %collective-permute-start.3 = (f32[72,128]{1,0:T(8,128)S(1)}, f32[72,128]{1,0:T(8,128)S(1)}, u32[]{:S(2)}, u32[]{:S(2)}) collective-permute-start(f32[72,128]{1,0:T(8,128)S(1)} %get-tuple-element.22), channel_id=1, source_target_pairs={{0,4},{4,8},{8,12},{12,0},{1,5},{5,9},{9,13},{13,1},{2,6},{6,10},{... | collective-permute-start | bytes 110600 | tf_op jit(solution)/shard_map/ppermute | solution.py:717
  11.0 2.1 %collective-permute-start.4 = (f32[72,128]{1,0:T(8,128)S(1)}, f32[72,128]{1,0:T(8,128)S(1)}, u32[]{:S(2)}, u32[]{:S(2)}) collective-permute-start(f32[72,128]{1,0:T(8,128)S(1)} %get-tuple-element.23), channel_id=1, source_target_pairs={{0,12},{4,0},{8,4},{12,8},{1,13},{5,1},{9,5},{13,9},{2,14},{6,2},{... | collective-permute-start | bytes 110600 | tf_op jit(solution)/shard_map/ppermute | solution.py:718
  13.1 0.9 %collective-permute-start.5 = (f32[24,128]{1,0:T(8,128)S(1)}, f32[24,128]{1,0:T(8,128)S(1)}, u32[]{:S(2)}, u32[]{:S(2)}) collective-permute-start(f32[24,128]{1,0:T(8,128)S(1)} %get-tuple-element.24), channel_id=1, source_target_pairs={{0,8},{4,12},{8,0},{12,4},{1,9},{5,13},{9,1},{13,5},{2,10},{6,14},... | collective-permute-start | bytes 36872 | tf_op jit(solution)/shard_map/ppermute | solution.py:720
  14.1 3.6 %collective-permute-done.5 = f32[24,128]{1,0:T(8,128)S(1)} collective-permute-done((f32[24,128]{1,0:T(8,128)S(1)}, f32[24,128]{1,0:T(8,128)S(1)}, u32[]{:S(2)}, u32[]{:S(2)}) %collective-permute-start.5) | collective-permute-done | bytes 12320 | tf_op jit(solution)/shard_map/ppermute | solution.py:720
  17.7 0.0 collective-permute-done.3.west
  17.7 0.0 collective-permute-done.4.east
  17.7 0.6 %shard_map.85.cols = f32[96,128]{1,0:T(8,128)S(1)} custom-call(f32[8,128]{1,0:T(8,128)S(1)} %get-tuple-element.16.lam, f32[2,192,128]{2,1,0:T(8,128)S(1)} %get-tuple-element.21.full, f32[72,128]{1,0:T(8,128)S(1)} %collective-permute-done.3.west, f32[72,128]{1,0:T(8,128)S(1)} %collective-permute-done.4.east, f32[24,128]{1,0:T(8,128)S(1)} %slice_add_fusion.plane, ...), custom_call_target="tpu_custom_call" | custom-call | tf_op jit(solution)/shard_map/pallas_call | solution.py:636
  18.4 0.0 collective-permute-done.6.rest_0_
  18.4 2.2 %shard_map.86 = f32[19,64,128]{2,1,0:T(8,128)} custom-call(f32[8,128]{1,0:T(8,128)S(1)} %get-tuple-element.16.lam, f32[20,2,48,128]{3,2,1,0:T(8,128)S(1)} %get-tuple-element.19.laid, f32[96,128]{1,0:T(8,128)S(1)} %shard_map.85.cols, f32[584,128]{1,0:T(8,128)S(1)} %collective-permute-done.6.rest_0_), custom_call_target="tpu_custom_call" | custom-call | tf_op jit(solution)/shard_map/pallas_call | solution.py:636
  (1 shorter events, 0.0 us)
Async XLA Ops:
  2.4 3.1 %collective-permute-start = (f32[224,128]{1,0:T(8,128)S(1)}, f32[224,128]{1,0:T(8,128)S(1)}, u32[]{:S(2)}, u32[]{:S(2)}) collective-permute-start(f32[224,128]{1,0:T(8,128)S(1)} %get-tuple-element.18), channel_id=1, source_target_pairs={{0,1},{1,0},{2,3},{3,2},{4,5},{5,4},{6,7},{7,6},{8,9},{9,8},{10,11... | collective-permute-start | bytes 344072 | tf_op jit(solution)/shard_map/ppermute | solution.py:692
  2.9 4.5 %collective-permute-start.1 = (f32[64,128]{1,0:T(8,128)S(1)}, f32[64,128]{1,0:T(8,128)S(1)}, u32[]{:S(2)}, u32[]{:S(2)}) collective-permute-start(f32[64,128]{1,0:T(8,128)S(1)} %get-tuple-element.20.refs_0_), channel_id=1, source_target_pairs={{0,2},{2,0},{1,3},{3,1},{4,6},{6,4},{5,7},{7,5},{8,10},{10,8},{9,1... | collective-permute-start | bytes 98312 | tf_op jit(solution)/shard_map/ppermute | solution.py:687
  5.7 12.7 %collective-permute-start.6 = (f32[584,128]{1,0:T(8,128)S(1)}, f32[584,128]{1,0:T(8,128)S(1)}, u32[]{:S(2)}, u32[]{:S(2)}) collective-permute-start(f32[584,128]{1,0:T(8,128)S(1)} %get-tuple-element.26), channel_id=1, source_target_pairs={{0,2},{2,0},{1,3},{3,1},{4,6},{6,4},{5,7},{7,5},{8,10},{10,8},{9,1... | collective-permute-start | bytes 897032 | tf_op jit(solution)/shard_map/ppermute | solution.py:687
  7.5 1.2 %collective-permute-start.2 = (f32[64,128]{1,0:T(8,128)S(1)}, f32[64,128]{1,0:T(8,128)S(1)}, u32[]{:S(2)}, u32[]{:S(2)}) collective-permute-start(f32[64,128]{1,0:T(8,128)S(1)} %collective-permute-done.1.refs_2_), channel_id=1, source_target_pairs={{0,1},{1,0},{2,3},{3,2},{4,5},{5,4},{6,7},{7,6},{8,9},{9,8},{10,11... | collective-permute-start | bytes 98312 | tf_op jit(solution)/shard_map/ppermute | solution.py:703
  9.0 8.8 %collective-permute-start.3 = (f32[72,128]{1,0:T(8,128)S(1)}, f32[72,128]{1,0:T(8,128)S(1)}, u32[]{:S(2)}, u32[]{:S(2)}) collective-permute-start(f32[72,128]{1,0:T(8,128)S(1)} %get-tuple-element.22), channel_id=1, source_target_pairs={{0,4},{4,8},{8,12},{12,0},{1,5},{5,9},{9,13},{13,1},{2,6},{6,10},{... | collective-permute-start | bytes 110600 | tf_op jit(solution)/shard_map/ppermute | solution.py:717
  11.0 6.7 %collective-permute-start.4 = (f32[72,128]{1,0:T(8,128)S(1)}, f32[72,128]{1,0:T(8,128)S(1)}, u32[]{:S(2)}, u32[]{:S(2)}) collective-permute-start(f32[72,128]{1,0:T(8,128)S(1)} %get-tuple-element.23), channel_id=1, source_target_pairs={{0,12},{4,0},{8,4},{12,8},{1,13},{5,1},{9,5},{13,9},{2,14},{6,2},{... | collective-permute-start | bytes 110600 | tf_op jit(solution)/shard_map/ppermute | solution.py:718
  13.1 4.6 %collective-permute-start.5 = (f32[24,128]{1,0:T(8,128)S(1)}, f32[24,128]{1,0:T(8,128)S(1)}, u32[]{:S(2)}, u32[]{:S(2)}) collective-permute-start(f32[24,128]{1,0:T(8,128)S(1)} %get-tuple-element.24), channel_id=1, source_target_pairs={{0,8},{4,12},{8,0},{12,4},{1,9},{5,13},{9,1},{13,5},{2,10},{6,14},... | collective-permute-start | bytes 36872 | tf_op jit(solution)/shard_map/ppermute | solution.py:720

commit v5 on v4

--- a/solution.py
+++ b/solution.py
@@ -512,13 +512,15 @@
     result, early, late, out, sem = rest[count:]
     gx, gy = lax.axis_index("gx"), lax.axis_index("gy")
     at_end = gx == total_x // COLS - 1
-    bottom, top = gy == 0, gy == total_y // ROWS - 1
     lane = lanes((8, 128))
     at_first, at_last = lane == 0, lane == COLS - 1
     zone = jnp.broadcast_to(lam[0:1, :], (8, 128))
 
     def column(step, index, at):
         return jnp.broadcast_to(cols[pl.ds(48 * step + at, 8), index : index + 1], (8, 128))
+
+    def turned(step, index, at, lane_at):
+        return pltpu.roll(cols[pl.ds(48 * step + at, 8), :], (lane_at - index) % 128, 1)
 
     def goals(step, slot, at, wanted, gate):
         density, vx, vy, vz = (column(step, 80 + 8 * k + slot, at) for k in range(4))
@@ -536,30 +538,36 @@
             for i in fields:
                 early[i, slot, rows, :] = keep * field(i, slot, rows) + goal[i]
 
-    def pull(ref, slot, lead, step, at, lift, mine):
+    def pull(ref, slot, lead, step, at, lift, mine, bottom=False, top=False):
         r = at - lift
         g = []
         for i in range(19):
             cx, cy, cz = lattice_vel[i]
+            wall, kept = False, i
+            if mine and cy == 1 and slot == 2:
+                wall, kept = bottom, opposite[i]
+            if mine and cy == -1 and slot == 3:
+                wall, kept = top, mirror_pop[i]
+            if wall is True:
+                g.append(ref[kept, slot - lead, pl.ds(r, 8), :])
+                continue
             v = ref[i, slot - cy - lead, pl.ds(r - cz, 8), :]
             if cx == 1:
-                edge = column(step, EAST.index(i) * 8 + slot, at)
+                edge = turned(step, EAST.index(i) * 8 + slot, at, 0)
                 v = jnp.where(at_first, edge, pltpu.roll(v, 1, 1))
             if cx == -1:
-                edge = column(step, 40 + WEST.index(i) * 8 + slot, at)
+                edge = turned(step, 40 + WEST.index(i) * 8 + slot, at, COLS - 1)
                 if step == 1:
                     edge = jnp.where(at_end, ref[i, slot - lead, pl.ds(r, 8), :], edge)
                 v = jnp.where(at_last, edge, pltpu.roll(v, COLS - 1, 1))
-            if mine and cy == 1 and slot == 2:
-                v = jnp.where(bottom, ref[opposite[i], slot - lead, pl.ds(r, 8), :], v)
-            if mine and cy == -1 and slot == 3:
-                v = jnp.where(top, ref[mirror_pop[i], slot - lead, pl.ds(r, 8), :], v)
+            if wall is not False:
+                v = jnp.where(wall, ref[kept, slot - lead, pl.ds(r, 8), :], v)
             g.append(v)
         return g
 
-    def collide(slot, wanted, chunk, came=None):
+    def collide(slot, wanted, chunk, came=None, **walls):
         at = 1 + 8 * chunk
-        g = pull(early, slot, 0, 0, at, 0, came is None)
+        g = pull(early, slot, 0, 0, at, 0, came is None, **walls)
         total = sums(g)
         if came is not None:
             density, mx, mz = (came[pl.ds(SUMS_AT + n * (DEPTH + 2) + 8 * chunk, 8), :] for n in range(3))
@@ -574,9 +582,6 @@
         for i in wanted:
             v = jnp.where(wall, g[opposite[i]], (1.0 - relax_rate) * g[i] + eq[i])
             late[i, slot - 1, pl.ds(8 * chunk, 8), :] = keep * v + goal[i]
-
-    for slot in (2, 3):
-        finish(slot, range(19))
 
     def beside(n, came_up):
         near_slot, far_slot = (1, 0) if came_up else (4, 5)
@@ -594,36 +599,49 @@
         moving = UP if came_up else DOWN
         finish(near_slot, FLAT_Y + moving)
         finish(far_slot, moving)
+        return near_slot, moving
+
+    def advance(near, **walls):
         for chunk in range(5):
-            collide(near_slot, moving, chunk, bulk[n])
-
+            for came, slot, moving in near:
+                collide(slot, moving, chunk, came)
+            for slot in (2, 3):
+                collide(slot, range(19), chunk, **walls)
+        stores = []
+        for chunk in range(DEPTH // 8):
+            for y in range(ROWS):
+                g = pull(late, 2 + y, 1, 1, 2 + 8 * chunk, 1, True, **walls)
+                for i in range(19):
+                    out[i, pl.ds(16 * chunk + y, 8, stride=2), :] = g[i]
+            rows = pl.ds(16 * chunk, 16)
+            stores.append(pltpu.make_async_copy(out.at[:, rows, :], result.at[:, rows, :], sem.at[chunk]))
+            stores[-1].start()
+        for copy in stores:
+            copy.wait()
+
+    if ways == (None,):
+        for came_up in (False, True):
+
+            @pl.when(gy == int(came_up))
+            def _():
+                for slot in (2, 3):
+                    finish(slot, range(19))
+                slot, moving = beside(0, came_up)
+                advance([(bulk[0], slot, moving)], bottom=not came_up, top=came_up)
+
+        return
+    for slot in (2, 3):
+        finish(slot, range(19))
+    bottom, top = gy == 0, gy == total_y // ROWS - 1
     for n, way in enumerate(ways):
-        if way is not False:
-
-            @pl.when(jnp.logical_not(bottom))
-            def _():
-                beside(n, True)
-
-        if way is not True:
-
-            @pl.when(jnp.logical_not(top))
-            def _():
-                beside(n, False)
-
-    stores = []
-    for chunk in range(5):
-        for slot in (2, 3):
-            collide(slot, range(19), chunk)
-    for chunk in range(1, 5):
-        for y in range(ROWS):
-            g = pull(late, 2 + y, 1, 1, 8 * chunk - 6, 1, True)
-            for i in range(19):
-                out[i, pl.ds(16 * (chunk - 1) + y, 8, stride=2), :] = g[i]
-        rows = pl.ds(16 * (chunk - 1), 16)
-        stores.append(pltpu.make_async_copy(out.at[:, rows, :], result.at[:, rows, :], sem.at[chunk - 1]))
-        stores[-1].start()
-    for copy in stores:
-        copy.wait()
+
+        @pl.when(jnp.logical_not(bottom if way else top))
+        def _():
+            slot, moving = beside(n, way)
+            for chunk in range(5):
+                collide(slot, moving, chunk, bulk[n])
+
+    advance([], bottom=bottom, top=top)
 
 
 def call(kernel, outs, scratch, limit, *args, held=False, leave=False):

time: 20.8 us -> 20.5 us (0.986)
  Pallas kernels: 5.06 us -> 4.81 us
    pallas_call x5, Pallas kernels: 5.06 us -> 4.81 us  [call(): pl.pallas_call(kernel, out_shape=[jax.ShapeDtypeStruct(s, jnp.float32) fo...]
where the time goes in v5:
time: 20.5 us; the launch traced here: 20.3 us
  starting transfers between devices  9.49 us (46%)
  waiting for transfers between devices  5.35 us (26%)
  Pallas kernels  4.81 us (23%)
  between operations  0.68 us (3%)
    pallas_call x5, Pallas kernels, call(): pl.pallas_call(kernel, out_shape=[jax.ShapeDtypeStruct(s, jnp.float32) fo...  4.81 us
    ppermute x2, starting transfers between devices, across(): return lax.ppermute(v, 'gy', ring(2, 1))  3.87 us
    ppermute x1, waiting for transfers between devices, body(): far = lax.ppermute(plane, 'gx', ring(4, 2))  3.65 us
    ppermute x1, starting transfers between devices, body(): east = lax.ppermute(left, 'gx', ring(size_x, -1))  2.09 us
    ppermute x1, starting transfers between devices, body(): west = lax.ppermute(right, 'gx', ring(size_x, 1))  2.07 us
    ppermute x1, waiting for transfers between devices, body(): beside_other = [lax.ppermute(v, 'gz', ring(2, 1)) for v in beside]  1.2 us
    ppermute x1, starting transfers between devices, body(): far = lax.ppermute(plane, 'gx', ring(4, 2))  0.95 us
    ppermute x1, starting transfers between devices, body(): z_in = lax.ppermute(z_out, 'gz', ring(2, 1))  0.52 us
  transfers between devices with their start and end apart: 7, of which 3 were waited for; matrix products, arithmetic and copies ran while one was open for 0% of the time, Pallas kernels for 5%

profile of v5, /device:TPU:0, one launch (start us, length us, event | category | flops | bytes accessed | tf_op | source)
XLA Modules:
  0.0 20.3 jit_solution(18099892967063720145)
XLA Ops:
  0.7 1.7 %shard_map.82 = (f32[20,2,32,128]{3,2,1,0:T(8,128)S(1)}, f32[8,128]{1,0:T(8,128)S(1)}, f32[64,128]{1,0:T(8,128)S(1)}, f32[224,128]{1,0:T(8,128)S(1)}) custom-call(s32[1]{0:T(128)S(6)} %copy.9.refs_0_, f32[19,64,128]{2,1,0:T(8,128)} %bitcast.3, s32[64,128]{1,0:T(8,128)} %bitcast.4, s32[2]{0:T(128)} %refs_3_.1, s32[2]{0:T(128)} %refs_4_.1, f32[2]{0:T(128)} %refs_5_.1, ...), custom_call_target="tpu_custom_call" | custom-call | tf_op jit(solution)/shard_map/pallas_call | solution.py:654
  2.4 0.5 %collective-permute-start = (f32[224,128]{1,0:T(8,128)S(1)}, f32[224,128]{1,0:T(8,128)S(1)}, u32[]{:S(2)}, u32[]{:S(2)}) collective-permute-start(f32[224,128]{1,0:T(8,128)S(1)} %get-tuple-element.18), channel_id=1, source_target_pairs={{0,1},{1,0},{2,3},{3,2},{4,5},{5,4},{6,7},{7,6},{8,9},{9,8},{10,11... | collective-permute-start | bytes 344072 | tf_op jit(solution)/shard_map/ppermute | solution.py:710
  2.9 2.6 %collective-permute-start.1 = (f32[64,128]{1,0:T(8,128)S(1)}, f32[64,128]{1,0:T(8,128)S(1)}, u32[]{:S(2)}, u32[]{:S(2)}) collective-permute-start(f32[64,128]{1,0:T(8,128)S(1)} %get-tuple-element.20.refs_0_), channel_id=1, source_target_pairs={{0,2},{2,0},{1,3},{3,1},{4,6},{6,4},{5,7},{7,5},{8,10},{10,8},{9,1... | collective-permute-start | bytes 98312 | tf_op jit(solution)/shard_map/ppermute | solution.py:705
  5.5 0.0 collective-permute-done.z_in.refs_1_
  5.5 0.2 shard_map.83
  5.7 1.3 %collective-permute-start.6 = (f32[584,128]{1,0:T(8,128)S(1)}, f32[584,128]{1,0:T(8,128)S(1)}, u32[]{:S(2)}, u32[]{:S(2)}) collective-permute-start(f32[584,128]{1,0:T(8,128)S(1)} %get-tuple-element.26), channel_id=1, source_target_pairs={{0,2},{2,0},{1,3},{3,1},{4,6},{6,4},{5,7},{7,5},{8,10},{10,8},{9,1... | collective-permute-start | bytes 897032 | tf_op jit(solution)/shard_map/ppermute | solution.py:705
  7.0 0.5 %collective-permute-done.1.refs_2_ = f32[64,128]{1,0:T(8,128)S(1)} collective-permute-done((f32[64,128]{1,0:T(8,128)S(1)}, f32[64,128]{1,0:T(8,128)S(1)}, u32[]{:S(2)}, u32[]{:S(2)}) %collective-permute-start.1) | collective-permute-done | bytes 32800 | tf_op jit(solution)/shard_map/ppermute | solution.py:705
  7.5 0.0 collective-permute-start.2
  7.5 1.2 %collective-permute-done.2.refs_3_ = f32[64,128]{1,0:T(8,128)S(1)} collective-permute-done((f32[64,128]{1,0:T(8,128)S(1)}, f32[64,128]{1,0:T(8,128)S(1)}, u32[]{:S(2)}, u32[]{:S(2)}) %collective-permute-start.2) | collective-permute-done | bytes 32800 | tf_op jit(solution)/shard_map/ppermute | solution.py:721
  8.7 0.3 %shard_map.84 = (f32[2,192,128]{2,1,0:T(8,128)S(1)}, f32[72,128]{1,0:T(8,128)S(1)}, f32[72,128]{1,0:T(8,128)S(1)}, f32[24,128]{1,0:T(8,128)S(1)}, f32[32,128]{1,0:T(8,128)S(1)}) custom-call(f32[8,128]{1,0:T(8,128)S(1)} %get-tuple-element.16.lam, f32[64,128]{1,0:T(8,128)S(1)} %get-tuple-element.20.refs_0_, f32[224,128]{1,0:T(8,128)S(1)} %collective-permute-done.z_in.refs_1_, ...), custom_call_target="tpu_custom_call" | custom-call | tf_op jit(solution)/shard_map/pallas_call | solution.py:654
  9.0 2.1 %collective-permute-start.3 = (f32[72,128]{1,0:T(8,128)S(1)}, f32[72,128]{1,0:T(8,128)S(1)}, u32[]{:S(2)}, u32[]{:S(2)}) collective-permute-start(f32[72,128]{1,0:T(8,128)S(1)} %get-tuple-element.22), channel_id=1, source_target_pairs={{0,4},{4,8},{8,12},{12,0},{1,5},{5,9},{9,13},{13,1},{2,6},{6,10},{... | collective-permute-start | bytes 110600 | tf_op jit(solution)/shard_map/ppermute | solution.py:735
  11.0 2.1 %collective-permute-start.4 = (f32[72,128]{1,0:T(8,128)S(1)}, f32[72,128]{1,0:T(8,128)S(1)}, u32[]{:S(2)}, u32[]{:S(2)}) collective-permute-start(f32[72,128]{1,0:T(8,128)S(1)} %get-tuple-element.23), channel_id=1, source_target_pairs={{0,12},{4,0},{8,4},{12,8},{1,13},{5,1},{9,5},{13,9},{2,14},{6,2},{... | collective-permute-start | bytes 110600 | tf_op jit(solution)/shard_map/ppermute | solution.py:736
  13.1 0.9 %collective-permute-start.5 = (f32[24,128]{1,0:T(8,128)S(1)}, f32[24,128]{1,0:T(8,128)S(1)}, u32[]{:S(2)}, u32[]{:S(2)}) collective-permute-start(f32[24,128]{1,0:T(8,128)S(1)} %get-tuple-element.24), channel_id=1, source_target_pairs={{0,8},{4,12},{8,0},{12,4},{1,9},{5,13},{9,1},{13,5},{2,10},{6,14},... | collective-permute-start | bytes 36872 | tf_op jit(solution)/shard_map/ppermute | solution.py:738
  14.1 3.6 %collective-permute-done.5 = f32[24,128]{1,0:T(8,128)S(1)} collective-permute-done((f32[24,128]{1,0:T(8,128)S(1)}, f32[24,128]{1,0:T(8,128)S(1)}, u32[]{:S(2)}, u32[]{:S(2)}) %collective-permute-start.5) | collective-permute-done | bytes 12320 | tf_op jit(solution)/shard_map/ppermute | solution.py:738
  17.7 0.0 collective-permute-done.3.west
  17.7 0.0 collective-permute-done.4.east
  17.7 0.6 %shard_map.85.cols = f32[96,128]{1,0:T(8,128)S(1)} custom-call(f32[8,128]{1,0:T(8,128)S(1)} %get-tuple-element.16.lam, f32[2,192,128]{2,1,0:T(8,128)S(1)} %get-tuple-element.21.full, f32[72,128]{1,0:T(8,128)S(1)} %collective-permute-done.3.west, f32[72,128]{1,0:T(8,128)S(1)} %collective-permute-done.4.east, f32[24,128]{1,0:T(8,128)S(1)} %slice_add_fusion.plane, ...), custom_call_target="tpu_custom_call" | custom-call | tf_op jit(solution)/shard_map/pallas_call | solution.py:654
  18.4 0.0 collective-permute-done.6.rest_0_
  18.4 2.0 %shard_map.86 = f32[19,64,128]{2,1,0:T(8,128)} custom-call(f32[8,128]{1,0:T(8,128)S(1)} %get-tuple-element.16.lam, f32[20,2,48,128]{3,2,1,0:T(8,128)S(1)} %get-tuple-element.19.laid, f32[96,128]{1,0:T(8,128)S(1)} %shard_map.85.cols, f32[584,128]{1,0:T(8,128)S(1)} %collective-permute-done.6.rest_0_), custom_call_target="tpu_custom_call" | custom-call | tf_op jit(solution)/shard_map/pallas_call | solution.py:654
  (1 shorter events, 0.0 us)
Async XLA Ops:
  2.4 3.1 %collective-permute-start = (f32[224,128]{1,0:T(8,128)S(1)}, f32[224,128]{1,0:T(8,128)S(1)}, u32[]{:S(2)}, u32[]{:S(2)}) collective-permute-start(f32[224,128]{1,0:T(8,128)S(1)} %get-tuple-element.18), channel_id=1, source_target_pairs={{0,1},{1,0},{2,3},{3,2},{4,5},{5,4},{6,7},{7,6},{8,9},{9,8},{10,11... | collective-permute-start | bytes 344072 | tf_op jit(solution)/shard_map/ppermute | solution.py:710
  2.9 4.5 %collective-permute-start.1 = (f32[64,128]{1,0:T(8,128)S(1)}, f32[64,128]{1,0:T(8,128)S(1)}, u32[]{:S(2)}, u32[]{:S(2)}) collective-permute-start(f32[64,128]{1,0:T(8,128)S(1)} %get-tuple-element.20.refs_0_), channel_id=1, source_target_pairs={{0,2},{2,0},{1,3},{3,1},{4,6},{6,4},{5,7},{7,5},{8,10},{10,8},{9,1... | collective-permute-start | bytes 98312 | tf_op jit(solution)/shard_map/ppermute | solution.py:705
  5.7 12.7 %collective-permute-start.6 = (f32[584,128]{1,0:T(8,128)S(1)}, f32[584,128]{1,0:T(8,128)S(1)}, u32[]{:S(2)}, u32[]{:S(2)}) collective-permute-start(f32[584,128]{1,0:T(8,128)S(1)} %get-tuple-element.26), channel_id=1, source_target_pairs={{0,2},{2,0},{1,3},{3,1},{4,6},{6,4},{5,7},{7,5},{8,10},{10,8},{9,1... | collective-permute-start | bytes 897032 | tf_op jit(solution)/shard_map/ppermute | solution.py:705
  7.5 1.2 %collective-permute-start.2 = (f32[64,128]{1,0:T(8,128)S(1)}, f32[64,128]{1,0:T(8,128)S(1)}, u32[]{:S(2)}, u32[]{:S(2)}) collective-permute-start(f32[64,128]{1,0:T(8,128)S(1)} %collective-permute-done.1.refs_2_), channel_id=1, source_target_pairs={{0,1},{1,0},{2,3},{3,2},{4,5},{5,4},{6,7},{7,6},{8,9},{9,8},{10,11... | collective-permute-start | bytes 98312 | tf_op jit(solution)/shard_map/ppermute | solution.py:721
  9.0 8.8 %collective-permute-start.3 = (f32[72,128]{1,0:T(8,128)S(1)}, f32[72,128]{1,0:T(8,128)S(1)}, u32[]{:S(2)}, u32[]{:S(2)}) collective-permute-start(f32[72,128]{1,0:T(8,128)S(1)} %get-tuple-element.22), channel_id=1, source_target_pairs={{0,4},{4,8},{8,12},{12,0},{1,5},{5,9},{9,13},{13,1},{2,6},{6,10},{... | collective-permute-start | bytes 110600 | tf_op jit(solution)/shard_map/ppermute | solution.py:735
  11.0 6.7 %collective-permute-start.4 = (f32[72,128]{1,0:T(8,128)S(1)}, f32[72,128]{1,0:T(8,128)S(1)}, u32[]{:S(2)}, u32[]{:S(2)}) collective-permute-start(f32[72,128]{1,0:T(8,128)S(1)} %get-tuple-element.23), channel_id=1, source_target_pairs={{0,12},{4,0},{8,4},{12,8},{1,13},{5,1},{9,5},{13,9},{2,14},{6,2},{... | collective-permute-start | bytes 110600 | tf_op jit(solution)/shard_map/ppermute | solution.py:736
  13.1 4.6 %collective-permute-start.5 = (f32[24,128]{1,0:T(8,128)S(1)}, f32[24,128]{1,0:T(8,128)S(1)}, u32[]{:S(2)}, u32[]{:S(2)}) collective-permute-start(f32[24,128]{1,0:T(8,128)S(1)} %get-tuple-element.24), channel_id=1, source_target_pairs={{0,8},{4,12},{8,0},{12,4},{1,9},{5,13},{9,1},{13,5},{2,10},{6,14},... | collective-permute-start | bytes 36872 | tf_op jit(solution)/shard_map/ppermute | solution.py:738

commit v6 on v5

--- a/solution.py
+++ b/solution.py
@@ -194,6 +194,11 @@
             here_z = pl.ds(8 * chunk, 8)
             for f in range(20):
                 relaxed[f, y, here_z, :] = field[f]
+                at = TROWS + (f * 2 + y) * EDGE
+                if chunk == 0:
+                    zmsg[pl.ds(at, 2), :] = field[f][:2]
+                if chunk == pieces - 1:
+                    zmsg[pl.ds(at + 2, 2), :] = field[f][6:]
             for half in range(2):
                 fixed = jnp.zeros((8, 128), jnp.float32)
                 moving = jnp.zeros((8, 128), jnp.float32)
@@ -213,21 +218,23 @@
         columns[pl.ds(at, many), :] = v
         zmsg[pl.ds(at, many), :] = v
         at += many
-    for f in range(20):
-        for y in range(ROWS):
-            at = TROWS + (f * 2 + y) * EDGE
-            zmsg[pl.ds(at, 2), :] = relaxed[f, y, pl.ds(0, 2), :]
-            zmsg[pl.ds(at + 2, 2), :] = relaxed[f, y, pl.ds(DEPTH - 2, 2), :]
 
 
 def pack_kernel(ways, relaxed, lam, z_in, *rest):
     laid, bulk, inside = rest[0], rest[1:-1], rest[-1]
-    for f in range(20):
-        for y in range(ROWS):
+    row = lam[0:1, :]
+    for y in range(ROWS):
+        at = TROWS + (MASK * 2 + y) * EDGE
+        keep = 1.0 - (1.0 - relaxed[MASK, y, :, :]) * jnp.broadcast_to(row, (DEPTH, 128))
+        keep_edge = 1.0 - (1.0 - z_in[pl.ds(at, EDGE), :]) * jnp.broadcast_to(row, (EDGE, 128))
+        for f in range(20):
             at = TROWS + (f * 2 + y) * EDGE
-            laid[f, y, pl.ds(0, 2), :] = z_in[pl.ds(at + 2, 2), :]
-            laid[f, y, pl.ds(2, DEPTH), :] = relaxed[f, y, :, :]
-            laid[f, y, pl.ds(DEPTH + 2, 2), :] = z_in[pl.ds(at, 2), :]
+            v, edge = relaxed[f, y, :, :], z_in[pl.ds(at, EDGE), :]
+            if f != MASK:
+                v, edge = v * keep, edge * keep_edge
+            laid[f, y, pl.ds(0, 2), :] = edge[2:]
+            laid[f, y, pl.ds(2, DEPTH), :] = v
+            laid[f, y, pl.ds(DEPTH + 2, 2), :] = edge[:2]
     lane = lanes((8, 128))
     zone = jnp.broadcast_to(lam[0:1, :], (8, 128))
     zero = jnp.zeros((8, 128), jnp.float32)
@@ -536,7 +543,8 @@
             goal = goals(0, slot, 8 * chunk, fields, gate)
             keep = 1.0 - gate
             for i in fields:
-                early[i, slot, rows, :] = keep * field(i, slot, rows) + goal[i]
+                v = field(i, slot, rows)
+                early[i, slot, rows, :] = goal[i] + (v if slot in (2, 3) else keep * v)
 
     def pull(ref, slot, lead, step, at, lift, mine, bottom=False, top=False):
         r = at - lift

time: 20.5 us -> 20.4 us (level)
  transfers between devices with their start and end apart: 7 -> 7, of which waited for: 3 -> 3; matrix products, arithmetic and copies ran while one was open for 0% -> 0% of each run, Pallas kernels for 5% -> 6%
where the time goes in v6:
time: 20.4 us; the launch traced here: 20.3 us
  starting transfers between devices  9.49 us (47%)
  waiting for transfers between devices  5.33 us (26%)
  Pallas kernels  4.75 us (23%)
  between operations  0.68 us (3%)
    pallas_call x5, Pallas kernels, call(): pl.pallas_call(kernel, out_shape=[jax.ShapeDtypeStruct(s, jnp.float32) fo...  4.75 us
    ppermute x2, starting transfers between devices, across(): return lax.ppermute(v, 'gy', ring(2, 1))  3.87 us
    ppermute x1, waiting for transfers between devices, body(): far = lax.ppermute(plane, 'gx', ring(4, 2))  3.65 us
    ppermute x1, starting transfers between devices, body(): east = lax.ppermute(left, 'gx', ring(size_x, -1))  2.09 us
    ppermute x1, starting transfers between devices, body(): west = lax.ppermute(right, 'gx', ring(size_x, 1))  2.07 us
    ppermute x1, waiting for transfers between devices, body(): beside_other = [lax.ppermute(v, 'gz', ring(2, 1)) for v in beside]  1.2 us
    ppermute x1, starting transfers between devices, body(): far = lax.ppermute(plane, 'gx', ring(4, 2))  0.95 us
    ppermute x1, starting transfers between devices, body(): z_in = lax.ppermute(z_out, 'gz', ring(2, 1))  0.52 us
  transfers between devices with their start and end apart: 7, of which 3 were waited for; matrix products, arithmetic and copies ran while one was open for 0% of the time, Pallas kernels for 6%

profile of v6, /device:TPU:0, one launch (start us, length us, event | category | flops | bytes accessed | tf_op | source)
XLA Modules:
  0.0 20.3 jit_solution(3979358260963801363)
XLA Ops:
  0.7 1.7 %shard_map.82 = (f32[20,2,32,128]{3,2,1,0:T(8,128)S(1)}, f32[8,128]{1,0:T(8,128)S(1)}, f32[64,128]{1,0:T(8,128)S(1)}, f32[224,128]{1,0:T(8,128)S(1)}) custom-call(s32[1]{0:T(128)S(6)} %copy.9.refs_0_, f32[19,64,128]{2,1,0:T(8,128)} %bitcast.3, s32[64,128]{1,0:T(8,128)} %bitcast.4, s32[2]{0:T(128)} %refs_3_.1, s32[2]{0:T(128)} %refs_4_.1, f32[2]{0:T(128)} %refs_5_.1, ...), custom_call_target="tpu_custom_call" | custom-call | tf_op jit(solution)/shard_map/pallas_call | solution.py:662
  2.4 0.5 %collective-permute-start = (f32[224,128]{1,0:T(8,128)S(1)}, f32[224,128]{1,0:T(8,128)S(1)}, u32[]{:S(2)}, u32[]{:S(2)}) collective-permute-start(f32[224,128]{1,0:T(8,128)S(1)} %get-tuple-element.18), channel_id=1, source_target_pairs={{0,1},{1,0},{2,3},{3,2},{4,5},{5,4},{6,7},{7,6},{8,9},{9,8},{10,11... | collective-permute-start | bytes 344072 | tf_op jit(solution)/shard_map/ppermute | solution.py:718
  2.9 2.6 %collective-permute-start.1 = (f32[64,128]{1,0:T(8,128)S(1)}, f32[64,128]{1,0:T(8,128)S(1)}, u32[]{:S(2)}, u32[]{:S(2)}) collective-permute-start(f32[64,128]{1,0:T(8,128)S(1)} %get-tuple-element.20.refs_0_), channel_id=1, source_target_pairs={{0,2},{2,0},{1,3},{3,1},{4,6},{6,4},{5,7},{7,5},{8,10},{10,8},{9,1... | collective-permute-start | bytes 98312 | tf_op jit(solution)/shard_map/ppermute | solution.py:713
  5.4 0.0 collective-permute-done.z_in.refs_1_
  5.4 0.2 shard_map.83
  5.7 1.3 %collective-permute-start.6 = (f32[584,128]{1,0:T(8,128)S(1)}, f32[584,128]{1,0:T(8,128)S(1)}, u32[]{:S(2)}, u32[]{:S(2)}) collective-permute-start(f32[584,128]{1,0:T(8,128)S(1)} %get-tuple-element.26), channel_id=1, source_target_pairs={{0,2},{2,0},{1,3},{3,1},{4,6},{6,4},{5,7},{7,5},{8,10},{10,8},{9,1... | collective-permute-start | bytes 897032 | tf_op jit(solution)/shard_map/ppermute | solution.py:713
  7.0 0.5 %collective-permute-done.1.refs_2_ = f32[64,128]{1,0:T(8,128)S(1)} collective-permute-done((f32[64,128]{1,0:T(8,128)S(1)}, f32[64,128]{1,0:T(8,128)S(1)}, u32[]{:S(2)}, u32[]{:S(2)}) %collective-permute-start.1) | collective-permute-done | bytes 32800 | tf_op jit(solution)/shard_map/ppermute | solution.py:713
  7.4 0.0 collective-permute-start.2
  7.4 1.2 %collective-permute-done.2.refs_3_ = f32[64,128]{1,0:T(8,128)S(1)} collective-permute-done((f32[64,128]{1,0:T(8,128)S(1)}, f32[64,128]{1,0:T(8,128)S(1)}, u32[]{:S(2)}, u32[]{:S(2)}) %collective-permute-start.2) | collective-permute-done | bytes 32800 | tf_op jit(solution)/shard_map/ppermute | solution.py:729
  8.6 0.3 %shard_map.84 = (f32[2,192,128]{2,1,0:T(8,128)S(1)}, f32[72,128]{1,0:T(8,128)S(1)}, f32[72,128]{1,0:T(8,128)S(1)}, f32[24,128]{1,0:T(8,128)S(1)}, f32[32,128]{1,0:T(8,128)S(1)}) custom-call(f32[8,128]{1,0:T(8,128)S(1)} %get-tuple-element.16.lam, f32[64,128]{1,0:T(8,128)S(1)} %get-tuple-element.20.refs_0_, f32[224,128]{1,0:T(8,128)S(1)} %collective-permute-done.z_in.refs_1_, ...), custom_call_target="tpu_custom_call" | custom-call | tf_op jit(solution)/shard_map/pallas_call | solution.py:662
  8.9 2.1 %collective-permute-start.3 = (f32[72,128]{1,0:T(8,128)S(1)}, f32[72,128]{1,0:T(8,128)S(1)}, u32[]{:S(2)}, u32[]{:S(2)}) collective-permute-start(f32[72,128]{1,0:T(8,128)S(1)} %get-tuple-element.22), channel_id=1, source_target_pairs={{0,4},{4,8},{8,12},{12,0},{1,5},{5,9},{9,13},{13,1},{2,6},{6,10},{... | collective-permute-start | bytes 110600 | tf_op jit(solution)/shard_map/ppermute | solution.py:743
  11.0 2.1 %collective-permute-start.4 = (f32[72,128]{1,0:T(8,128)S(1)}, f32[72,128]{1,0:T(8,128)S(1)}, u32[]{:S(2)}, u32[]{:S(2)}) collective-permute-start(f32[72,128]{1,0:T(8,128)S(1)} %get-tuple-element.23), channel_id=1, source_target_pairs={{0,12},{4,0},{8,4},{12,8},{1,13},{5,1},{9,5},{13,9},{2,14},{6,2},{... | collective-permute-start | bytes 110600 | tf_op jit(solution)/shard_map/ppermute | solution.py:744
  13.1 0.9 %collective-permute-start.5 = (f32[24,128]{1,0:T(8,128)S(1)}, f32[24,128]{1,0:T(8,128)S(1)}, u32[]{:S(2)}, u32[]{:S(2)}) collective-permute-start(f32[24,128]{1,0:T(8,128)S(1)} %get-tuple-element.24), channel_id=1, source_target_pairs={{0,8},{4,12},{8,0},{12,4},{1,9},{5,13},{9,1},{13,5},{2,10},{6,14},... | collective-permute-start | bytes 36872 | tf_op jit(solution)/shard_map/ppermute | solution.py:746
  14.0 3.6 %collective-permute-done.5 = f32[24,128]{1,0:T(8,128)S(1)} collective-permute-done((f32[24,128]{1,0:T(8,128)S(1)}, f32[24,128]{1,0:T(8,128)S(1)}, u32[]{:S(2)}, u32[]{:S(2)}) %collective-permute-start.5) | collective-permute-done | bytes 12320 | tf_op jit(solution)/shard_map/ppermute | solution.py:746
  17.7 0.0 collective-permute-done.3.west
  17.7 0.0 collective-permute-done.4.east
  17.7 0.6 %shard_map.85.cols = f32[96,128]{1,0:T(8,128)S(1)} custom-call(f32[8,128]{1,0:T(8,128)S(1)} %get-tuple-element.16.lam, f32[2,192,128]{2,1,0:T(8,128)S(1)} %get-tuple-element.21.full, f32[72,128]{1,0:T(8,128)S(1)} %collective-permute-done.3.west, f32[72,128]{1,0:T(8,128)S(1)} %collective-permute-done.4.east, f32[24,128]{1,0:T(8,128)S(1)} %slice_add_fusion.plane, ...), custom_call_target="tpu_custom_call" | custom-call | tf_op jit(solution)/shard_map/pallas_call | solution.py:662
  18.3 0.0 collective-permute-done.6.rest_0_
  18.3 1.9 %shard_map.86 = f32[19,64,128]{2,1,0:T(8,128)} custom-call(f32[8,128]{1,0:T(8,128)S(1)} %get-tuple-element.16.lam, f32[20,2,48,128]{3,2,1,0:T(8,128)S(1)} %get-tuple-element.19.laid, f32[96,128]{1,0:T(8,128)S(1)} %shard_map.85.cols, f32[584,128]{1,0:T(8,128)S(1)} %collective-permute-done.6.rest_0_), custom_call_target="tpu_custom_call" | custom-call | tf_op jit(solution)/shard_map/pallas_call | solution.py:662
  (1 shorter events, 0.0 us)
Async XLA Ops:
  2.4 3.1 %collective-permute-start = (f32[224,128]{1,0:T(8,128)S(1)}, f32[224,128]{1,0:T(8,128)S(1)}, u32[]{:S(2)}, u32[]{:S(2)}) collective-permute-start(f32[224,128]{1,0:T(8,128)S(1)} %get-tuple-element.18), channel_id=1, source_target_pairs={{0,1},{1,0},{2,3},{3,2},{4,5},{5,4},{6,7},{7,6},{8,9},{9,8},{10,11... | collective-permute-start | bytes 344072 | tf_op jit(solution)/shard_map/ppermute | solution.py:718
  2.9 4.5 %collective-permute-start.1 = (f32[64,128]{1,0:T(8,128)S(1)}, f32[64,128]{1,0:T(8,128)S(1)}, u32[]{:S(2)}, u32[]{:S(2)}) collective-permute-start(f32[64,128]{1,0:T(8,128)S(1)} %get-tuple-element.20.refs_0_), channel_id=1, source_target_pairs={{0,2},{2,0},{1,3},{3,1},{4,6},{6,4},{5,7},{7,5},{8,10},{10,8},{9,1... | collective-permute-start | bytes 98312 | tf_op jit(solution)/shard_map/ppermute | solution.py:713
  5.7 12.7 %collective-permute-start.6 = (f32[584,128]{1,0:T(8,128)S(1)}, f32[584,128]{1,0:T(8,128)S(1)}, u32[]{:S(2)}, u32[]{:S(2)}) collective-permute-start(f32[584,128]{1,0:T(8,128)S(1)} %get-tuple-element.26), channel_id=1, source_target_pairs={{0,2},{2,0},{1,3},{3,1},{4,6},{6,4},{5,7},{7,5},{8,10},{10,8},{9,1... | collective-permute-start | bytes 897032 | tf_op jit(solution)/shard_map/ppermute | solution.py:713
  7.4 1.2 %collective-permute-start.2 = (f32[64,128]{1,0:T(8,128)S(1)}, f32[64,128]{1,0:T(8,128)S(1)}, u32[]{:S(2)}, u32[]{:S(2)}) collective-permute-start(f32[64,128]{1,0:T(8,128)S(1)} %collective-permute-done.1.refs_2_), channel_id=1, source_target_pairs={{0,1},{1,0},{2,3},{3,2},{4,5},{5,4},{6,7},{7,6},{8,9},{9,8},{10,11... | collective-permute-start | bytes 98312 | tf_op jit(solution)/shard_map/ppermute | solution.py:729
  8.9 8.8 %collective-permute-start.3 = (f32[72,128]{1,0:T(8,128)S(1)}, f32[72,128]{1,0:T(8,128)S(1)}, u32[]{:S(2)}, u32[]{:S(2)}) collective-permute-start(f32[72,128]{1,0:T(8,128)S(1)} %get-tuple-element.22), channel_id=1, source_target_pairs={{0,4},{4,8},{8,12},{12,0},{1,5},{5,9},{9,13},{13,1},{2,6},{6,10},{... | collective-permute-start | bytes 110600 | tf_op jit(solution)/shard_map/ppermute | solution.py:743
  11.0 6.7 %collective-permute-start.4 = (f32[72,128]{1,0:T(8,128)S(1)}, f32[72,128]{1,0:T(8,128)S(1)}, u32[]{:S(2)}, u32[]{:S(2)}) collective-permute-start(f32[72,128]{1,0:T(8,128)S(1)} %get-tuple-element.23), channel_id=1, source_target_pairs={{0,12},{4,0},{8,4},{12,8},{1,13},{5,1},{9,5},{13,9},{2,14},{6,2},{... | collective-permute-start | bytes 110600 | tf_op jit(solution)/shard_map/ppermute | solution.py:744
  13.1 4.6 %collective-permute-start.5 = (f32[24,128]{1,0:T(8,128)S(1)}, f32[24,128]{1,0:T(8,128)S(1)}, u32[]{:S(2)}, u32[]{:S(2)}) collective-permute-start(f32[24,128]{1,0:T(8,128)S(1)} %get-tuple-element.24), channel_id=1, source_target_pairs={{0,8},{4,12},{8,0},{12,4},{1,9},{5,13},{9,1},{13,5},{2,10},{6,14},... | collective-permute-start | bytes 36872 | tf_op jit(solution)/shard_map/ppermute | solution.py:746
